TPU v7x, 128 devices: a whole 4x4x4 slice. The times are simulated.
128 devices in a mesh: dp: 16 (over y_lo, x, core), head: 8 (over z, y_hi).
Axes of the slice: x: 4, y: 4 (y_hi: 2, y_lo: 2; y = y_hi * 2 + y_lo), z: 4, core: 2. Of those that a mesh axis runs over, the one named last changes fastest.
Arguments:
- tokens: bfloat16 [16384, 1024], P(('dp', 'head')), may hold values from -6 to 6
- w_project: bfloat16 [1024, 3072], P(None, ('dp', 'head')), may hold values from -0.1875 to 0.1875
- w_attend: bfloat16 [1024, 1024], P(None, ('dp', 'head')), may hold values from -1 to 1
- first_gain: bfloat16 [1024], P(('dp', 'head')), may hold values from 0.099609375 to 1.8984375
- first_shift: bfloat16 [1024], P(('dp', 'head')), may hold values from -3 to 3
- w_expand: bfloat16 [1024, 4096], P(None, ('dp', 'head')), may hold values from -0.1875 to 0.1875
- w_reduce: bfloat16 [4096, 1024], P(None, ('dp', 'head')), may hold values from -0.09375 to 0.09375
- second_gain: bfloat16 [1024], P(('dp', 'head')), may hold values from 0.099609375 to 1.8984375
- second_shift: bfloat16 [1024], P(('dp', 'head')), may hold values from -3 to 3
- position_table: bfloat16 [512, 1024], P(None, ('dp', 'head')), may hold values from -6 to 6
- w_query: bfloat16 [1024, 1024], P('dp', 'head'), may hold values from -0.1875 to 0.1875
- w_key: bfloat16 [1024, 1024], P('dp', 'head'), may hold values from -0.1875 to 0.1875
- lengths: int32 [32], P('dp'), may hold values from 64 to 512, as said below
- cotangent: bfloat16 [16384, 1024], P(('dp', 'head')), may hold values from -24 to 24
Outputs:
- layer_output: bfloat16 [16384, 1024], P(('dp', 'head'))
- tokens_grad: bfloat16 [16384, 1024], P(('dp', 'head'))
- grad_project: float32 [1024, 3072], P(None, ('dp', 'head'))
- grad_attend: float32 [1024, 1024], P(None, ('dp', 'head'))
- grad_first_gain: float32 [1024], P(('dp', 'head'))
- grad_first_shift: float32 [1024], P(('dp', 'head'))
- grad_expand: float32 [1024, 4096], P(None, ('dp', 'head'))
- grad_reduce: float32 [4096, 1024], P(None, ('dp', 'head'))
- grad_second_gain: float32 [1024], P(('dp', 'head'))
- grad_second_shift: float32 [1024], P(('dp', 'head'))
- grad_table: float32 [512, 1024], P(None, ('dp', 'head'))
- grad_query: float32 [1024, 1024], P('dp', 'head')
- grad_key: float32 [1024, 1024], P('dp', 'head')
Inputs may be any that keep to these rules, and one draw needn't show every extreme that they name: `lengths`: in each aligned block of 2 rows, one row has length 512.
All inputs are finite; a program needn't handle non-finite values.
Results may differ from a plain program's by a relative error of at most 0.02.
Values may be sent and summed in bfloat16 or wider, within the bound.
No kernel may reach another device: no remote copies, remote signals or barrier semaphores. Data moves between devices by JAX's collectives and lax.ppermute only.
A program may use at most 192 MiB of HBM per device.

v0:
```python
import math

import jax
import jax.numpy as jnp
import numpy as np
from jax import lax
from jax.sharding import PartitionSpec as P

D = 1024
HEADS = 16
HEAD_DIM = 64
SPAN = 256
SEQ = 512


EPS = 1e-07
MASKED = -1e30


def bucket_values(offset, span):
    middle = span // 2
    absolute = np.where((offset < middle) & (offset > -middle), middle - 1, np.abs(offset))
    log_place = (
        np.ceil(np.log(absolute / middle) / np.log((2 * span - 1) / middle) * (middle - 1)) + middle
    )
    buckets = np.where(absolute <= middle, offset, log_place * np.sign(offset)).astype(np.int64)
    return np.clip(buckets + span, 0, 2 * span - 1).astype(np.int32)


def contract_rows(left, right, precision=None):
    return lax.dot_general(
        left,
        right,
        (((0,), (0,)), ((), ())),
        precision=precision,
        preferred_element_type=jnp.float32,
    )


def contract_cols(left, right, precision=None):
    return lax.dot_general(
        left,
        right,
        (((1,), (1,)), ((), ())),
        precision=precision,
        preferred_element_type=jnp.float32,
    )


def normalize(value, gain, shift):
    center = value - jnp.mean(value, axis=-1, keepdims=True)
    inverse = lax.rsqrt(jnp.mean(center * center, axis=-1, keepdims=True) + EPS)
    scaled = center * inverse
    return (scaled * gain + shift, scaled, inverse)


def normalize_back(incoming, scaled, inverse, gain):
    grad_scaled = incoming * gain
    middle = (
        grad_scaled
        - jnp.mean(grad_scaled, axis=-1, keepdims=True)
        - scaled * jnp.mean(grad_scaled * scaled, axis=-1, keepdims=True)
    )
    return (inverse * middle, jnp.sum(incoming * scaled, axis=0), jnp.sum(incoming, axis=0))


def smooth_gate(value):
    return jax.nn.gelu(value, approximate=False)


def skew_grid(values):
    count = values.shape[-2]
    padded = jnp.pad(values, ((0, 0), (0, 0), (0, 1)))
    flat = padded.reshape(values.shape[0], count * 2 * count)
    flat = flat[:, count - 1 : count - 1 + count * (2 * count - 1)]
    return flat.reshape(values.shape[0], count, 2 * count - 1)[:, :, :count]


def unskew_grid(values):
    count = values.shape[-1]
    padded = jnp.pad(values, ((0, 0), (0, 0), (0, count - 1)))
    flat = padded.reshape(values.shape[0], count * (2 * count - 1))
    flat = jnp.pad(flat, ((0, 0), (count - 1, 1)))
    return flat.reshape(values.shape[0], count, 2 * count)[:, :, : 2 * count - 1]


def split_sum(columns, selector):
    upper = columns.astype(jnp.bfloat16)
    lower = (columns - upper.astype(jnp.float32)).astype(jnp.bfloat16)
    return jnp.einsum(
        "him,mr->hir", upper, selector, preferred_element_type=jnp.float32
    ) + jnp.einsum("him,mr->hir", lower, selector, preferred_element_type=jnp.float32)


def bucket_sums(grid, leftmost_distance, far_right):
    count = grid.shape[-1]
    middle = SPAN // 2
    columns = unskew_grid(grid)
    near_part = columns[:, :, count - 1 - middle : count + middle][:, :, ::-1]
    high_part = split_sum(columns[:, :, : count - 1 - middle], leftmost_distance)
    low_part = split_sum(columns[:, :, count + middle :], far_right)
    return jnp.concatenate([low_part, near_part, high_part], axis=-1)


def attention_logits(
    query_rows, key_rows, relative_key_rows, relative_query_rows, length, score_scale
):
    direct = jnp.einsum("ihd,jhd->hij", query_rows, key_rows, preferred_element_type=jnp.float32)
    key_position_scores = jnp.einsum(
        "awo,fwo->waf", query_rows, relative_key_rows, preferred_element_type=jnp.float32
    )
    query_position_scores = jnp.einsum(
        "bzi,qzi->zbq", key_rows, relative_query_rows, preferred_element_type=jnp.float32
    )
    gathered_key = skew_grid(key_position_scores)
    gathered_query = skew_grid(query_position_scores)
    logits = (direct + gathered_key + jnp.swapaxes(gathered_query, 1, 2)) * score_scale
    valid = jnp.arange(key_rows.shape[0]) < length
    return jnp.where(valid[None, None, :], logits, MASKED)


def per_device(
    tokens,
    w_project,
    w_attend,
    first_gain,
    first_shift,
    w_expand,
    w_reduce,
    second_gain,
    second_shift,
    position_table,
    w_query,
    w_key,
    lengths,
    cotangent,
):
    groups = lax.axis_size("head")
    local_tok = tokens.shape[0]
    stretch_w = D // groups
    heads_here = HEADS // groups
    score_scale = 1.0 / math.sqrt(3 * HEAD_DIM)
    highest = lax.Precision.HIGHEST
    middle = SPAN // 2
    column_bucket = bucket_values(SEQ - 1 - np.arange(2 * SEQ - 1), SPAN)
    column_ids = jnp.asarray(column_bucket)
    leftmost_distance = jnp.asarray(
        (
            column_bucket[: SEQ - 1 - middle][:, None]
            == np.arange(SPAN + middle + 1, 2 * SPAN)[None, :]
        ).astype(np.float32)
    ).astype(jnp.bfloat16)
    far_right = jnp.asarray(
        (column_bucket[SEQ + middle :][:, None] == np.arange(0, SPAN - middle)[None, :]).astype(
            np.float32
        )
    ).astype(jnp.bfloat16)
    full_project, full_attend, full_table, gain_attn, shift_attn = (
        lax.all_gather(w_project, ("dp", "head"), axis=1, tiled=True),
        lax.all_gather(w_attend, ("dp", "head"), axis=1, tiled=True),
        lax.all_gather(position_table, ("dp", "head"), axis=1, tiled=True),
        lax.all_gather(first_gain.reshape(1, -1), ("dp", "head"), axis=1, tiled=True),
        lax.all_gather(first_shift.reshape(1, -1), ("dp", "head"), axis=1, tiled=True),
    )
    pos_query, pos_key = (
        lax.all_gather(w_query, "dp", axis=0, tiled=True),
        lax.all_gather(w_key, "dp", axis=0, tiled=True),
    )
    packed = jnp.dot(tokens, full_project, preferred_element_type=jnp.float32).astype(jnp.bfloat16)
    head_layout = lax.all_to_all(
        packed.reshape(local_tok, 3, groups, stretch_w),
        "head",
        split_axis=2,
        concat_axis=0,
        tiled=True,
    )
    sequences = head_layout.shape[0] // SEQ
    head_layout = head_layout.reshape(sequences, SEQ, 3, heads_here, HEAD_DIM)
    rel_keys = (
        jnp.dot(full_table, pos_key, preferred_element_type=jnp.float32)
        .astype(jnp.bfloat16)
        .reshape(-1, heads_here, HEAD_DIM)
    )
    rel_queries = (
        jnp.dot(full_table, pos_query, preferred_element_type=jnp.float32)
        .astype(jnp.bfloat16)
        .reshape(-1, heads_here, HEAD_DIM)
    )
    table_rows = rel_keys.shape[0]
    relative_key_rows = rel_keys[column_ids]
    relative_query_rows = rel_queries[column_ids]

    def forward_one(pieces):
        query_rows, key_rows, values, length = pieces
        logits = attention_logits(
            query_rows, key_rows, relative_key_rows, relative_query_rows, length, score_scale
        )
        maximum = jnp.max(logits, axis=-1, keepdims=True)
        exponent = jnp.exp(logits - maximum)
        totals = jnp.sum(exponent, axis=-1, keepdims=True)
        weighting = (exponent / totals).astype(jnp.bfloat16)
        context = jnp.einsum(
            "hij,jhd->ihd", weighting, values, preferred_element_type=jnp.float32
        ).astype(jnp.bfloat16)
        return (context, (maximum + jnp.log(totals))[..., 0])

    context, log_partition_sum = lax.map(
        forward_one, (head_layout[:, :, 0], head_layout[:, :, 1], head_layout[:, :, 2], lengths)
    )
    context_rows = lax.all_to_all(
        context.reshape(sequences * SEQ, 1, stretch_w),
        "head",
        split_axis=0,
        concat_axis=1,
        tiled=True,
    ).reshape(local_tok, D)
    attended = jnp.dot(context_rows, full_attend, preferred_element_type=jnp.float32)
    gain_one = gain_attn.reshape(-1).astype(jnp.float32)
    first_norm, scaled_one, inverse_one = normalize(
        tokens.astype(jnp.float32) + attended, gain_one, shift_attn.reshape(-1).astype(jnp.float32)
    )
    first_low = first_norm.astype(jnp.bfloat16)
    full_expand, full_reduce, gain_ffn, shift_ffn = (
        lax.all_gather(w_expand, ("dp", "head"), axis=1, tiled=True),
        lax.all_gather(w_reduce, ("dp", "head"), axis=1, tiled=True),
        lax.all_gather(second_gain.reshape(1, -1), ("dp", "head"), axis=1, tiled=True),
        lax.all_gather(second_shift.reshape(1, -1), ("dp", "head"), axis=1, tiled=True),
    )
    inner = jnp.dot(first_low, full_expand, preferred_element_type=jnp.float32)
    activ = smooth_gate(inner).astype(jnp.bfloat16)
    ffn = jnp.dot(activ, full_reduce, preferred_element_type=jnp.float32)
    gain_two = gain_ffn.reshape(-1).astype(jnp.float32)
    output, scaled_two, inverse_two = normalize(
        first_norm + ffn, gain_two, shift_ffn.reshape(-1).astype(jnp.float32)
    )
    full_expand, full_reduce, gain_ffn = (
        lax.all_gather(w_expand, ("dp", "head"), axis=1, tiled=True),
        lax.all_gather(w_reduce, ("dp", "head"), axis=1, tiled=True),
        lax.all_gather(second_gain.reshape(1, -1), ("dp", "head"), axis=1, tiled=True),
    )
    gain_two = gain_ffn.reshape(-1).astype(jnp.float32)
    grad_resid2, grad_gain2, grad_shift2 = normalize_back(
        cotangent.astype(jnp.float32), scaled_two, inverse_two, gain_two
    )
    grad_ffn = grad_resid2.astype(jnp.bfloat16)
    grad_reduce = contract_rows(activ, grad_ffn)
    grad_activ = contract_cols(grad_ffn, full_reduce)
    gate_value, gate_pull = jax.vjp(smooth_gate, inner)
    grad_inner = gate_pull(grad_activ)[0].astype(jnp.bfloat16)
    grad_expand = contract_rows(first_low, grad_inner)
    grad_first = grad_resid2 + contract_cols(grad_inner, full_expand)
    ffn_shards = (
        lax.psum_scatter(grad_expand, ("dp", "head"), scatter_dimension=1, tiled=True),
        lax.psum_scatter(grad_reduce, ("dp", "head"), scatter_dimension=1, tiled=True),
        lax.psum_scatter(grad_gain2[None], ("dp", "head"), scatter_dimension=1, tiled=True),
        lax.psum_scatter(grad_shift2[None], ("dp", "head"), scatter_dimension=1, tiled=True),
    )
    full_project, full_attend, full_table, gain_attn = (
        lax.all_gather(w_project, ("dp", "head"), axis=1, tiled=True),
        lax.all_gather(w_attend, ("dp", "head"), axis=1, tiled=True),
        lax.all_gather(position_table, ("dp", "head"), axis=1, tiled=True),
        lax.all_gather(first_gain.reshape(1, -1), ("dp", "head"), axis=1, tiled=True),
    )
    gain_one = gain_attn.reshape(-1).astype(jnp.float32)
    grad_resid1, grad_gain1, grad_shift1 = normalize_back(
        grad_first, scaled_one, inverse_one, gain_one
    )
    grad_attended = grad_resid1.astype(jnp.bfloat16)
    grad_attend = contract_rows(context_rows, grad_attended)
    grad_context = contract_cols(grad_attended, full_attend).astype(jnp.bfloat16)
    grad_heads = lax.all_to_all(
        grad_context.reshape(local_tok, groups, stretch_w),
        "head",
        split_axis=1,
        concat_axis=0,
        tiled=True,
    )
    grad_heads = grad_heads.reshape(sequences, SEQ, heads_here, HEAD_DIM)

    def backward_one(carry, pieces):
        key_acc, query_acc = carry
        query_rows, key_rows, values, length, lse_rows, grad_ctx = pieces
        logits = attention_logits(
            query_rows, key_rows, relative_key_rows, relative_query_rows, length, score_scale
        )
        weighting = jnp.exp(logits - lse_rows[:, :, None])
        grad_values = jnp.einsum(
            "hij,ihd->jhd",
            weighting.astype(jnp.bfloat16),
            grad_ctx,
            preferred_element_type=jnp.float32,
        )
        grad_weights = jnp.einsum(
            "ihd,jhd->hij", grad_ctx, values, preferred_element_type=jnp.float32
        )
        grad_logits = (
            weighting
            * (grad_weights - jnp.sum(weighting * grad_weights, axis=-1, keepdims=True))
            * score_scale
        )
        direct_grad = grad_logits.astype(jnp.bfloat16)
        by_key_grad = bucket_sums(grad_logits, leftmost_distance, far_right).astype(jnp.bfloat16)
        by_query_grad = bucket_sums(
            jnp.swapaxes(grad_logits, 1, 2), leftmost_distance, far_right
        ).astype(jnp.bfloat16)
        grad_queries = jnp.einsum(
            "hij,jhd->ihd", direct_grad, key_rows, preferred_element_type=jnp.float32
        ) + jnp.einsum("hir,rhd->ihd", by_key_grad, rel_keys, preferred_element_type=jnp.float32)
        grad_keys = jnp.einsum(
            "hij,ihd->jhd", direct_grad, query_rows, preferred_element_type=jnp.float32
        ) + jnp.einsum(
            "hjr,rhd->jhd", by_query_grad, rel_queries, preferred_element_type=jnp.float32
        )
        key_acc = key_acc + jnp.einsum(
            "hir,ihd->rhd", by_key_grad, query_rows, preferred_element_type=jnp.float32
        )
        query_acc = query_acc + jnp.einsum(
            "hjr,jhd->rhd", by_query_grad, key_rows, preferred_element_type=jnp.float32
        )
        stacked = jnp.stack([grad_queries, grad_keys, grad_values], axis=1).astype(jnp.bfloat16)
        return ((key_acc, query_acc), stacked)

    zero_acc = jnp.zeros((table_rows, heads_here, HEAD_DIM), jnp.float32)
    (key_acc, query_acc), grad_stack = lax.scan(
        backward_one,
        (zero_acc, zero_acc),
        (
            head_layout[:, :, 0],
            head_layout[:, :, 1],
            head_layout[:, :, 2],
            lengths,
            log_partition_sum,
            grad_heads,
        ),
    )
    grad_packed = lax.all_to_all(
        grad_stack.reshape(sequences * SEQ, 3, 1, stretch_w),
        "head",
        split_axis=0,
        concat_axis=2,
        tiled=True,
    ).reshape(local_tok, 3 * D)
    grad_project = contract_rows(tokens, grad_packed)
    tokens_grad = (grad_resid1 + contract_cols(grad_packed, full_project)).astype(jnp.bfloat16)
    key_flat = key_acc.reshape(table_rows, stretch_w)
    query_flat = query_acc.reshape(table_rows, stretch_w)
    table_float = full_table.astype(jnp.float32)
    grad_key_w = contract_rows(table_float, key_flat, highest)
    grad_query_w = contract_rows(table_float, query_flat, highest)
    grad_table = contract_cols(key_flat, pos_key.astype(jnp.float32), highest) + contract_cols(
        query_flat, pos_query.astype(jnp.float32), highest
    )
    query_shard, key_shard = (
        lax.psum_scatter(
            grad_query_w.astype(jnp.bfloat16), "dp", scatter_dimension=0, tiled=True
        ).astype(jnp.float32),
        lax.psum_scatter(
            grad_key_w.astype(jnp.bfloat16), "dp", scatter_dimension=0, tiled=True
        ).astype(jnp.float32),
    )
    attn_shards = (
        lax.psum_scatter(grad_project, ("dp", "head"), scatter_dimension=1, tiled=True),
        lax.psum_scatter(grad_attend, ("dp", "head"), scatter_dimension=1, tiled=True),
        lax.psum_scatter(grad_table, ("dp", "head"), scatter_dimension=1, tiled=True),
        lax.psum_scatter(grad_gain1[None], ("dp", "head"), scatter_dimension=1, tiled=True),
        lax.psum_scatter(grad_shift1[None], ("dp", "head"), scatter_dimension=1, tiled=True),
    )
    return (
        output.astype(jnp.bfloat16),
        tokens_grad,
        attn_shards[0],
        attn_shards[1],
        attn_shards[3].reshape(-1),
        attn_shards[4].reshape(-1),
        ffn_shards[0],
        ffn_shards[1],
        ffn_shards[2].reshape(-1),
        ffn_shards[3].reshape(-1),
        attn_shards[2],
        query_shard,
        key_shard,
    )


def solution(mesh):
    in_specs = (
        P(("dp", "head"), None),
        P(None, ("dp", "head")),
        P(None, ("dp", "head")),
        P(("dp", "head")),
        P(("dp", "head")),
        P(None, ("dp", "head")),
        P(None, ("dp", "head")),
        P(("dp", "head")),
        P(("dp", "head")),
        P(None, ("dp", "head")),
        P("dp", "head"),
        P("dp", "head"),
        P("dp"),
        P(("dp", "head"), None),
    )
    out_specs = (
        P(("dp", "head"), None),
        P(("dp", "head"), None),
        P(None, ("dp", "head")),
        P(None, ("dp", "head")),
        P(("dp", "head")),
        P(("dp", "head")),
        P(None, ("dp", "head")),
        P(None, ("dp", "head")),
        P(("dp", "head")),
        P(("dp", "head")),
        P(None, ("dp", "head")),
        P("dp", "head"),
        P("dp", "head"),
    )
    return jax.shard_map(
        per_device, mesh=mesh, in_specs=in_specs, out_specs=out_specs, check_vma=False
    )
```

profile of v0, /device:TPU:0, one launch (start us, length us, event | category | flops | bytes accessed | tf_op | source)
XLA Modules:
  0.0 5322.6 jit_solution(3198497611413281911)
XLA Ops:
  10.6 20.7 all_gather.42
  31.3 291.1 %all-gather.10.cloned.1.call-done = bf16[1024,3072]{0,1:T(8,128)(2,1)} async-done(((bf16[1024,24]{0,1:T(8,128)(2,1)}), bf16[1024,3072]{0,1:T(8,128)(2,1)}) %all-gather.10.cloned.1.call-update) | async-done | bytes 6291472 | tf_op jit(solution)/shard_map/all_gather | solution.py:159
  329.1 7.4 all-to-all-start
  336.6 18.1 all_gather.43
  354.6 261.7 %all-gather.12.cloned.1.call-done = bf16[512,1024]{0,1:T(8,128)(2,1)} async-done(((bf16[512,8]{0,1:T(8,128)(2,1)}), bf16[512,1024]{0,1:T(8,128)(2,1)}) %all-gather.12.cloned.1.call-update) | async-done | bytes 1048592 | tf_op jit(solution)/shard_map/all_gather | solution.py:161
  633.1 99.0 %while.32 = (s32[]{:T(128)}, bf16[2,512,2,64]{1,3,2,0:T(8,128)(2,1)}, f32[2,2,512]{2,1,0:T(2,128)S(1)}, bf16[2,512,2,64]{1,3,2,0:T(8,128)(2,1)}, s32[2]{0:T(128)...) while((s32[]{:T(128)}, ...), condition=%wide.region_3.4_spmd, body=%wide.region_0.3_spmd.sunk | while | flops 407698944 | bytes 100912376 | solution.py:207
  643.5 9.5 reshape.407
  663.2 9.5 reshape.408
  692.7 9.5 reshape.407
  712.4 9.5 reshape.408
  737.3 8.0 all-to-all-start.1
  746.3 66.5 %all-reduce.17 = (bf16[1024]{0:T(1024)(128)(2,1)S(1)}, bf16[1024]{0:T(1024)(128)(2,1)S(1)}, bf16[1024]{0:T(1024)(128)(2,1)S(1)}, bf16[1024]{0:T(1024)(128)(2,1)S(1)}) all-reduce(bf16[1024]{0:T(1024)(128)(2,1)S(1)} %dynamic-update-slice.1, bf16[1024]{0:T(1024)(128)(2,1)S(1)} %dynamic-update-slice, ...), channel_id=3, replica_groups=mesh['dp'=16,'head'=8] {'dp','head'}, use_global_device_ids=true, to_apply=%add.9 | all-reduce | flops 4096 | bytes 16384
  813.4 106.9 %all-gather.14.cloned.1.call-done = bf16[1024,1024]{0,1:T(8,128)(2,1)} async-done(((bf16[1024,8]{0,1:T(8,128)(2,1)}), bf16[1024,1024]{0,1:T(8,128)(2,1)}) %all-gather.14.cloned.1.call-update) | async-done | bytes 2097168 | tf_op jit(solution)/shard_map/all_gather | solution.py:160
  923.1 311.3 %all-gather.16.cloned.1.call-done = bf16[1024,4096]{0,1:T(8,128)(2,1)} async-done(((bf16[1024,32]{0,1:T(8,128)(2,1)}), bf16[1024,4096]{0,1:T(8,128)(2,1)}) %all-gather.16.cloned.1.call-update) | async-done | bytes 8388624 | tf_op jit(solution)/shard_map/all_gather | solution.py:224
  1234.3 7.7 fusion.203
  1242.0 306.3 %all-gather.18.cloned.1.call-done = bf16[4096,1024]{0,1:T(8,128)(2,1)} async-done(((bf16[4096,8]{0,1:T(8,128)(2,1)}), bf16[4096,1024]{0,1:T(8,128)(2,1)}) %all-gather.18.cloned.1.call-update) | async-done | bytes 8388624 | tf_op jit(solution)/shard_map/all_gather | solution.py:225
  1548.3 10.4 fusion.209
  1560.6 7.7 add_convert_fusion
  1578.2 10.1 all-to-all-done.2
  1589.3 307.8 %while.33 = (s32[]{:T(128)}, f32[512,2,64]{0,2,1:T(8,128)}, f32[512,2,64]{0,2,1:T(8,128)}, bf16[2,512,3,2,64]{1,4,3,2,0:T(8,128)(2,1)}, bf16[2,512,2,64]{1,3,2,0...) while((s32[]{:T(128)}, f32[512,2,64]{0,2,1:T(8,128)}, ...), condition=%wide.region_14.15_spmd.clone.clone, body=%wide.region_12.14_spmd.clone.clone.sunk | while | flops 2039931904 | bytes 267313968 | solution.py:324
  1594.1 9.5 slice.230
  1603.7 9.5 reshape.409
  1623.5 9.5 reshape.410
  1651.1 9.8 reshape.411
  1660.8 5.9 pad.141
  1671.4 10.6 reverse.4
  1691.8 9.8 reshape.412
  1701.5 5.9 pad.143
  1712.1 10.6 reverse.5
  1744.4 9.3 slice.230
  1753.7 9.5 reshape.409
  1773.5 9.5 reshape.410
  1801.3 9.8 reshape.411
  1811.1 5.9 pad.141
  1821.7 10.5 reverse.4
  1842.0 9.8 reshape.412
  1851.8 5.9 pad.143
  1862.4 10.6 reverse.5
  1915.2 21.5 all_to_all.60
  1937.6 6.3 convolution_bitcast_fusion.6
  1945.3 8.2 fusion.201
  1954.7 11.0 fusion.191
  1966.4 63.3 %all-reduce.16 = (f32[1,1024]{1,0:T(1,128)S(1)}, f32[1,1024]{1,0:T(1,128)S(1)}, f32[1,1024]{1,0:T(1,128)S(1)}, f32[1,1024]{1,0:T(1,128)S(1)}) all-reduce(f32[1,1024]{1,0:T(1,128)S(1)} %bitcast.465, f32[1,1024]{1,0:T(1,128)S(1)} %bitcast.466, f32[1,1024]{1,0:T(1,128)S(1)} %bitcast.463, ...), channel_id=8, replica_groups=mesh['dp'=16,'head'=8] {'dp','head'}, use_global_device_ids=true, to_apply=%region_18.19.clone | all-reduce | flops 4096 | bytes 32768
  2039.6 622.0 %reduce-scatter.24.cloned.1.call-done = f32[512,8]{0,1:T(8,128)} async-done(((f32[512,1024]{0,1:T(8,128)}), f32[512,8]{0,1:T(8,128)}) %reduce-scatter.24.cloned.1.call-update) | async-done | bytes 16400 | tf_op jit(solution)/shard_map/reduce_scatter | solution.py:364
  2661.6 641.3 %reduce-scatter.18.cloned.1.call-done = f32[1024,8]{0,1:T(8,128)} async-done(((f32[1024,1024]{0,1:T(8,128)}), f32[1024,8]{0,1:T(8,128)}) %reduce-scatter.18.cloned.1.call-update) | async-done | bytes 32784 | tf_op jit(solution)/shard_map/reduce_scatter | solution.py:363
  3302.9 661.8 %reduce-scatter.16.cloned.1.call-done = f32[1024,24]{0,1:T(8,128)} async-done(((f32[1024,3072]{0,1:T(8,128)}), f32[1024,24]{0,1:T(8,128)}) %reduce-scatter.16.cloned.1.call-update) | async-done | bytes 98320 | tf_op jit(solution)/shard_map/reduce_scatter | solution.py:362
  3964.7 675.5 %reduce-scatter.20.cloned.1.call-done = f32[1024,32]{0,1:T(8,128)} async-done(((f32[1024,4096]{0,1:T(8,128)}), f32[1024,32]{0,1:T(8,128)}) %reduce-scatter.20.cloned.1.call-update) | async-done | bytes 131088 | tf_op jit(solution)/shard_map/reduce_scatter | solution.py:253
  4640.3 674.9 %reduce-scatter.22.cloned.1.call-done = f32[4096,8]{0,1:T(8,128)} async-done(((f32[4096,1024]{0,1:T(8,128)}), f32[4096,8]{0,1:T(8,128)}) %reduce-scatter.22.cloned.1.call-update) | async-done | bytes 131088 | tf_op jit(solution)/shard_map/reduce_scatter | solution.py:254
  (439 shorter events, 277.5 us)
Async XLA Ops:
  7.2 315.2 %all-gather.10.cloned.1.call-start = ((), (), s32[]{:S(2)}) async-start(), calls=%async_computation.11 | async-start | bytes 6340608 | tf_op jit(solution)/shard_map/all_gather | solution.py:159
  7.9 608.4 %all-gather.12.cloned.1.call-start = ((), (), s32[]{:S(2)}) async-start(), calls=%async_computation.12 | async-start | bytes 1056768 | tf_op jit(solution)/shard_map/all_gather | solution.py:161
  8.7 911.7 %all-gather.14.cloned.1.call-start = ((), (), s32[]{:S(2)}) async-start(), calls=%async_computation.13 | async-start | bytes 2113536 | tf_op jit(solution)/shard_map/all_gather | solution.py:160
  9.4 1225.0 %all-gather.16.cloned.1.call-start = ((), (), s32[]{:S(2)}) async-start(), calls=%async_computation.14 | async-start | bytes 8454144 | tf_op jit(solution)/shard_map/all_gather | solution.py:224
  10.0 1538.4 %all-gather.18.cloned.1.call-start = ((), (), s32[]{:S(2)}) async-start(), calls=%async_computation.15 | async-start | bytes 8454144 | tf_op jit(solution)/shard_map/all_gather | solution.py:225
  31.3 585.0 %copy-start.31 = (bf16[1024,128]{1,0:T(8,128)(2,1)}, bf16[1024,128]{1,0:T(8,128)(2,1)S(1)}, u32[]{:S(2)}) copy-start(bf16[1024,128]{1,0:T(8,128)(2,1)S(1)} %all_gather.42) | copy-start | bytes 786436
  327.5 9.1 copy-start.67
  329.1 299.2 %all-to-all-start = ((bf16[128,3,8,128]{0,3,1,2:T(8,128)(2,1)}), bf16[128,3,8,128]{0,3,1,2:T(8,128)(2,1)S(1)}, u32[]{:S(2)}, u32[]{:S(2)}) async-start(bf16[128,3,8,128]{0,3,1,2:T(8,128)(2,1)} %copy.97), calls=%async_computation | async-start | bytes 1572864 | tf_op jit(solution)/shard_map/all_to_all | solution.py:170
  354.6 269.0 %copy-start.33 = (bf16[1024,128]{1,0:T(8,128)(2,1)}, bf16[1024,128]{1,0:T(8,128)(2,1)S(1)}, u32[]{:S(2)}) copy-start(bf16[1024,128]{1,0:T(8,128)(2,1)S(1)} %all_gather.43) | copy-start | bytes 786436
  732.1 81.0 %copy-start.55 = (f32[2,2,512]{2,1,0:T(2,128)}, f32[2,2,512]{2,1,0:T(2,128)S(1)}, u32[]{:S(2)}) copy-start(f32[2,2,512]{2,1,0:T(2,128)S(1)} %get-tuple-element.812) | copy-start | bytes 24580
  732.1 13.2 copy-start.78
  732.2 13.4 copy-start.79
  732.2 13.6 copy-start.80
  732.2 13.9 copy-start.81
  733.8 186.5 %copy-start.29 = (bf16[128,1024]{1,0:T(8,128)(2,1)S(1)}, bf16[128,1024]{1,0:T(8,128)(2,1)}, u32[]{:S(2)}) copy-start(bf16[128,1024]{1,0:T(8,128)(2,1)} %param.21) | copy-start | bytes 786436
  737.3 75.5 %all-to-all-start.1 = ((bf16[8,2,8192]{2,1,0:T(2,128)(2,1)}), bf16[8,2,8192]{2,1,0:T(2,128)(2,1)S(1)}, u32[]{:S(2)}, u32[]{:S(2)}) async-start(bf16[8,2,8192]{2,1,0:T(2,128)(2,1)} %reshape.399), calls=%async_computation.1 | async-start | bytes 524288 | tf_op jit(solution)/shard_map/all_to_all | solution.py:210
  812.8 735.5 %copy-start.51 = (f32[1024]{0:T(1024)}, f32[1024]{0:T(1024)S(1)}, u32[]{:S(2)}) copy-start(f32[1024]{0:T(1024)S(1)} %add.220) | copy-start | bytes 12292
  812.8 757.9 %copy-start.49 = (f32[1024]{0:T(1024)}, f32[1024]{0:T(1024)S(1)}, u32[]{:S(2)}) copy-start(f32[1024]{0:T(1024)S(1)} %mul.200) | copy-start | bytes 12292
  812.8 755.5 %copy-start.57 = (f32[1024]{0:T(1024)}, f32[1024]{0:T(1024)S(1)}, u32[]{:S(2)}) copy-start(f32[1024]{0:T(1024)S(1)} %mul.201) | copy-start | bytes 12292
  813.4 428.6 %copy-start.35 = (bf16[128,8,1,128]{0,3,1,2:T(8,128)(2,1)}, bf16[128,8,1,128]{0,3,1,2:T(8,128)(2,1)S(1)}, u32[]{:S(2)}) copy-start(bf16[128,8,1,128]{0,3,1,2:T(8,128)(2,1)S(1)} %copy.108) | copy-start | bytes 786436
  922.8 647.9 %copy-start.12 = (f32[128,1024]{1,0:T(8,128)}, f32[128,1024]{1,0:T(8,128)S(1)}, u32[]{:S(2)}) copy-start(f32[128,1024]{1,0:T(8,128)S(1)} %get-tuple-element.623) | copy-start | bytes 1572868
  922.8 647.9 %copy-start.59 = (f32[128]{0:T(128)}, f32[128]{0:T(128)S(1)}, u32[]{:S(2)}) copy-start(f32[128]{0:T(128)S(1)} %broadcast_multiply_fusion.5) | copy-start | bytes 1540
  923.1 647.7 %copy-start.61 = (f32[128]{0:T(128)}, f32[128]{0:T(128)S(1)}, u32[]{:S(2)}) copy-start(f32[128]{0:T(128)S(1)} %add_rsqrt_fusion.1) | copy-start | bytes 1540
  1242.0 317.0 %copy-start.38 = (bf16[128,1024]{1,0:T(8,128)(2,1)S(1)}, bf16[128,1024]{1,0:T(8,128)(2,1)}, u32[]{:S(2)}) copy-start(bf16[128,1024]{1,0:T(8,128)(2,1)} %param.34) | copy-start | bytes 786436
  1548.3 12.2 copy-start.37
  1548.3 12.2 copy-start.39
  1548.3 12.2 copy-start.77
  1558.7 9.6 copy-start.27
  1558.8 9.6 copy-start.68
  1558.8 9.6 slice-start.2
  1559.0 9.3 copy-start.71
  1571.0 17.4 copy-start.20
  1571.0 18.3 copy-start.3
  1571.0 18.3 copy-start.4
  1571.0 18.3 copy-start.56
  1571.0 18.3 copy-start.83
  1572.3 15.9 all-to-all-start.2
  1578.1 453.9 %reduce-scatter.26.cloned.1.call-start = ((), (), s32[]{:S(2)}) async-start(), calls=%async_computation.21 | async-start | bytes 278528
  1589.6 48.1 copy-start.7
  1589.6 48.1 copy-start.10
  1739.9 47.8 copy-start.7
  1739.9 47.8 copy-start.10
  1900.5 133.1 %reduce-scatter.28.cloned.1.call-start = ((), (), s32[]{:S(2)}) async-start(), calls=%async_computation.22 | async-start | bytes 278528
  1902.6 759.0 %reduce-scatter.24.cloned.1.call-start = ((), (), s32[]{:S(2)}) async-start(), calls=%async_computation.20 | async-start | bytes 2113536 | tf_op jit(solution)/shard_map/reduce_scatter | solution.py:364
  1906.1 1396.8 %reduce-scatter.18.cloned.1.call-start = ((), (), s32[]{:S(2)}) async-start(), calls=%async_computation.17 | async-start | bytes 4227072 | tf_op jit(solution)/shard_map/reduce_scatter | solution.py:363
  1909.9 2054.8 %reduce-scatter.16.cloned.1.call-start = ((), (), s32[]{:S(2)}) async-start(), calls=%async_computation.16 | async-start | bytes 12681216 | tf_op jit(solution)/shard_map/reduce_scatter | solution.py:362
  1944.0 2696.3 %reduce-scatter.20.cloned.1.call-start = ((), (), s32[]{:S(2)}) async-start(), calls=%async_computation.18 | async-start | bytes 16908288 | tf_op jit(solution)/shard_map/reduce_scatter | solution.py:253
  1953.6 3361.6 %reduce-scatter.22.cloned.1.call-start = ((), (), s32[]{:S(2)}) async-start(), calls=%async_computation.19 | async-start | bytes 16908288 | tf_op jit(solution)/shard_map/reduce_scatter | solution.py:254
  (78 other events, 193.8 us)
Sparse Core Ops, SparseCore 0:
  9.7 312.6 all-gather.9
  324.1 292.1 all-gather.11
  618.0 302.2 all-gather.13
  921.9 312.4 all-gather.15
  1235.9 312.4 all-gather.17
  1900.6 57.8 reduce-scatter.25
  1961.6 58.5 reduce-scatter.27
  2023.1 638.4 reduce-scatter.23
  2664.7 638.1 reduce-scatter.17
  3305.7 658.9 reduce-scatter.15
  3967.8 672.3 reduce-scatter.19
  4643.2 671.9 reduce-scatter.21
where the time goes:
time: 5330 us; the launch traced here: 5320 us
  waiting for transfers between devices  4570 us (86%)
  local copies, waits for them, and re-layouts  358 us (7%)
  blocking collectives  190 us (4%)
  matrix products  150 us (3%)
    reduce_scatter x1, waiting for transfers between devices, per_device(): lax.psum_scatter(grad_expand, ('dp', 'head'), scatter_dimension=1, tiled=...  676 us
    reduce_scatter x1, waiting for transfers between devices, per_device(): lax.psum_scatter(grad_reduce, ('dp', 'head'), scatter_dimension=1, tiled=...  675 us
    reduce_scatter x1, waiting for transfers between devices, per_device(): lax.psum_scatter(grad_project, ('dp', 'head'), scatter_dimension=1, tiled...  662 us
    reduce_scatter x1, waiting for transfers between devices, per_device(): lax.psum_scatter(grad_attend, ('dp', 'head'), scatter_dimension=1, tiled=...  641 us
    reduce_scatter x1, waiting for transfers between devices, per_device(): lax.psum_scatter(grad_table, ('dp', 'head'), scatter_dimension=1, tiled=T...  622 us
    all_gather x1, waiting for transfers between devices, per_device(): lax.all_gather(w_expand, ('dp', 'head'), axis=1, tiled=True)  311 us
    all_gather x1, waiting for transfers between devices, per_device(): lax.all_gather(w_reduce, ('dp', 'head'), axis=1, tiled=True)  306 us
    all_gather x1, waiting for transfers between devices, per_device(): lax.all_gather(w_project, ('dp', 'head'), axis=1, tiled=True)  291 us
  transfers between devices with their start and end apart: 15, of which 11 were waited for; matrix products, arithmetic and copies ran while one was open for 3% of the time, Pallas kernels for 0%

commit v1 on v0

v1 whole, which is shorter than its diff:
```python
import math

import jax
import jax.numpy as jnp
import numpy as np
from jax import lax
from jax.sharding import Mesh
from jax.sharding import PartitionSpec as P

D = 1024
HEADS = 16
HEAD_DIM = 64
FF = 4096
SPAN = 256
SEQ = 512

EPS = 1e-07
MASKED = -1e30

DP = ("yl", "x", "core")
GROUP = ("z", "yh")
COLUMN = ("yl", "x")
EVERY = DP + GROUP
CHIPS = ("z", "yh", "yl", "x")
DEVICES = ("core",) + CHIPS
bf16 = jnp.bfloat16
f32 = jnp.float32


def bucket_values(offset, span):
    middle = span // 2
    absolute = np.where((offset < middle) & (offset > -middle), middle - 1, np.abs(offset))
    log_place = (
        np.ceil(np.log(absolute / middle) / np.log((2 * span - 1) / middle) * (middle - 1)) + middle
    )
    buckets = np.where(absolute <= middle, offset, log_place * np.sign(offset)).astype(np.int64)
    return np.clip(buckets + span, 0, 2 * span - 1).astype(np.int32)


def dot_nn(left, right):
    return lax.dot_general(left, right, (((1,), (0,)), ((), ())), preferred_element_type=f32)


def dot_nt(left, right):
    return lax.dot_general(left, right, (((1,), (1,)), ((), ())), preferred_element_type=f32)


def dot_tn(left, right, precision=None):
    return lax.dot_general(
        left, right, (((0,), (0,)), ((), ())), precision=precision, preferred_element_type=f32
    )


def normalize(value, gain, shift):
    center = value - jnp.mean(value, axis=-1, keepdims=True)
    inverse = lax.rsqrt(jnp.mean(center * center, axis=-1, keepdims=True) + EPS)
    scaled = center * inverse
    return (scaled * gain + shift, scaled, inverse)


def normalize_back(incoming, scaled, inverse, gain):
    grad_scaled = incoming * gain
    middle = (
        grad_scaled
        - jnp.mean(grad_scaled, axis=-1, keepdims=True)
        - scaled * jnp.mean(grad_scaled * scaled, axis=-1, keepdims=True)
    )
    return (inverse * middle, jnp.sum(incoming * scaled, axis=0), jnp.sum(incoming, axis=0))


def smooth_gate(value):
    return jax.nn.gelu(value, approximate=False)


def skew_grid(values):
    count = values.shape[-2]
    padded = jnp.pad(values, ((0, 0), (0, 0), (0, 1)))
    flat = padded.reshape(values.shape[0], count * 2 * count)
    flat = flat[:, count - 1 : count - 1 + count * (2 * count - 1)]
    return flat.reshape(values.shape[0], count, 2 * count - 1)[:, :, :count]


def unskew_grid(values):
    count = values.shape[-1]
    padded = jnp.pad(values, ((0, 0), (0, 0), (0, count - 1)))
    flat = padded.reshape(values.shape[0], count * (2 * count - 1))
    flat = jnp.pad(flat, ((0, 0), (count - 1, 1)))
    return flat.reshape(values.shape[0], count, 2 * count)[:, :, : 2 * count - 1]


def split_sum(columns, selector):
    upper = columns.astype(bf16)
    lower = (columns - upper.astype(f32)).astype(bf16)
    return jnp.einsum("him,mr->hir", upper, selector, preferred_element_type=f32) + jnp.einsum(
        "him,mr->hir", lower, selector, preferred_element_type=f32
    )


def bucket_sums(grid, leftmost_distance, far_right):
    count = grid.shape[-1]
    middle = SPAN // 2
    columns = unskew_grid(grid)
    near_part = columns[:, :, count - 1 - middle : count + middle][:, :, ::-1]
    high_part = split_sum(columns[:, :, : count - 1 - middle], leftmost_distance)
    low_part = split_sum(columns[:, :, count + middle :], far_right)
    return jnp.concatenate([low_part, near_part, high_part], axis=-1)


def attention_logits(query, key, relative_key_rows, relative_query_rows, lengths, scale):
    direct = jnp.einsum("bid,bjd->bij", query, key, preferred_element_type=f32)
    by_key = jnp.einsum("bid,fd->bif", query, relative_key_rows, preferred_element_type=f32)
    by_query = jnp.einsum("bjd,fd->bjf", key, relative_query_rows, preferred_element_type=f32)
    logits = (direct + skew_grid(by_key) + jnp.swapaxes(skew_grid(by_query), 1, 2)) * scale
    valid = jnp.arange(SEQ)[None, :] < lengths[:, None]
    return jnp.where(valid[:, None, :], logits, MASKED)


def swap(value):
    return lax.ppermute(value, "core", [(0, 1), (1, 0)])


def exchange(value, axes):
    return lax.all_to_all(value, axes, 0, 0, tiled=True)


def per_device(
    tokens,
    w_project,
    w_attend,
    first_gain,
    first_shift,
    w_expand,
    w_reduce,
    second_gain,
    second_shift,
    position_table,
    w_query,
    w_key,
    lengths,
    cotangent,
):
    core = lax.axis_index("core")
    group = lax.axis_index(GROUP)
    column = lax.axis_index(COLUMN)
    local = tokens.shape[0]
    pair = 2 * local
    scale = 1.0 / math.sqrt(3 * HEAD_DIM)
    highest = lax.Precision.HIGHEST
    middle = SPAN // 2
    column_bucket = bucket_values(SEQ - 1 - np.arange(2 * SEQ - 1), SPAN)
    column_ids = jnp.asarray(column_bucket)
    leftmost_distance = jnp.asarray(
        (
            column_bucket[: SEQ - 1 - middle][:, None]
            == np.arange(SPAN + middle + 1, 2 * SPAN)[None, :]
        ).astype(np.float32)
    ).astype(bf16)
    far_right = jnp.asarray(
        (column_bucket[SEQ + middle :][:, None] == np.arange(0, SPAN - middle)[None, :]).astype(
            np.float32
        )
    ).astype(bf16)

    def by_core(zero, one):
        return jnp.where(core == 0, zero, one)

    def both(value):
        return jnp.concatenate([value, swap(value)], axis=0)

    def give_halves(value):
        mine = by_core(value[0], value[1])
        theirs = by_core(value[1], value[0])
        got = swap(theirs)
        return mine, got

    def sum_pair(partial):
        return partial[:local] + swap(partial[local:])

    project_rows = w_project.T
    vectors = jnp.stack([first_gain, first_shift, second_gain, second_shift])
    packet = jnp.concatenate(
        [
            project_rows[:, :512],
            project_rows[:, 512:],
            position_table.T,
            jnp.pad(vectors, ((0, 4), (0, 504))),
        ],
        axis=0,
    )
    gathered = lax.all_gather(packet, DEVICES, axis=0, tiled=False)
    gathered = gathered.reshape(2, 4, 2, 2, 4, 64, 512)
    project_all = (
        gathered[..., :48, :]
        .reshape(2, 4, 2, 2, 4, 2, 24, 512)
        .transpose(3, 4, 0, 1, 2, 6, 5, 7)
        .reshape(3, 8, 2, HEAD_DIM, D)
    )
    w_heads = lax.dynamic_index_in_dim(project_all, core, axis=2, keepdims=False).reshape(1536, D)
    table_cols = gathered[..., 48:56, :].transpose(3, 4, 0, 1, 2, 5, 6).reshape(D, 2 * SPAN)
    vec = (
        gathered[..., 56:60, :8].transpose(5, 3, 4, 0, 1, 2, 6).reshape(4, D).astype(f32)
    )
    gain_one, shift_one, gain_two, shift_two = vec[0], vec[1], vec[2], vec[3]

    position_weights = lax.all_gather(
        jnp.concatenate([w_key, w_query], axis=1), DP, axis=0, tiled=True
    )
    position_weights = lax.dynamic_index_in_dim(
        position_weights.reshape(D, 2, 2, HEAD_DIM), core, axis=2, keepdims=False
    ).reshape(D, 2 * HEAD_DIM)

    reduce_rows = w_reduce.T.reshape(8, 8, 2, 256)
    mine, got = give_halves(jnp.moveaxis(reduce_rows, 2, 0).reshape(2, 8, 2048))
    reduce_rows = jnp.concatenate([by_core(mine, got), by_core(got, mine)], axis=0)
    attend_rows = w_attend.T.reshape(8, 8, 2, HEAD_DIM)
    mine, got = give_halves(jnp.moveaxis(attend_rows, 2, 0).reshape(2, 8, 512))
    attend_rows = jnp.concatenate([by_core(mine, got), by_core(got, mine)], axis=0)
    packet = jnp.concatenate(
        [w_expand.T, reduce_rows.reshape(32, D), attend_rows.reshape(8, D)], axis=0
    )
    gathered = lax.all_gather(packet, CHIPS, axis=0, tiled=False).reshape(4, 2, 2, 4, 72, D)
    expand_t = gathered[..., :32, :].transpose(2, 3, 0, 1, 4, 5).reshape(2048, D)
    reduce_t = (
        gathered[..., 32:64, :]
        .reshape(4, 2, 2, 4, 2, 8, 2048)
        .transpose(2, 3, 4, 0, 1, 5, 6)
        .reshape(D, 2048)
    )
    attend_t = (
        gathered[..., 64:, :]
        .reshape(4, 2, 2, 4, 2, 8, 512)
        .transpose(2, 3, 4, 0, 1, 5, 6)
        .reshape(D, 512)
    )

    tokens_two = both(tokens)
    packed = dot_nt(tokens_two, w_heads).astype(bf16)
    packed = packed.reshape(pair, 3, 8, HEAD_DIM).transpose(2, 0, 1, 3).reshape(8, pair, 192)
    heads_in = exchange(packed, GROUP)
    heads_in = heads_in.reshape(8, 2, local, 3, HEAD_DIM).transpose(3, 1, 0, 2, 4)
    query, key, values = heads_in.reshape(3, 4, SEQ, HEAD_DIM)
    lengths_four = jnp.concatenate([lengths, swap(lengths)], axis=0)
    rel = dot_tn(table_cols, position_weights).astype(bf16)
    rel_keys, rel_queries = rel[:, :HEAD_DIM], rel[:, HEAD_DIM:]
    relative_key_rows = rel_keys[column_ids]
    relative_query_rows = rel_queries[column_ids]
    logits = attention_logits(
        query, key, relative_key_rows, relative_query_rows, lengths_four, scale
    )
    maximum = jnp.max(logits, axis=-1, keepdims=True)
    exponent = jnp.exp(logits - maximum)
    totals = jnp.sum(exponent, axis=-1, keepdims=True)
    weighting = (exponent / totals).astype(bf16)
    context = jnp.einsum("bij,bjd->bid", weighting, values, preferred_element_type=f32).astype(bf16)
    lse = maximum + jnp.log(totals)

    context = context.reshape(2, 8, local, HEAD_DIM).transpose(1, 0, 2, 3)
    context = exchange(context.reshape(8, pair, HEAD_DIM), GROUP)
    context_two = context.transpose(1, 0, 2).reshape(pair, 512)

    attended = sum_pair(dot_nt(context_two, attend_t))
    first_norm, scaled_one, inverse_one = normalize(
        tokens.astype(f32) + attended, gain_one, shift_one
    )
    first_two = both(first_norm.astype(bf16))
    inner = dot_nt(first_two, expand_t)
    activ = smooth_gate(inner).astype(bf16)
    ffn = sum_pair(dot_nt(activ, reduce_t))
    output, scaled_two, inverse_two = normalize(first_norm + ffn, gain_two, shift_two)
    grad_resid2, grad_gain2, grad_shift2 = normalize_back(
        cotangent.astype(f32), scaled_two, inverse_two, gain_two
    )
    grad_ffn = both(grad_resid2.astype(bf16))
    grad_reduce_t = dot_tn(grad_ffn, activ).astype(bf16)
    grad_activ = dot_nn(grad_ffn, reduce_t)
    gate_value, gate_pull = jax.vjp(smooth_gate, inner)
    grad_inner = gate_pull(grad_activ)[0].astype(bf16)
    grad_expand_t = dot_tn(grad_inner, first_two).astype(bf16)
    grad_first = grad_resid2 + sum_pair(dot_nn(grad_inner, expand_t))
    grad_resid1, grad_gain1, grad_shift1 = normalize_back(
        grad_first, scaled_one, inverse_one, gain_one
    )
    grad_attended = both(grad_resid1.astype(bf16))
    grad_attend_t = dot_tn(grad_attended, context_two).astype(bf16)
    grad_context = dot_nn(grad_attended, attend_t).astype(bf16)

    grad_context = grad_context.reshape(pair, 8, HEAD_DIM).transpose(1, 0, 2)
    grad_ctx = exchange(grad_context, GROUP)
    grad_ctx = grad_ctx.reshape(8, 2, local, HEAD_DIM).transpose(1, 0, 2, 3)
    grad_ctx = grad_ctx.reshape(4, SEQ, HEAD_DIM)
    logits = attention_logits(
        query, key, relative_key_rows, relative_query_rows, lengths_four, scale
    )
    weighting = jnp.exp(logits - lse)
    grad_values = jnp.einsum(
        "bij,bid->bjd", weighting.astype(bf16), grad_ctx, preferred_element_type=f32
    )
    grad_weights = jnp.einsum("bid,bjd->bij", grad_ctx, values, preferred_element_type=f32)
    grad_logits = (
        weighting
        * (grad_weights - jnp.sum(weighting * grad_weights, axis=-1, keepdims=True))
        * scale
    )
    direct_grad = grad_logits.astype(bf16)
    by_key_grad = bucket_sums(grad_logits, leftmost_distance, far_right).astype(bf16)
    by_query_grad = bucket_sums(
        jnp.swapaxes(grad_logits, 1, 2), leftmost_distance, far_right
    ).astype(bf16)
    grad_queries = jnp.einsum(
        "bij,bjd->bid", direct_grad, key, preferred_element_type=f32
    ) + jnp.einsum("bir,rd->bid", by_key_grad, rel_keys, preferred_element_type=f32)
    grad_keys = jnp.einsum(
        "bij,bid->bjd", direct_grad, query, preferred_element_type=f32
    ) + jnp.einsum("bjr,rd->bjd", by_query_grad, rel_queries, preferred_element_type=f32)
    key_acc = jnp.einsum("bir,bid->rd", by_key_grad, query, preferred_element_type=f32)
    query_acc = jnp.einsum("bjr,bjd->rd", by_query_grad, key, preferred_element_type=f32)
    grad_stack = jnp.stack([grad_queries, grad_keys, grad_values], axis=2).astype(bf16)

    grad_stack = grad_stack.reshape(2, 8, local, 192).transpose(1, 0, 2, 3)
    grad_packed = exchange(grad_stack.reshape(8, pair, 192), GROUP)
    grad_packed = grad_packed.reshape(8, pair, 3, HEAD_DIM).transpose(1, 2, 0, 3)
    grad_packed = grad_packed.reshape(pair, 1536)
    tokens_grad = grad_resid1 + sum_pair(dot_nn(grad_packed, w_heads))

    def scatter(blocks):
        received = exchange(blocks, CHIPS)
        return jnp.sum(received.astype(f32), axis=0)

    def owners(rows, count):
        return jnp.swapaxes(rows, 0, 1).reshape(64, count, D)

    expand_blocks = owners(grad_expand_t.reshape(8, 8, 32 * D), 32)
    reduce_blocks = owners(
        grad_reduce_t.reshape(8, 2, 8, 8 * 2048).transpose(0, 2, 1, 3), 32
    )
    attend_blocks = owners(grad_attend_t.reshape(8, 2, 8, 8 * 512).transpose(0, 2, 1, 3), 8)
    summed = scatter(jnp.concatenate([expand_blocks, reduce_blocks, attend_blocks], axis=1))
    grad_expand = summed[:32].T
    mine, got = give_halves(summed[32:64].reshape(2, 8, 2048))
    grad_reduce = jnp.stack(
        [by_core(mine, got).reshape(8, 8, 256), by_core(got, mine).reshape(8, 8, 256)], axis=2
    )
    grad_reduce = grad_reduce.reshape(8, FF).T
    mine, got = give_halves(summed[64:].reshape(2, 8, 512))
    grad_attend = jnp.stack(
        [by_core(mine, got).reshape(8, 8, HEAD_DIM), by_core(got, mine).reshape(8, 8, HEAD_DIM)],
        axis=2,
    )
    grad_attend = grad_attend.reshape(8, D).T

    triples = grad_packed.reshape(pair, 8, 3, HEAD_DIM)
    triples = by_core(triples[:, :, (0, 2, 1)], triples[:, :, (1, 0, 2)])
    grad_project_t = dot_tn(triples.reshape(pair, 1536), tokens_two).astype(bf16)
    project_sum = scatter(owners(grad_project_t.reshape(8, 8, 24 * D), 24))
    from_partner = swap(project_sum)
    unit = (3 * group + np.arange(24) // 8) // 8
    grad_project = jnp.where((unit % 2 == 0)[:, None], project_sum, from_partner).T

    vectors = jnp.stack([grad_gain1, grad_shift1, grad_gain2, grad_shift2])
    vectors = vectors.reshape(4, 128, 8).transpose(1, 0, 2).reshape(128, 1, 32)
    vectors = jnp.sum(exchange(vectors, EVERY), axis=0).reshape(4, 8)

    rel_grad = jnp.concatenate([key_acc, query_acc], axis=1).astype(bf16)
    rel_grad = exchange(jnp.broadcast_to(rel_grad[None], (8, 2 * SPAN, 2 * HEAD_DIM)), COLUMN)
    rel_grad = jnp.sum(rel_grad.astype(f32), axis=0)
    other = swap(rel_grad)
    first, second = by_core(rel_grad, other), by_core(other, rel_grad)
    table_own = lax.dynamic_slice_in_dim(table_cols, 64 * (2 * column + core), 64, axis=0)
    table_own = table_own.astype(f32)
    grad_key = jnp.dot(
        table_own,
        jnp.concatenate([first[:, :HEAD_DIM], second[:, :HEAD_DIM]], axis=1),
        precision=highest,
    )
    grad_query = jnp.dot(
        table_own,
        jnp.concatenate([first[:, HEAD_DIM:], second[:, HEAD_DIM:]], axis=1),
        precision=highest,
    )
    weights_own = lax.dynamic_slice_in_dim(position_weights, 128 * column, 128, axis=0)
    table_part = lax.dot_general(
        weights_own.astype(f32), rel_grad, (((1,), (1,)), ((), ())), precision=highest
    ).astype(bf16)
    table_part = table_part.reshape(2, 8, 8, 2 * SPAN).transpose(1, 0, 2, 3)
    table_part = jnp.sum(exchange(table_part, GROUP).astype(f32), axis=0)
    mine, got = give_halves(table_part)
    grad_table = (mine + got).T

    return (
        output.astype(bf16),
        tokens_grad.astype(bf16),
        grad_project,
        grad_attend,
        vectors[0],
        vectors[1],
        grad_expand,
        grad_reduce,
        vectors[2],
        vectors[3],
        grad_table,
        grad_query,
        grad_key,
    )


def solution(mesh):
    parts = Mesh(mesh.devices.reshape(2, 4, 2, 4, 2), EVERY)
    in_specs = (
        P(EVERY, None),
        P(None, EVERY),
        P(None, EVERY),
        P(EVERY),
        P(EVERY),
        P(None, EVERY),
        P(None, EVERY),
        P(EVERY),
        P(EVERY),
        P(None, EVERY),
        P(DP, GROUP),
        P(DP, GROUP),
        P(DP),
        P(EVERY, None),
    )
    out_specs = (
        P(EVERY, None),
        P(EVERY, None),
        P(None, EVERY),
        P(None, EVERY),
        P(EVERY),
        P(EVERY),
        P(None, EVERY),
        P(None, EVERY),
        P(EVERY),
        P(EVERY),
        P(None, EVERY),
        P(DP, GROUP),
        P(DP, GROUP),
    )
    return jax.shard_map(
        per_device, mesh=parts, in_specs=in_specs, out_specs=out_specs, check_vma=False
    )
```

time: 5330 us -> 785 us (0.15)
  the two profiles are of different devices: /device:TPU:0 before, /device:TPU:5 now
where the time goes in v1:
time: 785 us; the launch traced here: 777 us
  local copies, waits for them, and re-layouts  337 us (43%)
  waiting for transfers between devices  226 us (29%)
  matrix products  80 us (10%)
  starting transfers between devices  63.5 us (8%)
  other arithmetic  36.6 us (5%)
  blocking collectives  18.2 us (2%)
  between operations  16 us (2%)
    all_to_all x9, waiting for transfers between devices, exchange(): return lax.all_to_all(value, axes, 0, 0, tiled=True)  171 us
    unnamed x191, local copies, waits for them, and re-layouts  103 us
    all_to_all x9, starting transfers between devices, exchange(): return lax.all_to_all(value, axes, 0, 0, tiled=True)  51.7 us
    all_gather x1, waiting for transfers between devices, per_device(): gathered = lax.all_gather(packet, DEVICES, axis=0, tiled=False)  47.8 us
    reshape x2, local copies, waits for them, and re-layouts, skew_grid(): return flat.reshape(values.shape[0], count, 2 * count - 1)[:, :, :count]  31.7 us
    reshape x2, local copies, waits for them, and re-layouts, unskew_grid(): flat = padded.reshape(values.shape[0], count * (2 * count - 1))  30.2 us
    reshape x2, local copies, waits for them, and re-layouts, per_device(): project_all = gathered[..., :48, :].reshape(2, 4, 2, 2, 4, 2, 24, 512).tr...  19 us
    slice x2, local copies, waits for them, and re-layouts, skew_grid(): flat = flat[:, count - 1:count - 1 + count * (2 * count - 1)]  18.9 us
  transfers between devices with their start and end apart: 27, of which 15 were waited for; matrix products, arithmetic and copies ran while one was open for 34% of the time, Pallas kernels for 0%

profile of v1, /device:TPU:5, one launch (start us, length us, event | category | flops | bytes accessed | tf_op | source)
XLA Modules:
  0.0 777.2 jit_solution(15344575128316945006)
XLA Ops:
  16.8 18.2 %all_gather.17 = bf16[1024,256]{1,0:T(8,128)(2,1)S(1)} all-gather(bf16[64,256]{1,0:T(8,128)(2,1)S(1)} %pad_maximum_fusion.25), channel_id=1, replica_groups=mesh['yl'=2,'x'=4,'core'=2,'z'=4,'yh'=2] {'yl','x','core'}, dimensions={0}, use_global_device_ids=true | all-gather | bytes 557056 | tf_op jit(solution)/shard_map/all_gather | solution.py:205
  35.5 47.8 %all-gather.5.cloned.1.call-done = bf16[8192,512]{1,0:T(8,128)(2,1)} async-done(((bf16[64,512]{1,0:T(8,128)(2,1)}), bf16[8192,512]{1,0:T(8,128)(2,1)}) %all-gather.5.cloned.1.call-update) | async-done | bytes 8388624 | tf_op jit(solution)/shard_map/all_gather | solution.py:190
  86.7 7.9 %copy.385 = bf16[2,4,2,2,4,2,24,512]{7,5,6,2,1,0,4,3:T(2,128)(2,1)} copy(bf16[2,4,2,2,4,2,24,512]{7,6,5,4,3,2,1,0:T(8,128)(2,1)S(1)} %bitcast.256) | data formatting | bytes 12582912 | tf_op jit(solution)/shard_map/reshape | solution.py:194
  94.6 11.1 %reshape.349 = bf16[3,8,2,64,1024]{4,3,2,1,0:T(8,128)(2,1)} reshape(bf16[2,4,2,4,2,24,2,512]{7,6,5,4,3,2,1,0:T(2,128)(2,1)} %bitcast.255) | data formatting | bytes 12582912 | tf_op jit(solution)/shard_map/reshape | solution.py:196
  112.0 4.6 all-to-all-start
  125.7 10.8 %all-to-all-done = bf16[8,256,192]{1,2,0:T(8,128)(2,1)S(1)} async-done(((bf16[8,256,192]{1,2,0:T(8,128)(2,1)}), bf16[8,256,192]{1,2,0:T(8,128)(2,1)S(1)}, u32[]{:S(2)}, u32[]{:S(2)}) %all-to-all-start) | async-done | bytes 786464 | tf_op jit(solution)/shard_map/all_to_all | solution.py:123
  140.1 4.4 pad_bitcast_fusion.1
  144.5 12.2 %copy.329 = f32[1,4,512,1024]{3,1,2,0:T(4,128)} copy(f32[1,4,512,1024]{3,2,1,0:T(8,128)} %pad_bitcast_fusion.1) | data formatting | bytes 16777216
  156.7 9.6 %slice.264 = f32[4,523776]{1,0:T(4,128)} slice(f32[4,524288]{1,0:T(4,128)} %bitcast.250), slice={[0:4], [511:524287]} | slice | bytes 16760832 | tf_op jit(solution)/shard_map/slice | solution.py:79
  166.2 15.8 %reshape.358 = f32[4,512,1023]{2,1,0:T(8,128)} reshape(f32[4,523776]{1,0:T(4,128)} %slice.264) | data formatting | bytes 16760832 | tf_op jit(solution)/shard_map/reshape | solution.py:80
  182.1 4.7 slice.265
  186.8 5.6 copy.327
  197.8 12.2 %copy.330 = f32[1,4,512,1024]{3,1,2,0:T(4,128)} copy(f32[1,4,512,1024]{3,2,1,0:T(8,128)} %pad_bitcast_fusion) | data formatting | bytes 16777216
  210.0 9.4 %slice.267 = f32[4,523776]{1,0:T(4,128)} slice(f32[4,524288]{1,0:T(4,128)} %bitcast.251), slice={[0:4], [511:524287]} | slice | bytes 16760832 | tf_op jit(solution)/shard_map/slice | solution.py:79
  219.4 15.8 %reshape.360 = f32[4,512,1023]{2,1,0:T(8,128)} reshape(f32[4,523776]{1,0:T(4,128)} %slice.267) | data formatting | bytes 16760832 | tf_op jit(solution)/shard_map/reshape | solution.py:80
  248.1 5.8 all-to-all-done.1
  261.7 6.4 fusion.151
  268.2 7.1 reshape.372
  279.6 8.4 %multiply_convert_fusion = (bf16[256,2048]{1,0:T(8,128)(2,1)S(1)}, f32[256,2048]{1,0:T(8,128)}, f32[256,2048]{1,0:T(8,128)}) fusion(bf16[2048,1024]{1,0:T(8,128)(2,1)S(1)} %bitcast.273, bf16[128,1024]{1,0:T(8,128)(2,1)S(1)} %collective-permute-done.5, bf16[128,1024]{1,0:T(8,128)(2,1)S(1)} %fusion.67), kind=kOutput, calls=%fused_computation.48 | convolution fusion | flops 1108869120 | bytes 9961472 | tf_op jit(solution)/shard_map/dot_general | solution.py:45
  316.4 8.4 %all-to-all-done.2 = bf16[8,256,64]{1,2,0:T(8,128)(2,1)S(1)} async-done(((bf16[8,256,64]{1,2,0:T(8,128)(2,1)}), bf16[8,256,64]{1,2,0:T(8,128)(2,1)S(1)}, u32[]{:S(2)}, u32[]{:S(2)}) %all-to-all-start.2) | async-done | bytes 262176 | tf_op jit(solution)/shard_map/all_to_all | solution.py:123
  329.0 7.7 multiply_multiply_fusion
  341.9 5.3 copy.328
  347.2 6.7 pad.30.clone
  353.9 15.0 %reshape.377 = f32[4,523776]{1,0:T(4,128)} reshape(f32[4,512,1023]{2,1,0:T(8,128)} %pad.30.clone) | data formatting | bytes 16760832 | tf_op jit(solution)/shard_map/reshape | solution.py:86
  368.9 7.2 pad.31
  376.0 4.9 copy.384
  391.4 15.2 %reshape.379 = f32[4,523776]{1,0:T(4,128)} reshape(f32[4,512,1023]{2,1,0:T(8,128)} %pad.32) | data formatting | bytes 16760832 | tf_op jit(solution)/shard_map/reshape | solution.py:86
  406.6 9.5 %pad.33 = f32[4,524288]{1,0:T(4,128)} pad(f32[4,523776]{1,0:T(4,128)} %reshape.379, f32[]{:T(128)} %constant.45.clone.1), padding=0_0x511_1 | pad | bytes 16769028 | tf_op jit(solution)/shard_map/jit(_pad)/pad | solution.py:87
  416.1 8.4 %copy.383 = f32[1,4,512,1024]{3,2,1,0:T(8,128)S(1)} copy(f32[1,4,512,1024]{3,1,2,0:T(4,128)} %bitcast.249) | data formatting | bytes 16777216
  431.9 16.9 %reverse.1 = bf16[4,512,384]{2,1,0:T(8,128)(2,1)} reverse(bf16[4,512,384]{2,1,0:T(8,128)(2,1)S(1)} %bitcast.267), dimensions={2} | reverse | bytes 3145728
  459.0 5.1 reverse
  478.6 9.7 %all-to-all-done.3 = bf16[8,256,192]{1,2,0:T(8,128)(2,1)S(1)} async-done(((bf16[8,256,192]{1,2,0:T(8,128)(2,1)}), bf16[8,256,192]{1,2,0:T(8,128)(2,1)S(1)}, u32[]{:S(2)}, u32[]{:S(2)}) %all-to-all-start.3) | async-done | bytes 786464 | tf_op jit(solution)/shard_map/all_to_all | solution.py:123
  489.4 4.5 all-to-all-start.7
  496.7 10.4 %all-to-all-done.7 = bf16[8,512,128]{2,1,0:T(8,128)(2,1)S(1)} async-done(((bf16[8,512,128]{2,1,0:T(8,128)(2,1)}), bf16[8,512,128]{2,1,0:T(8,128)(2,1)S(1)}, u32[]{:S(2)}, u32[]{:S(2)}) %all-to-all-start.7) | async-done | bytes 1048608 | tf_op jit(solution)/shard_map/all_to_all | solution.py:123
  507.1 7.9 %all-to-all-start.6 = ((f32[128,1,32]{2,1,0:T(1,128)}), f32[128,1,32]{2,1,0:T(1,128)S(1)}, u32[]{:S(2)}, u32[]{:S(2)}) async-start(f32[128,1,32]{2,1,0:T(1,128)} %copy.304), calls=%async_computation.6 | async-start | bytes 131072 | tf_op jit(solution)/shard_map/all_to_all | solution.py:123
  516.9 5.6 all-to-all-done.6
  529.0 4.8 reshape.384
  541.0 10.5 %all-to-all-start.4 = ((bf16[64,24,1024]{2,1,0:T(8,128)(2,1)}), bf16[64,24,1024]{2,1,0:T(8,128)(2,1)}, u32[]{:S(2)}, u32[]{:S(2)}) async-start(bf16[64,24,1024]{2,1,0:T(8,128)(2,1)} %bitcast.260), calls=%async_computation.4 | async-start | bytes 6291456 | tf_op jit(solution)/shard_map/all_to_all | solution.py:123
  554.9 7.4 reshape.386
  562.3 4.5 copy.296
  566.8 4.5 copy.334
  574.6 7.6 reshape.388
  582.2 8.5 %copy.386 = bf16[8,2,8,16384]{3,1,0,2:T(2,128)(2,1)} copy(bf16[8,2,8,16384]{3,2,1,0:T(8,128)(2,1)} %reshape.388) | data formatting | bytes 8388608 | tf_op jit(solution)/shard_map/reshape | solution.py:334
  590.7 7.9 %reshape.389 = bf16[64,32,1024]{2,1,0:T(8,128)(2,1)} reshape(bf16[8,8,2,16384]{3,2,1,0:T(2,128)(2,1)} %bitcast.258) | data formatting | bytes 8388608 | tf_op jit(solution)/shard_map/reshape | solution.py:330
  603.1 9.0 %pad_maximum_fusion = bf16[64,72,1024]{2,1,0:T(8,128)(2,1)} fusion(bf16[64,8,1024]{2,1,0:T(8,128)(2,1)S(1)} %reshape.391, bf16[64,32,1024]{2,1,0:T(8,128)(2,1)} %reshape.389, bf16[64,32,1024]{2,1,0:T(8,128)(2,1)} %bitcast.259), kind=kLoop, calls=%fused_computation.6 | loop fusion | flops 28311552 | bytes 18874368 | tf_op jit(solution)/shard_map/concatenate | solution.py:337
  612.1 10.1 %all-to-all-start.5 = ((bf16[64,72,1024]{2,1,0:T(8,128)(2,1)}), bf16[64,72,1024]{2,1,0:T(8,128)(2,1)}, u32[]{:S(2)}, u32[]{:S(2)}) async-start(bf16[64,72,1024]{2,1,0:T(8,128)(2,1)} %pad_maximum_fusion), calls=%async_computation.5 | async-start | bytes 18874368 | tf_op jit(solution)/shard_map/all_to_all | solution.py:123
  638.3 120.0 %all-to-all-done.5 = bf16[64,72,1024]{2,1,0:T(8,128)(2,1)} async-done(((bf16[64,72,1024]{2,1,0:T(8,128)(2,1)}), bf16[64,72,1024]{2,1,0:T(8,128)(2,1)}, u32[]{:S(2)}, u32[]{:S(2)}) %all-to-all-start.5) | async-done | bytes 9437216 | tf_op jit(solution)/shard_map/all_to_all | solution.py:123
  758.3 6.0 convert_reduce_fusion
  (406 shorter events, 194.3 us)
Async XLA Ops:
  7.2 28.0 %copy-start.81 = (s32[1023]{0:T(1024)S(1)}, s32[1023]{0:T(1024)}, u32[]{:S(2)}) copy-start(s32[1023]{0:T(1024)} %constant.212) | copy-start | bytes 12280
  7.2 28.1 %copy-start.84 = (s32[2]{0:T(128)S(1)}, s32[2]{0:T(128)}, u32[]{:S(2)}) copy-start(s32[2]{0:T(128)} %param.32) | copy-start | bytes 28
  7.2 28.0 %copy-start.48 = (bf16[128,1024]{1,0:T(8,128)(2,1)S(1)}, bf16[128,1024]{1,0:T(8,128)(2,1)}, u32[]{:S(2)}) copy-start(bf16[128,1024]{1,0:T(8,128)(2,1)} %param.20) | copy-start | bytes 786436
  7.2 76.0 %all-gather.5.cloned.1.call-start = ((), (), s32[]{:S(2)}) async-start(), calls=%async_computation.9 | async-start | bytes 8454144 | tf_op jit(solution)/shard_map/all_gather | solution.py:190
  10.1 236.1 %all-gather.7.cloned.1.call-start = ((), (), s32[]{:S(2)}) async-start(), calls=%async_computation.10 | async-start | bytes 9584640 | tf_op jit(solution)/shard_map/all_gather | solution.py:221
  11.1 1.7 collective-permute-start.3
  12.6 1.3 collective-permute-start.2
  15.5 19.8 %collective-permute-start = (s32[2]{0:T(128)}, s32[2]{0:T(128)S(1)}, u32[]{:S(2)}, u32[]{:S(2)}) collective-permute-start(s32[2]{0:T(128)} %param.32), channel_id=1, source_target_pairs={{0,8},{8,0},{1,9},{9,1},{2,10},{10,2},{3,11},{11,3},{4,12},{12,4},... | collective-permute-start | bytes 32 | tf_op jit(solution)/shard_map/ppermute | solution.py:119
  15.7 19.7 %collective-permute-start.1 = (bf16[128,1024]{1,0:T(8,128)(2,1)}, bf16[128,1024]{1,0:T(8,128)(2,1)S(1)}, u32[]{:S(2)}, u32[]{:S(2)}) collective-permute-start(bf16[128,1024]{1,0:T(8,128)(2,1)} %param.20), channel_id=1, source_target_pairs={{0,8},{8,0},{1,9},{9,1},{2,10},{10,2},{3,11},{11,3},{4,12},{12,4},... | collective-permute-start | bytes 786440 | tf_op jit(solution)/shard_map/ppermute | solution.py:119
  35.3 82.8 %copy-start.34 = (bf16[1024,2,1,64]{0,3,2,1:T(8,128)(2,1)}, bf16[1024,2,1,64]{0,3,2,1:T(8,128)(2,1)S(1)}, u32[]{:S(2)}) copy-start(bf16[1024,2,1,64]{0,3,2,1:T(8,128)(2,1)S(1)} %constant_dynamic-slice_fusion) | copy-start | bytes 786436
  35.5 72.6 %copy-start.35 = (bf16[256,1024]{1,0:T(8,128)(2,1)}, bf16[256,1024]{1,0:T(8,128)(2,1)S(1)}, u32[]{:S(2)}) copy-start(bf16[256,1024]{1,0:T(8,128)(2,1)S(1)} %constant_dynamic-update-slice_fusion) | copy-start | bytes 1572868
  112.0 24.5 %all-to-all-start = ((bf16[8,256,192]{1,2,0:T(8,128)(2,1)}), bf16[8,256,192]{1,2,0:T(8,128)(2,1)S(1)}, u32[]{:S(2)}, u32[]{:S(2)}) async-start(bf16[8,256,192]{1,2,0:T(8,128)(2,1)} %bitcast.12), calls=%async_computation | async-start | bytes 1572864 | tf_op jit(solution)/shard_map/all_to_all | solution.py:123
  137.9 102.0 %copy-start.65 = (bf16[4,512,64]{1,0,2:T(4,128)(2,1)}, bf16[4,512,64]{1,0,2:T(4,128)(2,1)S(1)}, u32[]{:S(2)}) copy-start(bf16[4,512,64]{1,0,2:T(4,128)(2,1)S(1)} %unstack.23) | copy-start | bytes 786436
  138.8 197.9 %copy-start.7 = (bf16[4,512,64]{1,0,2:T(4,128)(2,1)}, bf16[4,512,64]{1,0,2:T(4,128)(2,1)S(1)}, u32[]{:S(2)}) copy-start(bf16[4,512,64]{1,0,2:T(4,128)(2,1)S(1)} %unstack.19) | copy-start | bytes 786436
  242.8 11.1 %all-to-all-start.1 = ((bf16[8,256,64]{1,2,0:T(8,128)(2,1)}), bf16[8,256,64]{1,2,0:T(8,128)(2,1)S(1)}, u32[]{:S(2)}, u32[]{:S(2)}) async-start(bf16[8,256,64]{1,2,0:T(8,128)(2,1)} %reshape.362), calls=%async_computation.1 | async-start | bytes 524288 | tf_op jit(solution)/shard_map/all_to_all | solution.py:123
  255.4 4.6 collective-permute-start.4
  261.6 17.9 %copy-start.39 = (bf16[128,1024]{1,0:T(8,128)(2,1)}, bf16[128,1024]{1,0:T(8,128)(2,1)S(1)}, u32[]{:S(2)}) copy-start(bf16[128,1024]{1,0:T(8,128)(2,1)S(1)} %fusion.67) | copy-start | bytes 786436
  261.6 17.9 %collective-permute-start.5 = (bf16[128,1024]{1,0:T(8,128)(2,1)S(1)}, bf16[128,1024]{1,0:T(8,128)(2,1)S(1)}, u32[]{:S(2)}, u32[]{:S(2)}) collective-permute-start(bf16[128,1024]{1,0:T(8,128)(2,1)S(1)} %fusion.67), channel_id=1, source_target_pairs={{0,8},{8,0},{1,9},{9,1},{2,10},{10,2},{3,11},{11,3},{4,12},{12,4},... | collective-permute-start | bytes 786440 | tf_op jit(solution)/shard_map/ppermute | solution.py:119
  290.3 2.0 collective-permute-start.6
  294.9 1.6 collective-permute-start.7
  303.1 2.2 collective-permute-start.8
  310.1 18.9 %copy-start.43 = (bf16[128,1024]{1,0:T(8,128)(2,1)}, bf16[128,1024]{1,0:T(8,128)(2,1)S(1)}, u32[]{:S(2)}) copy-start(bf16[128,1024]{1,0:T(8,128)(2,1)S(1)} %get-tuple-element.21) | copy-start | bytes 786436
  310.1 1.5 collective-permute-start.9
  312.9 11.9 %all-to-all-start.2 = ((bf16[8,256,64]{1,2,0:T(8,128)(2,1)}), bf16[8,256,64]{1,2,0:T(8,128)(2,1)S(1)}, u32[]{:S(2)}, u32[]{:S(2)}) async-start(bf16[8,256,64]{1,2,0:T(8,128)(2,1)} %bitcast.44), calls=%async_computation.2 | async-start | bytes 524288 | tf_op jit(solution)/shard_map/all_to_all | solution.py:123
  316.4 12.6 %copy-start.66 = (bf16[4,512,64]{1,0,2:T(4,128)(2,1)S(1)}, bf16[4,512,64]{1,0,2:T(4,128)(2,1)}, u32[]{:S(2)}) copy-start(bf16[4,512,64]{1,0,2:T(4,128)(2,1)} %copy-done.65) | copy-start | bytes 786436
  406.6 22.4 %slice-start = ((s8[8388608]{0:T(1024)(128)(4,1)}), s8[4194304]{0:T(1024)(128)(4,1)S(1)}, s32[]{:S(2)}) async-start(s8[8388608]{0:T(1024)(128)(4,1)} %bitcast.239), calls=%async_computation.11 | async-start | bytes 8388608
  416.1 12.9 %slice-start.1 = ((s8[8388608]{0:T(1024)(128)(4,1)}), s8[4194304]{0:T(1024)(128)(4,1)S(1)}, s32[]{:S(2)}) async-start(s8[8388608]{0:T(1024)(128)(4,1)} %bitcast.239), calls=%async_computation.12 | async-start | bytes 8388608
  471.8 16.4 %all-to-all-start.3 = ((bf16[8,256,192]{1,2,0:T(8,128)(2,1)}), bf16[8,256,192]{1,2,0:T(8,128)(2,1)S(1)}, u32[]{:S(2)}, u32[]{:S(2)}) async-start(bf16[8,256,192]{1,2,0:T(8,128)(2,1)} %reshape.381), calls=%async_computation.3 | async-start | bytes 1572864 | tf_op jit(solution)/shard_map/all_to_all | solution.py:123
  478.3 15.5 %copy-start.82 = (s32[3]{0:T(128)S(1)}, s32[3]{0:T(128)}, u32[]{:S(2)}) copy-start(s32[3]{0:T(128)} %constant.215) | copy-start | bytes 40
  478.4 15.5 %copy-start.83 = (s32[3]{0:T(128)S(1)}, s32[3]{0:T(128)}, u32[]{:S(2)}) copy-start(s32[3]{0:T(128)} %constant.214) | copy-start | bytes 40
  478.4 15.5 %copy-start.72 = (f32[1024]{0:T(1024)S(1)}, f32[1024]{0:T(1024)}, u32[]{:S(2)}) copy-start(f32[1024]{0:T(1024)} %get-tuple-element.15) | copy-start | bytes 12292
  478.4 15.7 %copy-start.71 = (f32[1024]{0:T(1024)S(1)}, f32[1024]{0:T(1024)}, u32[]{:S(2)}) copy-start(f32[1024]{0:T(1024)} %get-tuple-element.20) | copy-start | bytes 12292
  478.4 15.8 %copy-start.74 = (f32[1024]{0:T(1024)S(1)}, f32[1024]{0:T(1024)}, u32[]{:S(2)}) copy-start(f32[1024]{0:T(1024)} %get-tuple-element.13) | copy-start | bytes 12292
  478.4 16.0 %copy-start.73 = (f32[1024]{0:T(1024)S(1)}, f32[1024]{0:T(1024)}, u32[]{:S(2)}) copy-start(f32[1024]{0:T(1024)} %get-tuple-element.18) | copy-start | bytes 12292
  489.4 17.7 %all-to-all-start.7 = ((bf16[8,512,128]{2,1,0:T(8,128)(2,1)}), bf16[8,512,128]{2,1,0:T(8,128)(2,1)S(1)}, u32[]{:S(2)}, u32[]{:S(2)}) async-start(bf16[8,512,128]{2,1,0:T(8,128)(2,1)} %broadcast_in_dim.38), calls=%async_computation.7 | async-start | bytes 2097152 | tf_op jit(solution)/shard_map/all_to_all | solution.py:123
  496.7 29.7 %copy-start.36 = (bf16[256,1024]{1,0:T(8,128)(2,1)S(1)}, bf16[256,1024]{1,0:T(8,128)(2,1)}, u32[]{:S(2)}) copy-start(bf16[256,1024]{1,0:T(8,128)(2,1)} %copy-done.35) | copy-start | bytes 1572868
  507.1 15.5 %all-to-all-start.6 = ((f32[128,1,32]{2,1,0:T(1,128)}), f32[128,1,32]{2,1,0:T(1,128)S(1)}, u32[]{:S(2)}, u32[]{:S(2)}) async-start(f32[128,1,32]{2,1,0:T(1,128)} %copy.304), calls=%async_computation.6 | async-start | bytes 131072 | tf_op jit(solution)/shard_map/all_to_all | solution.py:123
  515.1 13.9 %copy-start.24 = (f32[512,128]{1,0:T(8,128)}, f32[512,128]{1,0:T(8,128)S(1)}, u32[]{:S(2)}) copy-start(f32[512,128]{1,0:T(8,128)S(1)} %convert_reduce_fusion.2) | copy-start | bytes 786436
  522.6 18.4 %all-to-all-start.8 = ((bf16[8,2,8,512]{3,2,1,0:T(8,128)(2,1)}), bf16[8,2,8,512]{3,2,1,0:T(8,128)(2,1)S(1)}, u32[]{:S(2)}, u32[]{:S(2)}) async-start(bf16[8,2,8,512]{3,2,1,0:T(8,128)(2,1)} %bitcast.233), calls=%async_computation.8 | async-start | bytes 262144 | tf_op jit(solution)/shard_map/all_to_all | solution.py:123
  541.0 71.1 %all-to-all-start.4 = ((bf16[64,24,1024]{2,1,0:T(8,128)(2,1)}), bf16[64,24,1024]{2,1,0:T(8,128)(2,1)}, u32[]{:S(2)}, u32[]{:S(2)}) async-start(bf16[64,24,1024]{2,1,0:T(8,128)(2,1)} %bitcast.260), calls=%async_computation.4 | async-start | bytes 6291456 | tf_op jit(solution)/shard_map/all_to_all | solution.py:123
  612.1 10.9 %copy-start.25 = (f32[512,128]{1,0:T(8,128)S(1)}, f32[512,128]{1,0:T(8,128)}, u32[]{:S(2)}) copy-start(f32[512,128]{1,0:T(8,128)} %copy-done.24) | copy-start | bytes 786436
  612.1 146.2 %all-to-all-start.5 = ((bf16[64,72,1024]{2,1,0:T(8,128)(2,1)}), bf16[64,72,1024]{2,1,0:T(8,128)(2,1)}, u32[]{:S(2)}, u32[]{:S(2)}) async-start(bf16[64,72,1024]{2,1,0:T(8,128)(2,1)} %pad_maximum_fusion), calls=%async_computation.5 | async-start | bytes 18874368 | tf_op jit(solution)/shard_map/all_to_all | solution.py:123
  623.0 6.5 collective-permute-start.15
  625.3 3.6 collective-permute-start.14
  628.4 7.9 %collective-permute-start.10 = (f32[128,1024]{1,0:T(8,128)S(1)}, f32[128,1024]{1,0:T(8,128)S(1)}, u32[]{:S(2)}, u32[]{:S(2)}) collective-permute-start(f32[128,1024]{1,0:T(8,128)S(1)} %slice.294), channel_id=1, source_target_pairs={{0,8},{8,0},{1,9},{9,1},{2,10},{10,2},{3,11},{11,3},{4,12},{12,4},... | collective-permute-start | bytes 1572872 | tf_op jit(solution)/shard_map/ppermute | solution.py:119
  635.9 1.6 collective-permute-start.11
  765.0 3.5 collective-permute-start.12
  767.7 1.7 collective-permute-start.13
  (67 other events, 297.0 us)
Sparse Core Ops, SparseCore 0:
  11.8 71.4 all-gather.4
  86.6 85.7 all-gather.6

commit v2 on v1

v2 whole, which is shorter than its diff:
```python
import math

import jax
import jax.numpy as jnp
import numpy as np
from jax import lax
from jax.experimental import pallas as pl
from jax.experimental.pallas import tpu as pltpu
from jax.sharding import Mesh
from jax.sharding import PartitionSpec as P

D = 1024
HEADS = 16
HEAD_DIM = 64
FF = 4096
SPAN = 256
SEQ = 512
BLOCK = 128
WINDOW = SEQ + BLOCK

EPS = 1e-07
MASKED = -1e30

DP = ("yl", "x", "core")
GROUP = ("z", "yh")
COLUMN = ("yl", "x")
EVERY = DP + GROUP
CHIPS = ("z", "yh", "yl", "x")
DEVICES = ("core",) + CHIPS
bf16 = jnp.bfloat16
f32 = jnp.float32


def bucket_values(offset, span):
    middle = span // 2
    absolute = np.where((offset < middle) & (offset > -middle), middle - 1, np.abs(offset))
    log_place = (
        np.ceil(np.log(absolute / middle) / np.log((2 * span - 1) / middle) * (middle - 1)) + middle
    )
    buckets = np.where(absolute <= middle, offset, log_place * np.sign(offset)).astype(np.int64)
    return np.clip(buckets + span, 0, 2 * span - 1).astype(np.int32)


def normalize(value, gain, shift):
    center = value - jnp.mean(value, axis=-1, keepdims=True)
    inverse = lax.rsqrt(jnp.mean(center * center, axis=-1, keepdims=True) + EPS)
    scaled = center * inverse
    return (scaled * gain + shift, scaled, inverse)


def normalize_back(incoming, scaled, inverse, gain):
    grad_scaled = incoming * gain
    middle = (
        grad_scaled
        - jnp.mean(grad_scaled, axis=-1, keepdims=True)
        - scaled * jnp.mean(grad_scaled * scaled, axis=-1, keepdims=True)
    )
    return inverse * middle


def smooth_gate(value):
    return jax.nn.gelu(value, approximate=False)


def dot_nn(left, right):
    return lax.dot_general(left, right, (((1,), (0,)), ((), ())), preferred_element_type=f32)


def dot_nt(left, right):
    return lax.dot_general(left, right, (((1,), (1,)), ((), ())), preferred_element_type=f32)


def dot_tn(left, right):
    return lax.dot_general(left, right, (((0,), (0,)), ((), ())), preferred_element_type=f32)


def window(block):
    start = SEQ - BLOCK - BLOCK * block
    return slice(start, start + WINDOW)


def rows(block):
    return slice(BLOCK * block, BLOCK * (block + 1))


def skew(values):
    return pltpu.roll(values, SEQ + 1, 1, stride=1, stride_axis=0)[:, :SEQ]


def unskew(values):
    wide = jnp.concatenate([values, jnp.zeros((BLOCK, BLOCK), f32)], axis=1)
    return pltpu.roll(wide, 0, 1, stride=1, stride_axis=0)


def one_head(value, head):
    lane = lax.broadcasted_iota(jnp.int32, value.shape, 1)
    return jnp.where(lane // HEAD_DIM == head, value, jnp.zeros_like(value))


def query_bias(key, rel_queries, bias):
    for block in range(SEQ // BLOCK):
        by_offset = dot_nt(key[rows(block)], rel_queries[window(block)])
        bias[:, rows(block)] = skew(by_offset).T


def probabilities(query, key, rel_keys, bias, block, length):
    part = query[rows(block)]
    logits = dot_nt(part, key) + skew(dot_nt(part, rel_keys[window(block)])) + bias[rows(block)]
    logits = logits * (1.0 / math.sqrt(3 * HEAD_DIM))
    column = lax.broadcasted_iota(jnp.int32, logits.shape, 1)
    logits = jnp.where(column < length, logits, MASKED)
    exponent = jnp.exp(logits - jnp.max(logits, axis=1, keepdims=True))
    return exponent / jnp.sum(exponent, axis=1, keepdims=True)


def attend_kernel(lengths, heads_in, rel, context, bias):
    length = lengths[pl.program_id(0)]
    query, key, values = (heads_in[:, part].reshape(SEQ, 128) for part in range(3))
    rel_keys, rel_queries = rel[:, :128], rel[:, 128:]
    total = [jnp.zeros((BLOCK, 128), f32) for _ in range(SEQ // BLOCK)]
    for head in range(2):
        query_h, key_h, values_h = (one_head(part, head) for part in (query, key, values))
        query_bias(key_h, rel_queries, bias)
        for block in range(SEQ // BLOCK):
            probs = probabilities(query_h, key, rel_keys, bias, block, length)
            total[block] = total[block] + dot_nn(probs.astype(bf16), values_h)
    for block in range(SEQ // BLOCK):
        context[block] = total[block].astype(bf16)


def attend_back_kernel(lengths, heads_in, rel, grad_context, grads, grad_rel, bias, probs_ref, grad_ref):
    length = lengths[pl.program_id(0)]
    query, key, values = (heads_in[:, part].reshape(SEQ, 128) for part in range(3))
    grad_ctx = grad_context[...].reshape(SEQ, 128)
    rel_keys, rel_queries = rel[:, :128], rel[:, 128:]
    blocks = SEQ // BLOCK
    first = lax.broadcasted_iota(jnp.int32, (BLOCK, BLOCK), 0)
    second = lax.broadcasted_iota(jnp.int32, (BLOCK, BLOCK), 1)
    mirror = jnp.where(first + second == BLOCK - 1, 1.0, 0.0).astype(bf16)

    @pl.when(pl.program_id(0) == 0)
    def _():
        grad_rel[...] = jnp.zeros_like(grad_rel)

    grad_q, grad_k, grad_v = ([0.0] * blocks for _ in range(3))
    for head in range(2):
        query_h, key_h, ctx_h = (one_head(part, head) for part in (query, key, grad_ctx))
        rel_keys_h, rel_queries_h = one_head(rel_keys, head), one_head(rel_queries, head)
        query_bias(key_h, rel_queries, bias)
        for block in range(blocks):
            probs = probabilities(query_h, key, rel_keys, bias, block, length)
            probs_ref[rows(block)] = probs.astype(bf16)
            grad_probs = dot_nt(ctx_h[rows(block)], values)
            inner = jnp.sum(probs * grad_probs, axis=1, keepdims=True)
            grad = (probs * (grad_probs - inner) * (1.0 / math.sqrt(3 * HEAD_DIM))).astype(bf16)
            grad_ref[rows(block)] = grad
            by_offset = unskew(dot_nn(mirror, grad)).astype(bf16)
            by_offset = dot_nn(mirror, by_offset).astype(bf16)
            grad_q[block] += dot_nn(grad, key_h) + dot_nn(by_offset, rel_keys_h[window(block)])
            grad_rel[window(block), :128] += dot_tn(by_offset, query_h[rows(block)])
        for block in range(blocks):
            grad = grad_ref[:, rows(block)]
            by_offset = unskew(dot_nt(mirror, grad)).astype(bf16)
            by_offset = dot_nn(mirror, by_offset).astype(bf16)
            grad_k[block] += dot_tn(grad, query_h) + dot_nn(by_offset, rel_queries_h[window(block)])
            grad_v[block] += dot_tn(probs_ref[:, rows(block)], ctx_h)
            grad_rel[window(block), 128:] += dot_tn(by_offset, key_h[rows(block)])
    for block in range(blocks):
        grads[block, 0] = grad_q[block].astype(bf16)
        grads[block, 1] = grad_k[block].astype(bf16)
        grads[block, 2] = grad_v[block].astype(bf16)


def attend(lengths, heads_in, rel):
    return pl.pallas_call(
        attend_kernel,
        grid=(2,),
        in_specs=[
            pl.BlockSpec(memory_space=pltpu.SMEM),
            pl.BlockSpec((4, 3, 128, 128), lambda row: (row, 0, 0, 0)),
            pl.BlockSpec((2 * SEQ, 256), lambda row: (0, 0)),
        ],
        out_specs=pl.BlockSpec((4, 128, 128), lambda row: (row, 0, 0)),
        out_shape=jax.ShapeDtypeStruct((8, 128, 128), bf16),
        scratch_shapes=[pltpu.VMEM((SEQ, SEQ), f32)],
        compiler_params=pltpu.CompilerParams(vmem_limit_bytes=48 * 2**20),
        name="attend",
    )(lengths, heads_in, rel)


def attend_back(lengths, heads_in, rel, grad_context):
    return pl.pallas_call(
        attend_back_kernel,
        grid=(2,),
        in_specs=[
            pl.BlockSpec(memory_space=pltpu.SMEM),
            pl.BlockSpec((4, 3, 128, 128), lambda row: (row, 0, 0, 0)),
            pl.BlockSpec((2 * SEQ, 256), lambda row: (0, 0)),
            pl.BlockSpec((4, 128, 128), lambda row: (row, 0, 0)),
        ],
        out_specs=[
            pl.BlockSpec((4, 3, 128, 128), lambda row: (row, 0, 0, 0)),
            pl.BlockSpec((2 * SEQ, 256), lambda row: (0, 0)),
        ],
        out_shape=[
            jax.ShapeDtypeStruct((8, 3, 128, 128), bf16),
            jax.ShapeDtypeStruct((2 * SEQ, 256), f32),
        ],
        scratch_shapes=[
            pltpu.VMEM((SEQ, SEQ), f32),
            pltpu.VMEM((SEQ, SEQ), bf16),
            pltpu.VMEM((SEQ, SEQ), bf16),
        ],
        compiler_params=pltpu.CompilerParams(vmem_limit_bytes=48 * 2**20),
        name="attend_back",
    )(lengths, heads_in, rel, grad_context)


def swap(value):
    return lax.ppermute(value, "core", [(0, 1), (1, 0)])


def exchange(value, axes):
    return lax.all_to_all(value, axes, 0, 0, tiled=True)


def per_device(
    tokens,
    w_project,
    w_attend,
    first_gain,
    first_shift,
    w_expand,
    w_reduce,
    second_gain,
    second_shift,
    position_table,
    w_query,
    w_key,
    lengths,
    cotangent,
):
    core = lax.axis_index("core")
    column = lax.axis_index(COLUMN)
    local = tokens.shape[0]
    pair = 2 * local
    highest = lax.Precision.HIGHEST
    column_bucket = bucket_values(SEQ - 1 - np.arange(2 * SEQ - 1), SPAN)
    column_ids = jnp.asarray(np.append(column_bucket, 0))
    fold = np.append(column_bucket, -1)[None, :] == np.arange(2 * SPAN)[:, None]
    fold = jnp.asarray(fold.astype(np.float32)).astype(bf16)

    def by_core(zero, one):
        return jnp.where(core == 0, zero, one)

    def in_order(mine, theirs):
        return by_core(mine, theirs), by_core(theirs, mine)

    def both(value):
        return jnp.concatenate([value, swap(value)], axis=0)

    def sum_pair(partial):
        got = swap(partial)
        return partial + jnp.concatenate([got[local:], got[:local]], axis=0)

    vectors = jnp.stack([first_gain, first_shift, second_gain, second_shift])
    packet = jnp.concatenate(
        [
            w_project.T,
            position_table.T.reshape(4, D),
            jnp.pad(vectors, ((0, 0), (0, D - 8))),
        ],
        axis=0,
    )
    gathered = lax.all_gather(packet, DEVICES, axis=0, tiled=False).reshape(2, 8, 8, 32, D)
    project_t = gathered[..., :24, :].transpose(2, 0, 1, 3, 4).reshape(3 * D, D)
    table_t = gathered[..., 24:28, :].transpose(2, 0, 1, 3, 4).reshape(D, 2 * SPAN)
    vec = gathered[..., 28:, :8].transpose(3, 2, 0, 1, 4).reshape(4, D).astype(f32)
    gain_one, shift_one, gain_two, shift_two = vec[0], vec[1], vec[2], vec[3]

    position_weights = lax.all_gather(
        jnp.concatenate([w_key, w_query], axis=1), DP, axis=0, tiled=True
    )

    reduce_rows = jnp.moveaxis(w_reduce.T.reshape(8, 8, 2, 256), 2, 0).reshape(2, 8, 2048)
    mine, theirs = in_order(reduce_rows[0], reduce_rows[1])
    reduce_rows = jnp.concatenate(in_order(mine, swap(theirs)), axis=0)
    attend_rows = w_attend.T
    attend_rows = jnp.concatenate(in_order(attend_rows, swap(attend_rows)), axis=0)
    packet = jnp.concatenate(
        [w_expand.T, reduce_rows[:, :D], reduce_rows[:, D:], attend_rows], axis=0
    )
    gathered = lax.all_gather(packet, CHIPS, axis=0, tiled=False).reshape(8, 8, 80, D)
    expand_t = gathered[..., :32, :].transpose(1, 0, 2, 3).reshape(2048, D)
    reduce_t = (
        gathered[..., 32:64, :]
        .reshape(8, 8, 2, 2, 8, D)
        .transpose(1, 3, 0, 4, 2, 5)
        .reshape(D, 2048)
    )
    attend_t = (
        gathered[..., 64:, :].reshape(8, 8, 2, 8, D).transpose(1, 2, 0, 3, 4).reshape(D, D)
    )

    packed = dot_nt(tokens, project_t).astype(bf16)
    heads_in = exchange(packed.reshape(local, 3, 8, 128).transpose(2, 1, 0, 3), GROUP)
    rel = dot_tn(table_t, position_weights).astype(bf16)[column_ids]
    context = exchange(attend(lengths, heads_in, rel), GROUP)
    context = context.transpose(1, 0, 2).reshape(local, D)
    halves = in_order(context[:, :512], context[:, 512:])
    context_half = jnp.concatenate([halves[0], swap(halves[1])], axis=0)
    tokens_two = both(tokens)
    cotangent_two = both(cotangent).astype(f32)

    resid1 = both(tokens.astype(f32) + dot_nt(context, attend_t))
    first_norm, scaled_one, inverse_one = normalize(resid1, gain_one, shift_one)
    first_two = first_norm.astype(bf16)
    inner = dot_nt(first_two, expand_t)
    activ = smooth_gate(inner).astype(bf16)
    ffn = sum_pair(dot_nt(activ, reduce_t))
    output, scaled_two, inverse_two = normalize(first_norm + ffn, gain_two, shift_two)
    grad_resid2 = normalize_back(cotangent_two, scaled_two, inverse_two, gain_two)
    grad_gain2 = jnp.sum((cotangent_two * scaled_two)[:local], axis=0)
    grad_shift2 = jnp.sum(cotangent_two[:local], axis=0)
    grad_ffn = grad_resid2.astype(bf16)
    grad_reduce_t = dot_tn(grad_ffn, activ).astype(bf16)
    grad_activ = dot_nn(grad_ffn, reduce_t)
    gate_value, gate_pull = jax.vjp(smooth_gate, inner)
    grad_inner = gate_pull(grad_activ)[0].astype(bf16)
    grad_expand_t = dot_tn(grad_inner, first_two).astype(bf16)
    grad_first = grad_resid2 + sum_pair(dot_nn(grad_inner, expand_t))
    grad_resid1 = normalize_back(grad_first, scaled_one, inverse_one, gain_one)
    grad_gain1 = jnp.sum((grad_first * scaled_one)[:local], axis=0)
    grad_shift1 = jnp.sum(grad_first[:local], axis=0)
    grad_attended = grad_resid1.astype(bf16)
    grad_attend_t = dot_tn(grad_attended, context_half).astype(bf16)
    grad_context = dot_nn(grad_attended[:local], attend_t).astype(bf16)

    def scatter(blocks):
        received = exchange(blocks, COLUMN + GROUP)
        return jnp.sum(received.astype(f32), axis=0)

    grad_ctx = exchange(grad_context.reshape(local, 8, 128).transpose(1, 0, 2), GROUP)
    expand_sum = scatter(grad_expand_t.reshape(64, 32, D))
    reduce_blocks = grad_reduce_t.reshape(8, 2, 8, 8, 2048).transpose(0, 2, 1, 3, 4)
    reduce_sum = scatter(reduce_blocks.reshape(64, 16, 2048))
    attend_blocks = grad_attend_t.reshape(8, 2, 8, 8, 512).transpose(0, 2, 1, 3, 4)
    attend_sum = scatter(attend_blocks.reshape(64, 16, 512))

    grads, rel_grad = attend_back(lengths, heads_in, rel, grad_ctx)
    grad_packed = exchange(grads, GROUP).transpose(2, 1, 0, 3).reshape(local, 3 * D)
    tokens_grad = grad_resid1[:local] + dot_nn(grad_packed, project_t)
    grad_own = lax.dynamic_index_in_dim(
        both(grad_packed).reshape(pair, 8, 2, 192), core, axis=2, keepdims=False
    )
    grad_project_t = dot_tn(grad_own.reshape(pair, 1536), tokens_two).astype(bf16)
    grad_project = scatter(grad_project_t.reshape(64, 24, D)).T

    grad_expand = expand_sum.T
    mine, theirs = in_order(reduce_sum[:8], reduce_sum[8:])
    parts = in_order(mine, swap(theirs))
    grad_reduce = jnp.stack([part.reshape(8, 8, 256) for part in parts], axis=2)
    grad_reduce = grad_reduce.reshape(8, FF).T
    mine, theirs = in_order(attend_sum[:8], attend_sum[8:])
    grad_attend = jnp.concatenate(in_order(mine, swap(theirs)), axis=1).T

    vectors = jnp.stack([grad_gain1, grad_shift1, grad_gain2, grad_shift2])
    vectors = vectors.reshape(4, 128, 8).transpose(1, 0, 2).reshape(128, 1, 32)
    vectors = jnp.sum(exchange(vectors, EVERY), axis=0).reshape(4, 8)

    upper = rel_grad.astype(bf16)
    lower = (rel_grad - upper.astype(f32)).astype(bf16)
    rel_grad = dot_nn(fold, upper) + dot_nn(fold, lower)
    rel_grad = rel_grad + swap(rel_grad)
    rel_grad = by_core(rel_grad[:, :128], rel_grad[:, 128:]).astype(bf16)
    rel_grad = exchange(jnp.broadcast_to(rel_grad[None], (8, 2 * SPAN, 128)), COLUMN)
    rel_grad = jnp.sum(rel_grad.astype(f32), axis=0)
    rel_key_grad, rel_query_grad = in_order(rel_grad, swap(rel_grad))
    own = 64 * (2 * column + core)
    table_own = lax.dynamic_slice_in_dim(table_t, own, 64, axis=0).astype(f32)
    grad_key = jnp.dot(table_own, rel_key_grad, precision=highest)
    grad_query = jnp.dot(table_own, rel_query_grad, precision=highest)
    weights_own = lax.dynamic_slice_in_dim(position_weights, own, 64, axis=0).astype(f32)
    table_part = lax.dot_general(
        weights_own,
        jnp.concatenate([rel_key_grad, rel_query_grad], axis=1),
        (((1,), (1,)), ((), ())),
        precision=highest,
    )
    grad_table = jnp.sum(exchange(table_part.reshape(8, 8, 2 * SPAN), GROUP), axis=0).T

    return (
        output[:local].astype(bf16),
        tokens_grad.astype(bf16),
        grad_project,
        grad_attend,
        vectors[0],
        vectors[1],
        grad_expand,
        grad_reduce,
        vectors[2],
        vectors[3],
        grad_table,
        grad_query,
        grad_key,
    )


def solution(mesh):
    parts = Mesh(mesh.devices.reshape(2, 4, 2, 4, 2), EVERY)
    in_specs = (
        P(EVERY, None),
        P(None, EVERY),
        P(None, EVERY),
        P(EVERY),
        P(EVERY),
        P(None, EVERY),
        P(None, EVERY),
        P(EVERY),
        P(EVERY),
        P(None, EVERY),
        P(DP, GROUP),
        P(DP, GROUP),
        P(DP),
        P(EVERY, None),
    )
    out_specs = (
        P(EVERY, None),
        P(EVERY, None),
        P(None, EVERY),
        P(None, EVERY),
        P(EVERY),
        P(EVERY),
        P(None, EVERY),
        P(None, EVERY),
        P(EVERY),
        P(EVERY),
        P(None, EVERY),
        P(DP, GROUP),
        P(DP, GROUP),
    )
    return jax.shard_map(
        per_device, mesh=parts, in_specs=in_specs, out_specs=out_specs, check_vma=False
    )
```

time: 785 us -> 554 us (0.71)
  the two profiles are of different devices: /device:TPU:5 before, /device:TPU:0 now
where the time goes in v2:
time: 554 us; the launch traced here: 543 us
  waiting for transfers between devices  269 us (49%)
  starting transfers between devices  55.5 us (10%)
  local copies, waits for them, and re-layouts  54.9 us (10%)
  matrix products  41.4 us (7%)
  Pallas kernels  37.7 us (7%)
  blocking collectives  37.3 us (7%)
  other arithmetic  31.5 us (6%)
  between operations  15.5 us (3%)
    all_to_all x10, waiting for transfers between devices, exchange(): return lax.all_to_all(value, axes, 0, 0, tiled=True)  178 us
    all_to_all x10, starting transfers between devices, exchange(): return lax.all_to_all(value, axes, 0, 0, tiled=True)  52.5 us
    all_gather x1, waiting for transfers between devices, per_device(): lax.all_gather(packet, DEVICES, axis=0, tiled=False).reshape(2, 8, 8, 32, D)  45.6 us
    all_gather x1, waiting for transfers between devices, per_device(): lax.all_gather(packet, CHIPS, axis=0, tiled=False).reshape(8, 8, 80, D)  39 us
    pallas_call x1, Pallas kernels, attend_back(): pl.pallas_call(attend_back_kernel, grid=(2,), in_specs=[pl.BlockSpec(memo...  28 us
    all_gather x1, blocking collectives, per_device(): lax.all_gather(jnp.concatenate([w_key, w_query], axis=1), DP, axis=0, til...  22.6 us
    all_to_all x1, blocking collectives, exchange(): return lax.all_to_all(value, axes, 0, 0, tiled=True)  14.6 us
    dot_general x4, matrix products, dot_nt(): lax.dot_general(left, right, (((1,), (1,)), ((), ())), preferred_element_...  12.4 us
  transfers between devices with their start and end apart: 25, of which 16 were waited for; matrix products, arithmetic and copies ran while one was open for 16% of the time, Pallas kernels for 2%

profile of v2, /device:TPU:0, one launch (start us, length us, event | category | flops | bytes accessed | tf_op | source)
XLA Modules:
  0.0 543.2 jit_solution(7298381732568400679)
XLA Ops:
  16.2 22.6 %all_gather.17 = bf16[1024,256]{1,0:T(8,128)(2,1)} all-gather(bf16[64,256]{1,0:T(8,128)(2,1)S(1)} %pad_maximum_fusion.5), channel_id=1, replica_groups=mesh['yl'=2,'x'=4,'core'=2,'z'=4,'yh'=2] {'yl','x','core'}, dimensions={0}, use_global_device_ids=true | all-gather | bytes 557056 | tf_op jit(solution)/shard_map/all_gather | solution.py:281
  38.8 45.6 %all-gather.5.cloned.1.call-done = bf16[4096,1024]{1,0:T(8,128)(2,1)} async-done(((bf16[32,1024]{1,0:T(8,128)(2,1)}), bf16[4096,1024]{1,0:T(8,128)(2,1)}) %all-gather.5.cloned.1.call-update) | async-done | bytes 8388624 | tf_op jit(solution)/shard_map/all_gather | solution.py:275
  84.4 3.5 slice_bitcast_fusion
  92.8 4.3 all-to-all-start
  97.1 2.1 slice_bitcast_fusion.3
  102.5 3.9 gather_fusion
  107.5 5.6 %all-to-all-done.heads_in = bf16[8,3,128,128]{3,2,1,0:T(8,128)(2,1)S(1)} async-done(((bf16[8,3,128,128]{3,2,1,0:T(8,128)(2,1)}), bf16[8,3,128,128]{3,2,1,0:T(8,128)(2,1)S(1)}, u32[]{:S(2)}, u32[]{:S(2)}) %all-to-all-start) | async-done | bytes 786464 | tf_op jit(solution)/shard_map/all_to_all | solution.py:224
  113.1 9.7 %attend.1 = bf16[8,128,128]{2,1,0:T(8,128)(2,1)} custom-call(s32[2]{0:T(128)S(1)} %copy-done, bf16[8,3,128,128]{3,2,1,0:T(8,128)(2,1)S(1)} %all-to-all-done.heads_in, bf16[1024,256]{1,0:T(8,128)(2,1)S(1)} %gather_fusion), custom_call_target="tpu_custom_call" | custom-call | tf_op jit(solution)/shard_map/attend/pallas_call | solution.py:175
  122.8 3.4 all-to-all-start.1
  126.6 11.2 %all-to-all-done.1 = bf16[8,128,128]{2,1,0:T(8,128)(2,1)S(1)} async-done(((bf16[8,128,128]{2,1,0:T(8,128)(2,1)}), bf16[8,128,128]{2,1,0:T(8,128)(2,1)S(1)}, u32[]{:S(2)}, u32[]{:S(2)}) %all-to-all-start.1) | async-done | bytes 262176 | tf_op jit(solution)/shard_map/all_to_all | solution.py:224
  138.1 39.0 %all-gather.7.cloned.1.call-done = bf16[5120,1024]{1,0:T(8,128)(2,1)} async-done(((bf16[80,1024]{1,0:T(8,128)(2,1)}), bf16[5120,1024]{1,0:T(8,128)(2,1)}) %all-gather.7.cloned.1.call-update) | async-done | bytes 10485776 | tf_op jit(solution)/shard_map/all_gather | solution.py:293
  177.1 1.9 slice_bitcast_fusion.2
  182.5 3.7 fusion.63
  186.2 10.6 %copy.100 = bf16[8,8,2,2,8,1024]{5,2,4,0,3,1:T(2,128)(2,1)S(1)} copy(bf16[8,8,2,2,8,1024]{5,4,3,2,1,0:T(8,128)(2,1)} %bitcast.130) | data formatting | bytes 8388608 | tf_op jit(solution)/shard_map/reshape | solution.py:297
  201.9 7.4 %multiply_convert_fusion = (bf16[256,2048]{1,0:T(8,128)(2,1)S(1)}, f32[256,2048]{1,0:T(8,128)}, f32[256,2048]{1,0:T(8,128)}) fusion(bf16[2048,1024]{1,0:T(8,128)(2,1)S(1)} %bitcast.141, f32[256,1024]{1,0:T(8,128)S(1)} %subtract_multiply_fusion.3, f32[1024]{0:T(1024)S(1)} %add.89, f32[1024]{0:T(1024)S(1)} %mul.132), kind=kOutput, calls=%fused_computation.16 | convolution fusion | flops 1108606976 | bytes 10493952 | tf_op jit(solution)/shard_map/dot_general | solution.py:70
  209.3 2.3 fusion.67
  212.2 2.8 collective-permute-done.3
  220.0 3.3 add_convert_fusion
  223.4 2.2 fusion.68
  225.8 2.0 fusion.57
  230.0 1.9 multiply_reduce_fusion.4
  236.5 6.3 %all-to-all-start.2 = ((bf16[8,128,128]{2,1,0:T(8,128)(2,1)}), bf16[8,128,128]{2,1,0:T(8,128)(2,1)S(1)}, u32[]{:S(2)}, u32[]{:S(2)}) async-start(bf16[8,128,128]{2,1,0:T(8,128)(2,1)} %bitcast.32), calls=%async_computation.2 | async-start | bytes 524288 | tf_op jit(solution)/shard_map/all_to_all | solution.py:224
  242.7 2.0 multiply_reduce_fusion.6
  246.5 5.3 all-to-all-done.2.grad_context
  251.8 28.0 %attend_back.1 = (bf16[8,3,128,128]{3,2,1,0:T(8,128)(2,1)}, f32[1024,256]{1,0:T(8,128)S(1)}) custom-call(s32[2]{0:T(128)S(1)} %copy-done, bf16[8,3,128,128]{3,2,1,0:T(8,128)(2,1)S(1)} %all-to-all-done.heads_in, bf16[1024,256]{1,0:T(8,128)(2,1)S(1)} %gather_fusion, bf16[8,128,128]{2,1,0:T(8,128)(2,1)S(1)} %all-to-all-done.2.grad_context), custom_call_target="tpu_custom_call" | custom-call | tf_op jit(solution)/shard_map/attend_back/pallas_call | solution.py:192
  281.0 14.6 %all_to_all.55 = f32[128,1,32]{2,1,0:T(1,128)} all-to-all(f32[128,1,32]{2,1,0:T(1,128)S(1)} %copy.112), channel_id=1, replica_groups=mesh['yl'=2,'x'=4,'core'=2,'z'=4,'yh'=2] {'yl','x','core','z','yh'}, dimensions={0} | all-to-all | bytes 32768 | tf_op jit(solution)/shard_map/all_to_all | solution.py:224
  295.6 3.5 all-to-all-start.3
  299.4 13.6 %all-to-all-done.3 = bf16[8,3,128,128]{3,2,1,0:T(8,128)(2,1)S(1)} async-done(((bf16[8,3,128,128]{3,2,1,0:T(8,128)(2,1)}), bf16[8,3,128,128]{3,2,1,0:T(8,128)(2,1)S(1)}, u32[]{:S(2)}, u32[]{:S(2)}) %all-to-all-start.3) | async-done | bytes 786464 | tf_op jit(solution)/shard_map/all_to_all | solution.py:224
  314.3 3.6 all-to-all-start.9
  322.0 10.0 %all-to-all-done.9 = bf16[8,512,128]{2,1,0:T(8,128)(2,1)S(1)} async-done(((bf16[8,512,128]{2,1,0:T(8,128)(2,1)}), bf16[8,512,128]{2,1,0:T(8,128)(2,1)S(1)}, u32[]{:S(2)}, u32[]{:S(2)}) %all-to-all-start.9) | async-done | bytes 1048608 | tf_op jit(solution)/shard_map/all_to_all | solution.py:224
  332.1 5.9 %all-to-all-start.5 = ((bf16[64,16,512]{2,1,0:T(8,128)(2,1)}), bf16[64,16,512]{2,1,0:T(8,128)(2,1)}, u32[]{:S(2)}, u32[]{:S(2)}) async-start(bf16[64,16,512]{2,1,0:T(8,128)(2,1)} %bitcast.145), calls=%async_computation.5 | async-start | bytes 2097152 | tf_op jit(solution)/shard_map/all_to_all | solution.py:224
  343.4 13.2 %all-to-all-done.5 = bf16[64,16,512]{2,1,0:T(8,128)(2,1)} async-done(((bf16[64,16,512]{2,1,0:T(8,128)(2,1)}), bf16[64,16,512]{2,1,0:T(8,128)(2,1)}, u32[]{:S(2)}, u32[]{:S(2)}) %all-to-all-start.5) | async-done | bytes 1048608 | tf_op jit(solution)/shard_map/all_to_all | solution.py:224
  356.6 3.4 all-to-all-start.10
  360.0 2.8 convolution_convert_fusion.1
  362.8 2.3 copy.113
  365.2 2.9 all-to-all-done.10
  368.1 6.5 %all-to-all-start.8 = ((bf16[64,16,2048]{2,1,0:T(8,128)(2,1)}), bf16[64,16,2048]{2,1,0:T(8,128)(2,1)}, u32[]{:S(2)}, u32[]{:S(2)}) async-start(bf16[64,16,2048]{2,1,0:T(8,128)(2,1)} %bitcast.128), calls=%async_computation.8 | async-start | bytes 8388608 | tf_op jit(solution)/shard_map/all_to_all | solution.py:224
  374.7 3.3 convolution_convert_fusion.2
  378.0 48.9 %all-to-all-done.8 = bf16[64,16,2048]{2,1,0:T(8,128)(2,1)} async-done(((bf16[64,16,2048]{2,1,0:T(8,128)(2,1)}), bf16[64,16,2048]{2,1,0:T(8,128)(2,1)}, u32[]{:S(2)}, u32[]{:S(2)}) %all-to-all-start.8) | async-done | bytes 4194336 | tf_op jit(solution)/shard_map/all_to_all | solution.py:224
  426.9 7.8 %all-to-all-start.7 = ((bf16[64,32,1024]{2,1,0:T(8,128)(2,1)}), bf16[64,32,1024]{2,1,0:T(8,128)(2,1)}, u32[]{:S(2)}, u32[]{:S(2)}) async-start(bf16[64,32,1024]{2,1,0:T(8,128)(2,1)} %bitcast.122), calls=%async_computation.7 | async-start | bytes 8388608 | tf_op jit(solution)/shard_map/all_to_all | solution.py:224
  436.4 2.0 convert_reduce_fusion.4
  438.6 2.6 convolution_convert_fusion
  441.2 46.7 %all-to-all-done.7 = bf16[64,32,1024]{2,1,0:T(8,128)(2,1)} async-done(((bf16[64,32,1024]{2,1,0:T(8,128)(2,1)}), bf16[64,32,1024]{2,1,0:T(8,128)(2,1)}, u32[]{:S(2)}, u32[]{:S(2)}) %all-to-all-start.7) | async-done | bytes 4194336 | tf_op jit(solution)/shard_map/all_to_all | solution.py:224
  487.9 7.7 %all-to-all-start.4 = ((bf16[64,24,1024]{2,1,0:T(8,128)(2,1)}), bf16[64,24,1024]{2,1,0:T(8,128)(2,1)S(1)}, u32[]{:S(2)}, u32[]{:S(2)}) async-start(bf16[64,24,1024]{2,1,0:T(8,128)(2,1)} %bitcast.38), calls=%async_computation.4 | async-start | bytes 6291456 | tf_op jit(solution)/shard_map/all_to_all | solution.py:224
  496.4 4.8 fusion.7
  505.9 2.9 convert_reduce_fusion
  509.4 3.7 convert_reduce_fusion.1
  513.8 21.0 %all-to-all-done.4 = bf16[64,24,1024]{2,1,0:T(8,128)(2,1)S(1)} async-done(((bf16[64,24,1024]{2,1,0:T(8,128)(2,1)}), bf16[64,24,1024]{2,1,0:T(8,128)(2,1)S(1)}, u32[]{:S(2)}, u32[]{:S(2)}) %all-to-all-start.4) | async-done | bytes 3145760 | tf_op jit(solution)/shard_map/all_to_all | solution.py:224
  (211 shorter events, 62.9 us)
Async XLA Ops:
  7.2 77.2 %all-gather.5.cloned.1.call-start = ((), (), s32[]{:S(2)}) async-start(), calls=%async_computation.11 | async-start | bytes 8454144 | tf_op jit(solution)/shard_map/all_gather | solution.py:275
  10.1 167.0 %all-gather.7.cloned.1.call-start = ((), (), s32[]{:S(2)}) async-start(), calls=%async_computation.12 | async-start | bytes 10649600 | tf_op jit(solution)/shard_map/all_gather | solution.py:293
  10.2 2.4 collective-permute-start.1
  11.1 1.4 collective-permute-start
  92.8 20.3 %all-to-all-start = ((bf16[8,3,128,128]{3,2,1,0:T(8,128)(2,1)}), bf16[8,3,128,128]{3,2,1,0:T(8,128)(2,1)S(1)}, u32[]{:S(2)}, u32[]{:S(2)}) async-start(bf16[8,3,128,128]{3,2,1,0:T(8,128)(2,1)} %bitcast.11), calls=%async_computation | async-start | bytes 1572864 | tf_op jit(solution)/shard_map/all_to_all | solution.py:224
  102.5 10.6 %copy-start = (s32[2]{0:T(128)S(1)}, s32[2]{0:T(128)}, u32[]{:S(2)}) copy-start(s32[2]{0:T(128)} %lengths.3) | copy-start | bytes 28
  122.8 15.1 %all-to-all-start.1 = ((bf16[8,128,128]{2,1,0:T(8,128)(2,1)}), bf16[8,128,128]{2,1,0:T(8,128)(2,1)S(1)}, u32[]{:S(2)}, u32[]{:S(2)}) async-start(bf16[8,128,128]{2,1,0:T(8,128)(2,1)} %attend.1), calls=%async_computation.1 | async-start | bytes 524288 | tf_op jit(solution)/shard_map/all_to_all | solution.py:224
  138.0 41.2 %copy-start.24 = (bf16[128,8,128]{0,2,1:T(8,128)(2,1)}, bf16[128,8,128]{0,2,1:T(8,128)(2,1)S(1)}, u32[]{:S(2)}) copy-start(bf16[128,8,128]{0,2,1:T(8,128)(2,1)S(1)} %copy.94) | copy-start | bytes 786436
  177.1 5.4 copy-start.7
  181.5 18.3 %collective-permute-start.2 = (f32[128,1024]{1,0:T(8,128)S(1)}, f32[128,1024]{1,0:T(8,128)S(1)}, u32[]{:S(2)}, u32[]{:S(2)}) collective-permute-start(f32[128,1024]{1,0:T(8,128)S(1)} %convolution_add_fusion.1), channel_id=1, source_target_pairs={{0,8},{8,0},{1,9},{9,1},{2,10},{10,2},{3,11},{11,3},{4,12},{12,4},... | collective-permute-start | bytes 1572872 | tf_op jit(solution)/shard_map/ppermute | solution.py:220
  198.3 10.9 %copy-start.17 = (bf16[128,8,2,1024]{3,1,2,0:T(8,128)(2,1)}, bf16[128,8,2,1024]{3,1,2,0:T(8,128)(2,1)S(1)}, u32[]{:S(2)}) copy-start(bf16[128,8,2,1024]{3,1,2,0:T(8,128)(2,1)S(1)} %copy.119) | copy-start | bytes 12582916
  200.3 9.0 %copy-start.41 = (f32[256]{0:T(256)}, f32[256]{0:T(256)S(1)}, u32[]{:S(2)}) copy-start(f32[256]{0:T(256)S(1)} %add_rsqrt_fusion.1) | copy-start | bytes 3076
  211.6 3.4 collective-permute-start.3
  211.6 6.8 %collective-permute-start.4 = (bf16[128,1024]{1,0:T(8,128)(2,1)S(1)}, bf16[128,1024]{1,0:T(8,128)(2,1)}, u32[]{:S(2)}, u32[]{:S(2)}) collective-permute-start(bf16[128,1024]{1,0:T(8,128)(2,1)S(1)} %copy-done.11), channel_id=1, source_target_pairs={{0,8},{8,0},{1,9},{9,1},{2,10},{10,2},{3,11},{11,3},{4,12},{12,4},... | collective-permute-start | bytes 786440 | tf_op jit(solution)/shard_map/ppermute | solution.py:220
  214.9 5.0 copy-start.44
  216.4 3.6 copy-start.18
  218.4 5.0 copy-start.35
  219.9 10.0 %copy-start.4 = (f32[256,1024]{1,0:T(8,128)}, f32[256,1024]{1,0:T(8,128)S(1)}, u32[]{:S(2)}) copy-start(f32[256,1024]{1,0:T(8,128)S(1)} %get-tuple-element.28) | copy-start | bytes 3145732
  219.9 3.5 copy-start.37
  225.6 3.0 collective-permute-start.5
  236.5 15.3 %all-to-all-start.2 = ((bf16[8,128,128]{2,1,0:T(8,128)(2,1)}), bf16[8,128,128]{2,1,0:T(8,128)(2,1)S(1)}, u32[]{:S(2)}, u32[]{:S(2)}) async-start(bf16[8,128,128]{2,1,0:T(8,128)(2,1)} %bitcast.32), calls=%async_computation.2 | async-start | bytes 524288 | tf_op jit(solution)/shard_map/all_to_all | solution.py:224
  251.8 28.0 %copy-start.10 = (bf16[512,1024]{1,0:T(8,128)(2,1)S(1)}, bf16[512,1024]{1,0:T(8,128)(2,1)}, u32[]{:S(2)}) copy-start(bf16[512,1024]{1,0:T(8,128)(2,1)} %constant.131) | copy-start | bytes 3145732
  280.8 18.4 %collective-permute-start.11 = (f32[512,256]{0,1:T(8,128)S(1)}, f32[512,256]{0,1:T(8,128)S(1)}, u32[]{:S(2)}, u32[]{:S(2)}) collective-permute-start(f32[512,256]{0,1:T(8,128)S(1)} %fusion.6), channel_id=1, source_target_pairs={{0,8},{8,0},{1,9},{9,1},{2,10},{10,2},{3,11},{11,3},{4,12},{12,4},... | collective-permute-start | bytes 1572872 | tf_op jit(solution)/shard_map/ppermute | solution.py:220
  295.6 17.5 %all-to-all-start.3 = ((bf16[8,3,128,128]{3,2,1,0:T(8,128)(2,1)}), bf16[8,3,128,128]{3,2,1,0:T(8,128)(2,1)S(1)}, u32[]{:S(2)}, u32[]{:S(2)}) async-start(bf16[8,3,128,128]{3,2,1,0:T(8,128)(2,1)} %get-tuple-element.15), calls=%async_computation.3 | async-start | bytes 1572864 | tf_op jit(solution)/shard_map/all_to_all | solution.py:224
  299.3 18.6 %copy-start.25 = (bf16[128,8,128]{0,2,1:T(8,128)(2,1)S(1)}, bf16[128,8,128]{0,2,1:T(8,128)(2,1)}, u32[]{:S(2)}) copy-start(bf16[128,8,128]{0,2,1:T(8,128)(2,1)} %copy-done.24) | copy-start | bytes 786436
  313.1 6.3 %copy-start.20 = (bf16[8,3,128,128]{3,2,1,0:T(8,128)(2,1)}, bf16[8,3,128,128]{3,2,1,0:T(8,128)(2,1)S(1)}, u32[]{:S(2)}) copy-start(bf16[8,3,128,128]{3,2,1,0:T(8,128)(2,1)S(1)} %all-to-all-done.3) | copy-start | bytes 2359300
  314.3 17.7 %all-to-all-start.9 = ((bf16[8,512,128]{2,1,0:T(8,128)(2,1)}), bf16[8,512,128]{2,1,0:T(8,128)(2,1)S(1)}, u32[]{:S(2)}, u32[]{:S(2)}) async-start(bf16[8,512,128]{2,1,0:T(8,128)(2,1)} %broadcast_in_dim.5), calls=%async_computation.9 | async-start | bytes 2097152 | tf_op jit(solution)/shard_map/all_to_all | solution.py:224
  317.9 1.4 collective-permute-start.8
  332.1 24.6 %all-to-all-start.5 = ((bf16[64,16,512]{2,1,0:T(8,128)(2,1)}), bf16[64,16,512]{2,1,0:T(8,128)(2,1)}, u32[]{:S(2)}, u32[]{:S(2)}) async-start(bf16[64,16,512]{2,1,0:T(8,128)(2,1)} %bitcast.145), calls=%async_computation.5 | async-start | bytes 2097152 | tf_op jit(solution)/shard_map/all_to_all | solution.py:224
  338.0 22.0 %copy-start.5 = (f32[256,1024]{1,0:T(8,128)S(1)}, f32[256,1024]{1,0:T(8,128)}, u32[]{:S(2)}) copy-start(f32[256,1024]{1,0:T(8,128)} %copy-done.4) | copy-start | bytes 3145732
  338.0 22.0 %copy-start.14 = (bf16[128,1024]{1,0:T(8,128)(2,1)S(1)}, bf16[128,1024]{1,0:T(8,128)(2,1)}, u32[]{:S(2)}) copy-start(bf16[128,1024]{1,0:T(8,128)(2,1)} %param.29) | copy-start | bytes 786436
  340.0 1.6 collective-permute-start.12
  341.6 21.2 %copy-start.26 = (f32[512,128]{0,1:T(8,128)}, f32[512,128]{0,1:T(8,128)S(1)}, u32[]{:S(2)}) copy-start(f32[512,128]{0,1:T(8,128)S(1)} %get-tuple-element.40) | copy-start | bytes 786436
  356.6 11.5 %all-to-all-start.10 = ((f32[8,8,512]{2,1,0:T(8,128)}), f32[8,8,512]{2,1,0:T(8,128)S(1)}, u32[]{:S(2)}, u32[]{:S(2)}) async-start(f32[8,8,512]{2,1,0:T(8,128)} %convolution_bitcast_fusion), calls=%async_computation.10 | async-start | bytes 262144 | tf_op jit(solution)/shard_map/all_to_all | solution.py:224
  368.1 6.5 %copy-start.23 = (bf16[256,2048]{1,0:T(8,128)(2,1)S(1)}, bf16[256,2048]{1,0:T(8,128)(2,1)}, u32[]{:S(2)}) copy-start(bf16[256,2048]{1,0:T(8,128)(2,1)} %copy-done.22) | copy-start | bytes 3145732
  368.1 58.8 %all-to-all-start.8 = ((bf16[64,16,2048]{2,1,0:T(8,128)(2,1)}), bf16[64,16,2048]{2,1,0:T(8,128)(2,1)}, u32[]{:S(2)}, u32[]{:S(2)}) async-start(bf16[64,16,2048]{2,1,0:T(8,128)(2,1)} %bitcast.128), calls=%async_computation.8 | async-start | bytes 8388608 | tf_op jit(solution)/shard_map/all_to_all | solution.py:224
  426.9 7.8 %copy-start.21 = (bf16[8,3,128,128]{3,2,1,0:T(8,128)(2,1)S(1)}, bf16[8,3,128,128]{3,2,1,0:T(8,128)(2,1)}, u32[]{:S(2)}) copy-start(bf16[8,3,128,128]{3,2,1,0:T(8,128)(2,1)} %copy-done.20) | copy-start | bytes 2359300
  426.9 8.3 %copy-start.31 = (bf16[128,1024]{1,0:T(8,128)(2,1)S(1)}, bf16[128,1024]{1,0:T(8,128)(2,1)}, u32[]{:S(2)}) copy-start(bf16[128,1024]{1,0:T(8,128)(2,1)} %param.16) | copy-start | bytes 786436
  426.9 8.8 %copy-start.34 = (f32[128,1,32]{2,1,0:T(1,128)S(1)}, f32[128,1,32]{2,1,0:T(1,128)}, u32[]{:S(2)}) copy-start(f32[128,1,32]{2,1,0:T(1,128)} %all_to_all.55) | copy-start | bytes 49156
  426.9 61.0 %all-to-all-start.7 = ((bf16[64,32,1024]{2,1,0:T(8,128)(2,1)}), bf16[64,32,1024]{2,1,0:T(8,128)(2,1)}, u32[]{:S(2)}, u32[]{:S(2)}) async-start(bf16[64,32,1024]{2,1,0:T(8,128)(2,1)} %bitcast.122), calls=%async_computation.7 | async-start | bytes 8388608 | tf_op jit(solution)/shard_map/all_to_all | solution.py:224
  435.1 6.1 %copy-start.8 = (bf16[128,3,8,128]{0,3,2,1:T(8,128)(2,1)}, bf16[128,3,8,128]{0,3,2,1:T(8,128)(2,1)S(1)}, u32[]{:S(2)}) copy-start(bf16[128,3,8,128]{0,3,2,1:T(8,128)(2,1)S(1)} %copy.105) | copy-start | bytes 2359300
  435.1 3.4 collective-permute-start.6
  435.2 3.4 collective-permute-start.7
  487.9 46.9 %all-to-all-start.4 = ((bf16[64,24,1024]{2,1,0:T(8,128)(2,1)}), bf16[64,24,1024]{2,1,0:T(8,128)(2,1)S(1)}, u32[]{:S(2)}, u32[]{:S(2)}) async-start(bf16[64,24,1024]{2,1,0:T(8,128)(2,1)} %bitcast.38), calls=%async_computation.4 | async-start | bytes 6291456 | tf_op jit(solution)/shard_map/all_to_all | solution.py:224
  496.4 4.9 collective-permute-start.9
  496.4 4.9 copy-start.33
  496.4 5.5 %copy-start.27 = (f32[512,128]{0,1:T(8,128)S(1)}, f32[512,128]{0,1:T(8,128)}, u32[]{:S(2)}) copy-start(f32[512,128]{0,1:T(8,128)} %copy-done.26) | copy-start | bytes 786436
  508.8 4.3 collective-permute-start.10
  (22 other events, 44.6 us)
Sparse Core Ops, SparseCore 0:
  11.7 72.5 all-gather.4
  87.7 89.3 all-gather.6

commit v3 on v2

--- a/solution.py
+++ b/solution.py
@@ -56,10 +56,6 @@
         - scaled * jnp.mean(grad_scaled * scaled, axis=-1, keepdims=True)
     )
     return inverse * middle
-
-
-def smooth_gate(value):
-    return jax.nn.gelu(value, approximate=False)
 
 
 def dot_nn(left, right):
@@ -216,12 +212,386 @@
     )(lengths, heads_in, rel, grad_context)
 
 
+def owner_rows(block):
+    wide = block.astype(f32).reshape(8, 2, 8, block.shape[-1])
+    return jnp.swapaxes(wide, 0, 1).reshape(128, block.shape[-1]).astype(bf16)
+
+
+def owner_blocks(rows128):
+    wide = rows128.reshape(2, 8, 8, rows128.shape[-1])
+    return jnp.swapaxes(wide, 0, 1)
+
+
+def project_back_kernel(context, tokens, weights, resid):
+    rows_in = jnp.concatenate([context[group] for group in range(8)], axis=1)
+    resid[...] = tokens[...].astype(f32) + dot_nt(rows_in, owner_rows(weights[:, 0]))
+
+
+def project_back(context, tokens, gathered):
+    return pl.pallas_call(
+        project_back_kernel,
+        grid=(8,),
+        in_specs=[
+            pl.BlockSpec((8, 128, 128), lambda k: (0, 0, 0)),
+            pl.BlockSpec((128, 128), lambda k: (0, k)),
+            pl.BlockSpec((8, 1, 16, D), lambda k: (0, k, 4, 0)),
+        ],
+        out_specs=pl.BlockSpec((128, 128), lambda k: (0, k)),
+        out_shape=jax.ShapeDtypeStruct((128, D), f32),
+        compiler_params=pltpu.CompilerParams(vmem_limit_bytes=48 * 2**20),
+        name="project_back",
+    )(context, tokens, gathered)
+
+
+def ffn_kernel(mine, theirs, vec, expand, reduce, act, slope, partial, low):
+    phase, k = pl.program_id(0), pl.program_id(1)
+
+    @pl.when((phase == 0) & (k == 0))
+    def _():
+        for half, resid in enumerate((mine, theirs)):
+            first_norm, scaled, inverse = normalize(resid[...], vec[0:1], vec[1:2])
+            low[128 * half : 128 * (half + 1)] = first_norm.astype(bf16)
+
+    @pl.when(phase == 0)
+    def _():
+        inner = dot_nt(low[...], expand[:, 0].reshape(256, D))
+        spread = 0.5 + 0.5 * lax.erf(inner * math.sqrt(0.5))
+        act[k] = (inner * spread).astype(bf16)
+        density = jnp.exp(-0.5 * inner * inner) * (1.0 / math.sqrt(2.0 * math.pi))
+        slope[0] = spread + inner * density
+
+    @pl.when(phase == 1)
+    def _():
+        total = jnp.zeros((256, 128), f32)
+        for half in range(2):
+            rows_in = jnp.concatenate([act[4 * half + part] for part in range(4)], axis=1)
+            weights = owner_rows(reduce[:, 0, 16 * half : 16 * (half + 1)])
+            total = total + dot_nt(rows_in, weights)
+        partial[...] = total
+
+
+def ffn_forward(mine, theirs, vec, gathered):
+    whole = lambda phase, k: (0, 0)
+    return pl.pallas_call(
+        ffn_kernel,
+        grid=(2, 8),
+        in_specs=[
+            pl.BlockSpec((128, D), whole),
+            pl.BlockSpec((128, D), whole),
+            pl.BlockSpec((4, D), whole),
+            pl.BlockSpec((8, 1, 32, D), lambda phase, k: (0, jnp.where(phase == 0, k, 7), 0, 0)),
+            pl.BlockSpec((8, 1, 32, D), lambda phase, k: (0, jnp.where(phase == 0, 0, k), 1, 0)),
+        ],
+        out_specs=[
+            pl.BlockSpec((8, 256, 256), lambda phase, k: (0, 0, 0)),
+            pl.BlockSpec((1, 256, 256), lambda phase, k: (jnp.where(phase == 0, k, 7), 0, 0)),
+            pl.BlockSpec((256, 128), lambda phase, k: (0, jnp.where(phase == 0, 0, k))),
+        ],
+        out_shape=[
+            jax.ShapeDtypeStruct((8, 256, 256), bf16),
+            jax.ShapeDtypeStruct((8, 256, 256), f32),
+            jax.ShapeDtypeStruct((256, D), f32),
+        ],
+        scratch_shapes=[pltpu.VMEM((256, D), bf16)],
+        compiler_params=pltpu.CompilerParams(vmem_limit_bytes=48 * 2**20),
+        name="ffn_forward",
+    )(mine, theirs, vec, gathered, gathered)
+
+
+def ffn_back_kernel(
+    mine,
+    theirs,
+    vec,
+    ffn_own,
+    ffn_got,
+    cot_own,
+    cot_got,
+    act,
+    slope,
+    expand,
+    reduce,
+    output,
+    blocks,
+    partial,
+    sums,
+    low,
+    grad_ffn,
+    grad_act,
+):
+    phase, k = pl.program_id(0), pl.program_id(1)
+
+    @pl.when((phase == 0) & (k == 0))
+    def _():
+        sums[...] = jnp.zeros_like(sums)
+        for half, (resid, cot) in enumerate(((mine, cot_own), (theirs, cot_got))):
+            span = slice(128 * half, 128 * (half + 1))
+            cross = slice(128 * (1 - half), 128 * (2 - half))
+            first_norm, scaled, inverse = normalize(resid[...], vec[0:1], vec[1:2])
+            low[span] = first_norm.astype(bf16)
+            resid2 = first_norm + (ffn_own[span] + ffn_got[cross])
+            normed, scaled, inverse = normalize(resid2, vec[2:3], vec[3:4])
+            grad = cot[...].astype(f32)
+            if half == 0:
+                output[...] = normed.astype(bf16)
+                sums[2:3] = jnp.sum(grad * scaled, axis=0, keepdims=True)
+                sums[3:4] = jnp.sum(grad, axis=0, keepdims=True)
+            grad = normalize_back(grad, scaled, inverse, vec[2:3])
+            partial[span] = 0.5 * grad
+            grad = grad.astype(bf16)
+            for chunk in range(8):
+                grad_ffn[chunk, span] = grad[:, 128 * chunk : 128 * (chunk + 1)]
+        grad_act[...] = jnp.zeros_like(grad_act)
+
+    @pl.when(phase == 0)
+    def _():
+        grad = grad_ffn[k]
+        for half in range(2):
+            weights = owner_rows(reduce[:, 0, 16 * half : 16 * (half + 1)])
+            made = []
+            for part in range(4):
+                chunk = 4 * half + part
+                grad_act[chunk] += dot_nn(grad, weights[:, 256 * part : 256 * (part + 1)])
+                made.append(dot_tn(grad, act[chunk]))
+            made = owner_blocks(jnp.concatenate(made, axis=1)).reshape(4, 2, 16, D)
+            blocks[0, :, 0, :, 16 * half : 16 * (half + 1)] = made.astype(bf16)
+
+    @pl.when(phase == 1)
+    def _():
+        weights = expand[:, 0].reshape(256, D)
+        grad = (slope[0] * grad_act[k]).astype(bf16)
+        blocks[0, :, 0] = dot_tn(grad, low[...]).astype(bf16).reshape(4, 2, 32, D)
+        partial[...] += dot_nn(grad, weights)
+
+
+def ffn_backward(mine, theirs, vec, ffn_own, ffn_got, cot_own, cot_got, act, slope, gathered):
+    whole = lambda phase, k: (0, 0)
+    return pl.pallas_call(
+        ffn_back_kernel,
+        grid=(2, 8),
+        in_specs=[
+            pl.BlockSpec((128, D), whole),
+            pl.BlockSpec((128, D), whole),
+            pl.BlockSpec((4, D), whole),
+            pl.BlockSpec((256, D), whole),
+            pl.BlockSpec((256, D), whole),
+            pl.BlockSpec((128, D), whole),
+            pl.BlockSpec((128, D), whole),
+            pl.BlockSpec((8, 256, 256), lambda phase, k: (0, 0, 0)),
+            pl.BlockSpec((1, 256, 256), lambda phase, k: (jnp.where(phase == 0, 0, k), 0, 0)),
+            pl.BlockSpec((8, 1, 32, D), lambda phase, k: (0, jnp.where(phase == 0, 0, k), 0, 0)),
+            pl.BlockSpec((8, 1, 32, D), lambda phase, k: (0, jnp.where(phase == 0, k, 7), 1, 0)),
+        ],
+        out_specs=[
+            pl.BlockSpec((128, D), whole),
+            pl.BlockSpec(
+                (1, 4, 1, 2, 32, D), lambda phase, k: (k % 4, 0, k // 4, 0, 1 - phase, 0)
+            ),
+            pl.BlockSpec((256, D), whole),
+            pl.BlockSpec((8, D), whole),
+        ],
+        out_shape=[
+            jax.ShapeDtypeStruct((128, D), bf16),
+            jax.ShapeDtypeStruct((4, 4, 2, 2, 80, D), bf16),
+            jax.ShapeDtypeStruct((256, D), f32),
+            jax.ShapeDtypeStruct((8, D), f32),
+        ],
+        scratch_shapes=[
+            pltpu.VMEM((256, D), bf16),
+            pltpu.VMEM((8, 256, 128), bf16),
+            pltpu.VMEM((8, 256, 256), f32),
+        ],
+        compiler_params=pltpu.CompilerParams(vmem_limit_bytes=56 * 2**20),
+        name="ffn_backward",
+    )(mine, theirs, vec, ffn_own, ffn_got, cot_own, cot_got, act, slope, gathered, gathered)
+
+
+def first_back_kernel(
+    mine,
+    theirs,
+    vec,
+    grad_own,
+    grad_got,
+    ctx_own,
+    ctx_got,
+    sums,
+    weights,
+    held,
+    grad_resid,
+    grad_context,
+    blocks,
+    grad_low,
+    total,
+    vec_sums,
+):
+    k = pl.program_id(0)
+
+    @pl.when(k == 0)
+    def _():
+        for half, resid in enumerate((mine, theirs)):
+            span = slice(128 * half, 128 * (half + 1))
+            cross = slice(128 * (1 - half), 128 * (2 - half))
+            normed, scaled, inverse = normalize(resid[...], vec[0:1], vec[1:2])
+            grad = grad_own[span] + grad_got[cross]
+            if half == 0:
+                both_sums = jnp.concatenate(
+                    [
+                        jnp.sum(grad * scaled, axis=0, keepdims=True),
+                        jnp.sum(grad, axis=0, keepdims=True),
+                        sums[2:],
+                    ],
+                    axis=0,
+                )
+                for chunk in range(8):
+                    vec_sums[chunk] = both_sums[:, 128 * chunk : 128 * (chunk + 1)]
+            grad = normalize_back(grad, scaled, inverse, vec[0:1])
+            if half == 0:
+                grad_resid[...] = grad
+            grad = grad.astype(bf16)
+            for chunk in range(8):
+                grad_low[chunk, span] = grad[:, 128 * chunk : 128 * (chunk + 1)]
+        total[...] = jnp.zeros_like(total)
+
+    grad = grad_low[k]
+    total[...] += dot_nn(grad[:128], owner_rows(weights[:, 0]))
+    ctx_half = jnp.concatenate([ctx_own[...], ctx_got[...]], axis=0)
+    made = owner_blocks(dot_tn(grad, ctx_half))
+    made = jnp.concatenate([made[:, 0], made[:, 1]], axis=-1)
+    row = jnp.concatenate([vec_sums[k], jnp.zeros((8, D - 128), f32)], axis=1)
+    row = jnp.broadcast_to(row[None], (8, 8, D))
+    made = jnp.concatenate([made, row], axis=1).astype(bf16)
+    blocks[0, :, 0] = made.reshape(4, 2, 16, D)
+
+    @pl.when(k == 7)
+    def _():
+        for group in range(8):
+            grad_context[group] = total[:, 128 * group : 128 * (group + 1)].astype(bf16)
+
+
+def first_backward(mine, theirs, vec, grad_own, grad_got, ctx_own, ctx_got, sums, gathered, blocks):
+    whole = lambda k: (0, 0)
+    return pl.pallas_call(
+        first_back_kernel,
+        grid=(8,),
+        in_specs=[
+            pl.BlockSpec((128, D), whole),
+            pl.BlockSpec((128, D), whole),
+            pl.BlockSpec((4, D), whole),
+            pl.BlockSpec((256, D), whole),
+            pl.BlockSpec((256, D), whole),
+            pl.BlockSpec((128, 512), whole),
+            pl.BlockSpec((128, 512), whole),
+            pl.BlockSpec((8, D), whole),
+            pl.BlockSpec((8, 1, 16, D), lambda k: (0, k, 4, 0)),
+            pl.BlockSpec(memory_space=pl.ANY),
+        ],
+        out_specs=[
+            pl.BlockSpec((128, D), whole),
+            pl.BlockSpec((8, 128, 128), lambda k: (0, 0, 0)),
+            pl.BlockSpec((1, 4, 1, 2, 16, D), lambda k: (k % 4, 0, k // 4, 0, 4, 0)),
+        ],
+        out_shape=[
+            jax.ShapeDtypeStruct((128, D), f32),
+            jax.ShapeDtypeStruct((8, 128, 128), bf16),
+            jax.ShapeDtypeStruct((4, 4, 2, 2, 80, D), bf16),
+        ],
+        scratch_shapes=[
+            pltpu.VMEM((8, 256, 128), bf16),
+            pltpu.VMEM((128, D), f32),
+            pltpu.VMEM((8, 8, 128), f32),
+        ],
+        input_output_aliases={9: 2},
+        compiler_params=pltpu.CompilerParams(vmem_limit_bytes=56 * 2**20),
+        name="first_backward",
+    )(mine, theirs, vec, grad_own, grad_got, ctx_own, ctx_got, sums, gathered, blocks)
+
+
 def swap(value):
     return lax.ppermute(value, "core", [(0, 1), (1, 0)])
 
 
 def exchange(value, axes):
     return lax.all_to_all(value, axes, 0, 0, tiled=True)
+
+
+def shifted(value, axis, size, step):
+    return lax.ppermute(value, axis, [(i, (i + step) % size) for i in range(size)])
+
+
+def ring_gather(value, axis, size):
+    place = lax.axis_index(axis)
+    blocks = jnp.stack([value] + [shifted(value, axis, size, step) for step in range(1, size)])
+    return jnp.take(blocks, (place - jnp.arange(size)) % size, axis=0)
+
+
+def ring_scatter(blocks, axis, size, dtype=f32):
+    place = lax.axis_index(axis)
+    total = lax.dynamic_index_in_dim(blocks, place, 0, keepdims=False).astype(f32)
+    for step in range(1, size):
+        sent = lax.dynamic_index_in_dim(blocks, (place + step) % size, 0, keepdims=False)
+        total = total + shifted(sent, axis, size, step).astype(f32)
+    return total.astype(dtype)
+
+
+def ring_sum(value, axis, size):
+    total = value
+    for step in range(1, size):
+        total = total + shifted(value, axis, size, step)
+    return total
+
+
+def arrange_kernel(core, mine, theirs, heads):
+    for column in range(8):
+        span = slice(192 * column, 192 * (column + 1))
+        own, other = mine[:, span].astype(f32), theirs[:, span].astype(f32)
+        first = core[0] == 0
+        joined = jnp.concatenate(
+            [jnp.where(first, own, other), jnp.where(first, other, own)], axis=1
+        )
+        for place in range(3):
+            chunk = 3 * column + place
+            heads[chunk % 8, chunk // 8] = joined[:, 128 * place : 128 * (place + 1)].astype(bf16)
+
+
+def arrange(core, mine, theirs):
+    return pl.pallas_call(
+        arrange_kernel,
+        in_specs=[
+            pl.BlockSpec(memory_space=pltpu.SMEM),
+            pl.BlockSpec(memory_space=pltpu.VMEM),
+            pl.BlockSpec(memory_space=pltpu.VMEM),
+        ],
+        out_specs=pl.BlockSpec(memory_space=pltpu.VMEM),
+        out_shape=jax.ShapeDtypeStruct((8, 3, 128, 128), bf16),
+        compiler_params=pltpu.CompilerParams(vmem_limit_bytes=32 * 2**20),
+        name="arrange",
+    )(core, mine, theirs)
+
+
+def split_kernel(core, heads, keep, give):
+    for column in range(8):
+        chunks = [3 * column + place for place in range(3)]
+        joined = jnp.concatenate(
+            [heads[chunk % 8, chunk // 8].astype(f32) for chunk in chunks], axis=1
+        )
+        first = core[0] == 0
+        zero, one = joined[:, :192], joined[:, 192:]
+        span = slice(192 * column, 192 * (column + 1))
+        keep[:, span] = jnp.where(first, zero, one).astype(bf16)
+        give[:, span] = jnp.where(first, one, zero).astype(bf16)
+
+
+def split(core, heads):
+    return pl.pallas_call(
+        split_kernel,
+        in_specs=[
+            pl.BlockSpec(memory_space=pltpu.SMEM),
+            pl.BlockSpec(memory_space=pltpu.VMEM),
+        ],
+        out_specs=[pl.BlockSpec(memory_space=pltpu.VMEM)] * 2,
+        out_shape=[jax.ShapeDtypeStruct((128, 1536), bf16)] * 2,
+        compiler_params=pltpu.CompilerParams(vmem_limit_bytes=32 * 2**20),
+        name="split",
+    )(core, heads)
 
 
 def per_device(
@@ -242,6 +612,7 @@
 ):
     core = lax.axis_index("core")
     column = lax.axis_index(COLUMN)
+    group = lax.axis_index(GROUP)
     local = tokens.shape[0]
     pair = 2 * local
     highest = lax.Precision.HIGHEST
@@ -259,122 +630,109 @@
     def both(value):
         return jnp.concatenate([value, swap(value)], axis=0)
 
-    def sum_pair(partial):
-        got = swap(partial)
-        return partial + jnp.concatenate([got[local:], got[:local]], axis=0)
+    tokens_two = both(tokens)
+    cotangent_got = swap(cotangent)
+    project_t = exchange(
+        jnp.broadcast_to(w_project.T[None], (64, 24, D)), COLUMN + GROUP
+    ).reshape(1536, D)
+    table = ring_gather(ring_gather(position_table.T, "yh", 2), "z", 4).reshape(64, 2 * SPAN)
+    table = jnp.concatenate([table, w_key, w_query], axis=1)
+    for axis, size in (("core", 2), ("x", 4), ("yl", 2)):
+        table = ring_gather(table, axis, size)
+    table = table.reshape(D, 2 * SPAN + 256)
+    table_t, position_weights = table[:, : 2 * SPAN], table[:, 2 * SPAN :]
 
     vectors = jnp.stack([first_gain, first_shift, second_gain, second_shift])
-    packet = jnp.concatenate(
-        [
-            w_project.T,
-            position_table.T.reshape(4, D),
-            jnp.pad(vectors, ((0, 0), (0, D - 8))),
-        ],
-        axis=0,
-    )
-    gathered = lax.all_gather(packet, DEVICES, axis=0, tiled=False).reshape(2, 8, 8, 32, D)
-    project_t = gathered[..., :24, :].transpose(2, 0, 1, 3, 4).reshape(3 * D, D)
-    table_t = gathered[..., 24:28, :].transpose(2, 0, 1, 3, 4).reshape(D, 2 * SPAN)
-    vec = gathered[..., 28:, :8].transpose(3, 2, 0, 1, 4).reshape(4, D).astype(f32)
-    gain_one, shift_one, gain_two, shift_two = vec[0], vec[1], vec[2], vec[3]
-
-    position_weights = lax.all_gather(
-        jnp.concatenate([w_key, w_query], axis=1), DP, axis=0, tiled=True
-    )
-
+    vectors = jnp.pad(vectors, ((0, 0), (0, D - 8)))
+    vectors = jnp.concatenate(in_order(vectors, swap(vectors)), axis=0)
     reduce_rows = jnp.moveaxis(w_reduce.T.reshape(8, 8, 2, 256), 2, 0).reshape(2, 8, 2048)
     mine, theirs = in_order(reduce_rows[0], reduce_rows[1])
     reduce_rows = jnp.concatenate(in_order(mine, swap(theirs)), axis=0)
     attend_rows = w_attend.T
     attend_rows = jnp.concatenate(in_order(attend_rows, swap(attend_rows)), axis=0)
     packet = jnp.concatenate(
-        [w_expand.T, reduce_rows[:, :D], reduce_rows[:, D:], attend_rows], axis=0
-    )
-    gathered = lax.all_gather(packet, CHIPS, axis=0, tiled=False).reshape(8, 8, 80, D)
-    expand_t = gathered[..., :32, :].transpose(1, 0, 2, 3).reshape(2048, D)
-    reduce_t = (
-        gathered[..., 32:64, :]
-        .reshape(8, 8, 2, 2, 8, D)
-        .transpose(1, 3, 0, 4, 2, 5)
-        .reshape(D, 2048)
-    )
-    attend_t = (
-        gathered[..., 64:, :].reshape(8, 8, 2, 8, D).transpose(1, 2, 0, 3, 4).reshape(D, D)
-    )
-
-    packed = dot_nt(tokens, project_t).astype(bf16)
-    heads_in = exchange(packed.reshape(local, 3, 8, 128).transpose(2, 1, 0, 3), GROUP)
+        [w_expand.T, reduce_rows[:, :D], reduce_rows[:, D:], attend_rows, vectors], axis=0
+    )
+    gathered = lax.all_gather(packet, CHIPS, axis=0, tiled=False).reshape(8, 8, 88, D)
+    vec = gathered[..., 80:, :8].reshape(8, 8, 2, 4, 8).transpose(3, 1, 2, 0, 4)
+    vec = vec.reshape(4, D).astype(f32)
+    gain_one, shift_one, gain_two, shift_two = vec[0], vec[1], vec[2], vec[3]
+
+    packed = dot_nt(tokens_two, project_t).astype(bf16)
+    core_id = core.reshape(1)
+    heads_in = exchange(arrange(core_id, packed[:local], swap(packed[local:])), GROUP)
     rel = dot_tn(table_t, position_weights).astype(bf16)[column_ids]
     context = exchange(attend(lengths, heads_in, rel), GROUP)
-    context = context.transpose(1, 0, 2).reshape(local, D)
-    halves = in_order(context[:, :512], context[:, 512:])
-    context_half = jnp.concatenate([halves[0], swap(halves[1])], axis=0)
-    tokens_two = both(tokens)
-    cotangent_two = both(cotangent).astype(f32)
-
-    resid1 = both(tokens.astype(f32) + dot_nt(context, attend_t))
-    first_norm, scaled_one, inverse_one = normalize(resid1, gain_one, shift_one)
-    first_two = first_norm.astype(bf16)
-    inner = dot_nt(first_two, expand_t)
-    activ = smooth_gate(inner).astype(bf16)
-    ffn = sum_pair(dot_nt(activ, reduce_t))
-    output, scaled_two, inverse_two = normalize(first_norm + ffn, gain_two, shift_two)
-    grad_resid2 = normalize_back(cotangent_two, scaled_two, inverse_two, gain_two)
-    grad_gain2 = jnp.sum((cotangent_two * scaled_two)[:local], axis=0)
-    grad_shift2 = jnp.sum(cotangent_two[:local], axis=0)
-    grad_ffn = grad_resid2.astype(bf16)
-    grad_reduce_t = dot_tn(grad_ffn, activ).astype(bf16)
-    grad_activ = dot_nn(grad_ffn, reduce_t)
-    gate_value, gate_pull = jax.vjp(smooth_gate, inner)
-    grad_inner = gate_pull(grad_activ)[0].astype(bf16)
-    grad_expand_t = dot_tn(grad_inner, first_two).astype(bf16)
-    grad_first = grad_resid2 + sum_pair(dot_nn(grad_inner, expand_t))
-    grad_resid1 = normalize_back(grad_first, scaled_one, inverse_one, gain_one)
-    grad_gain1 = jnp.sum((grad_first * scaled_one)[:local], axis=0)
-    grad_shift1 = jnp.sum(grad_first[:local], axis=0)
-    grad_attended = grad_resid1.astype(bf16)
-    grad_attend_t = dot_tn(grad_attended, context_half).astype(bf16)
-    grad_context = dot_nn(grad_attended[:local], attend_t).astype(bf16)
-
-    def scatter(blocks):
-        received = exchange(blocks, COLUMN + GROUP)
-        return jnp.sum(received.astype(f32), axis=0)
-
-    grad_ctx = exchange(grad_context.reshape(local, 8, 128).transpose(1, 0, 2), GROUP)
-    expand_sum = scatter(grad_expand_t.reshape(64, 32, D))
-    reduce_blocks = grad_reduce_t.reshape(8, 2, 8, 8, 2048).transpose(0, 2, 1, 3, 4)
-    reduce_sum = scatter(reduce_blocks.reshape(64, 16, 2048))
-    attend_blocks = grad_attend_t.reshape(8, 2, 8, 8, 512).transpose(0, 2, 1, 3, 4)
-    attend_sum = scatter(attend_blocks.reshape(64, 16, 512))
+    flat = context.transpose(1, 0, 2).reshape(local, D)
+    context_own, context_theirs = in_order(flat[:, :512], flat[:, 512:])
+    context_got = swap(context_theirs)
+
+    resid_own = project_back(context, tokens, gathered)
+    resid_got = swap(resid_own)
+    activ, slope, ffn_own = ffn_forward(resid_own, resid_got, vec, gathered)
+    output, blocks, grad_own, sums = ffn_backward(
+        resid_own,
+        resid_got,
+        vec,
+        ffn_own,
+        swap(ffn_own),
+        cotangent,
+        cotangent_got,
+        activ,
+        slope,
+        gathered,
+    )
+    grad_resid1, grad_context, blocks = first_backward(
+        resid_own,
+        resid_got,
+        vec,
+        grad_own,
+        swap(grad_own),
+        context_own,
+        context_got,
+        sums,
+        gathered,
+        blocks,
+    )
+
+    grad_ctx = exchange(grad_context, GROUP)
+    summed = lax.psum_scatter(
+        blocks.reshape(16, 4 * 80, D), ("x", "z"), scatter_dimension=0, tiled=True
+    )
+    summed = ring_scatter(summed.reshape(2, 2 * 80, D), "yl", 2, bf16)
+    summed = ring_scatter(summed.reshape(2, 80, D), "yh", 2)
+    expand_sum = summed[:32]
+    reduce_sum = jnp.concatenate([summed[32:48], summed[48:64]], axis=1)
+    attend_sum = summed[64:72].reshape(8, 2, 512)
+    vector_sum = summed[72:76, :128].reshape(4, 2, 8, 8)
+    vector_sum = lax.dynamic_index_in_dim(vector_sum, group, axis=2, keepdims=False)
 
     grads, rel_grad = attend_back(lengths, heads_in, rel, grad_ctx)
-    grad_packed = exchange(grads, GROUP).transpose(2, 1, 0, 3).reshape(local, 3 * D)
-    tokens_grad = grad_resid1[:local] + dot_nn(grad_packed, project_t)
-    grad_own = lax.dynamic_index_in_dim(
-        both(grad_packed).reshape(pair, 8, 2, 192), core, axis=2, keepdims=False
-    )
-    grad_project_t = dot_tn(grad_own.reshape(pair, 1536), tokens_two).astype(bf16)
-    grad_project = scatter(grad_project_t.reshape(64, 24, D)).T
+    keep, give = split(core_id, exchange(grads, GROUP))
+    grad_packed = jnp.concatenate([keep, swap(give)], axis=0)
+    grad_project_t = dot_tn(grad_packed, tokens_two).astype(bf16)
+    grad_project = exchange(grad_project_t.reshape(64, 24, D), COLUMN + GROUP)
+    grad_project = jnp.sum(grad_project.astype(f32), axis=0).T
+    tokens_part = dot_nn(grad_packed, project_t)
+    tokens_grad = grad_resid1 + (tokens_part[:local] + swap(tokens_part[local:]))
 
     grad_expand = expand_sum.T
     mine, theirs = in_order(reduce_sum[:8], reduce_sum[8:])
     parts = in_order(mine, swap(theirs))
     grad_reduce = jnp.stack([part.reshape(8, 8, 256) for part in parts], axis=2)
     grad_reduce = grad_reduce.reshape(8, FF).T
-    mine, theirs = in_order(attend_sum[:8], attend_sum[8:])
+    mine, theirs = in_order(attend_sum[:, 0], attend_sum[:, 1])
     grad_attend = jnp.concatenate(in_order(mine, swap(theirs)), axis=1).T
 
-    vectors = jnp.stack([grad_gain1, grad_shift1, grad_gain2, grad_shift2])
-    vectors = vectors.reshape(4, 128, 8).transpose(1, 0, 2).reshape(128, 1, 32)
-    vectors = jnp.sum(exchange(vectors, EVERY), axis=0).reshape(4, 8)
+    mine, theirs = in_order(vector_sum[:, 0], vector_sum[:, 1])
+    vectors = mine + swap(theirs)
 
     upper = rel_grad.astype(bf16)
     lower = (rel_grad - upper.astype(f32)).astype(bf16)
     rel_grad = dot_nn(fold, upper) + dot_nn(fold, lower)
     rel_grad = rel_grad + swap(rel_grad)
-    rel_grad = by_core(rel_grad[:, :128], rel_grad[:, 128:]).astype(bf16)
-    rel_grad = exchange(jnp.broadcast_to(rel_grad[None], (8, 2 * SPAN, 128)), COLUMN)
-    rel_grad = jnp.sum(rel_grad.astype(f32), axis=0)
+    rel_grad = by_core(rel_grad[:, :128], rel_grad[:, 128:])
+    rel_grad = ring_sum(ring_sum(rel_grad, "x", 4), "yl", 2)
     rel_key_grad, rel_query_grad = in_order(rel_grad, swap(rel_grad))
     own = 64 * (2 * column + core)
     table_own = lax.dynamic_slice_in_dim(table_t, own, 64, axis=0).astype(f32)
@@ -387,10 +745,11 @@
         (((1,), (1,)), ((), ())),
         precision=highest,
     )
-    grad_table = jnp.sum(exchange(table_part.reshape(8, 8, 2 * SPAN), GROUP), axis=0).T
+    table_part = ring_scatter(table_part.reshape(4, 2, 8, 2 * SPAN), "z", 4)
+    grad_table = ring_scatter(table_part, "yh", 2).T
 
     return (
-        output[:local].astype(bf16),
+        output,
         tokens_grad.astype(bf16),
         grad_project,
         grad_attend,

time: 554 us -> 410 us (0.74)
  the two profiles are of different devices: /device:TPU:0 before, /device:TPU:23 now
where the time goes in v3:
time: 410 us; the launch traced here: 403 us
  waiting for transfers between devices  139 us (34%)
  Pallas kernels  85.7 us (21%)
  starting transfers between devices  78.1 us (19%)
  local copies, waits for them, and re-layouts  30 us (7%)
  blocking collectives  20.7 us (5%)
  other arithmetic  19.1 us (5%)
  between operations  15.2 us (4%)
  matrix products  14.6 us (4%)
    ppermute x19, waiting for transfers between devices, shifted(): lax.ppermute(value, axis, [(i, (i + step) % size) for i in range(size)])  115 us
    all_to_all x4, starting transfers between devices, exchange(): return lax.all_to_all(value, axes, 0, 0, tiled=True)  30.7 us
    pallas_call x1, Pallas kernels, attend_back(): pl.pallas_call(attend_back_kernel, grid=(2,), in_specs=[pl.BlockSpec(memo...  28 us
    ppermute x19, starting transfers between devices, shifted(): lax.ppermute(value, axis, [(i, (i + step) % size) for i in range(size)])  26.8 us
    all_to_all x2, blocking collectives, exchange(): return lax.all_to_all(value, axes, 0, 0, tiled=True)  20.7 us
    ppermute x17, starting transfers between devices, swap(): return lax.ppermute(value, 'core', [(0, 1), (1, 0)])  20.5 us
    pallas_call x1, Pallas kernels, ffn_backward(): pl.pallas_call(ffn_back_kernel, grid=(2, 8), in_specs=[pl.BlockSpec((128,...  19.7 us
    all_to_all x4, waiting for transfers between devices, exchange(): return lax.all_to_all(value, axes, 0, 0, tiled=True)  15.8 us
  transfers between devices with their start and end apart: 42, of which 23 were waited for; matrix products, arithmetic and copies ran while one was open for 12% of the time, Pallas kernels for 10%

profile of v3, /device:TPU:23, one launch (start us, length us, event | category | flops | bytes accessed | tf_op | source)
XLA Modules:
  0.0 402.5 jit_solution(8736673846254640291)
XLA Ops:
  12.0 4.5 %concatenate.27 = bf16[88,1024]{1,0:T(8,128)(2,1)} concatenate(bf16[32,1024]{1,0:T(8,128)(2,1)} %bitcast.176, bf16[16,1024]{1,0:T(8,128)(2,1)S(1)} %get-tuple-element.57, bf16[16,1024]{1,0:T(8,128)(2,1)S(1)} %get-tuple-element.56, bf16[8,1024]{1,0:T(8,128)(2,1)S(1)} %get-tuple-element.65, bf16[8,1024]{1,0:T(8,128)(2,1)S(1)} %get-tuple-element.64, ...), dimensions={0} | concatenate | bytes 360448 | tf_op jit(solution)/shard_map/concatenate | solution.py:653
  17.0 2.8 broadcast_in_dim.79
  19.8 11.0 %all-to-all-start = ((bf16[64,24,1024]{2,1,0:T(8,128)(2,1)}), bf16[64,24,1024]{2,1,0:T(8,128)(2,1)}, u32[]{:S(2)}, u32[]{:S(2)}) async-start(bf16[64,24,1024]{2,1,0:T(8,128)(2,1)} %broadcast_in_dim.79), calls=%async_computation | async-start | bytes 6291456 | tf_op jit(solution)/shard_map/all_to_all | solution.py:513
  31.6 35.1 %collective-permute-done.2 = bf16[8,512]{1,0:T(8,128)(2,1)S(1)} collective-permute-done((bf16[8,512]{1,0:T(8,128)(2,1)S(1)}, bf16[8,512]{1,0:T(8,128)(2,1)S(1)}, u32[]{:S(2)}, u32[]{:S(2)}) %collective-permute-start.2) | collective-permute-done | bytes 8224 | tf_op jit(solution)/shard_map/ppermute | solution.py:517
  67.4 3.0 collective-permute-start.5
  71.8 2.6 collective-permute-done.4
  76.3 2.2 collective-permute-start.6
  80.1 2.1 collective-permute-start.8
  82.9 8.7 %collective-permute-done.9 = bf16[2,64,768]{2,1,0:T(8,128)(2,1)S(1)} collective-permute-done((bf16[2,64,768]{2,1,0:T(8,128)(2,1)S(1)}, bf16[2,64,768]{2,1,0:T(8,128)(2,1)S(1)}, u32[]{:S(2)}, u32[]{:S(2)}) %collective-permute-start.9) | collective-permute-done | bytes 196640 | tf_op jit(solution)/shard_map/ppermute | solution.py:517
  91.7 4.5 %collective-permute-done.8 = bf16[2,64,768]{2,1,0:T(8,128)(2,1)S(1)} collective-permute-done((bf16[2,64,768]{2,1,0:T(8,128)(2,1)S(1)}, bf16[2,64,768]{2,1,0:T(8,128)(2,1)S(1)}, u32[]{:S(2)}, u32[]{:S(2)}) %collective-permute-start.8) | collective-permute-done | bytes 196640 | tf_op jit(solution)/shard_map/ppermute | solution.py:517
  99.0 1.9 collective-permute-start.10
  100.9 2.9 convolution_convert_fusion.1
  108.3 5.2 %all-to-all-start.1 = ((bf16[8,3,128,128]{3,2,1,0:T(8,128)(2,1)}), bf16[8,3,128,128]{3,2,1,0:T(8,128)(2,1)S(1)}, u32[]{:S(2)}, u32[]{:S(2)}) async-start(bf16[8,3,128,128]{3,2,1,0:T(8,128)(2,1)} %arrange.1), calls=%async_computation.1 | async-start | bytes 1572864 | tf_op jit(solution)/shard_map/all_to_all | solution.py:513
  113.7 14.2 %collective-permute-done.10 = bf16[4,2,64,768]{3,2,1,0:T(8,128)(2,1)} collective-permute-done((bf16[4,2,64,768]{3,2,1,0:T(8,128)(2,1)}, bf16[4,2,64,768]{3,2,1,0:T(8,128)(2,1)}, u32[]{:S(2)}, u32[]{:S(2)}) %collective-permute-start.10) | collective-permute-done | bytes 786464 | tf_op jit(solution)/shard_map/ppermute | solution.py:517
  129.2 1.8 gather_fusion.4
  131.0 1.6 bitcast_select_fusion
  134.4 3.9 gather_fusion.5
  138.3 8.0 %all-to-all-done.1.heads_in = bf16[8,3,128,128]{3,2,1,0:T(8,128)(2,1)S(1)} async-done(((bf16[8,3,128,128]{3,2,1,0:T(8,128)(2,1)}), bf16[8,3,128,128]{3,2,1,0:T(8,128)(2,1)S(1)}, u32[]{:S(2)}, u32[]{:S(2)}) %all-to-all-start.1) | async-done | bytes 786464 | tf_op jit(solution)/shard_map/all_to_all | solution.py:513
  146.4 8.9 %attend.1 = bf16[8,128,128]{2,1,0:T(8,128)(2,1)S(1)} custom-call(s32[2]{0:T(128)S(1)} %copy-done.7, bf16[8,3,128,128]{3,2,1,0:T(8,128)(2,1)S(1)} %all-to-all-done.1.heads_in, bf16[1024,256]{1,0:T(8,128)(2,1)S(1)} %gather_fusion.5), custom_call_target="tpu_custom_call" | custom-call | tf_op jit(solution)/shard_map/attend/pallas_call | solution.py:171
  155.2 9.7 %all_to_all.30.context = bf16[8,128,128]{2,1,0:T(8,128)(2,1)S(1)} all-to-all(bf16[8,128,128]{2,1,0:T(8,128)(2,1)S(1)} %attend.1), channel_id=1, replica_groups=mesh['yl'=2,'x'=4,'core'=2,'z'=4,'yh'=2] {'z','yh'}, dimensions={0} | all-to-all | bytes 524288 | tf_op jit(solution)/shard_map/all_to_all | solution.py:513
  164.9 5.2 %project_back.1.mine = f32[128,1024]{1,0:T(8,128)S(1)} custom-call(bf16[8,128,128]{2,1,0:T(8,128)(2,1)S(1)} %all_to_all.30.context, bf16[128,1024]{1,0:T(8,128)(2,1)S(1)} %copy-done.5, bf16[8,8,88,1024]{3,2,1,0:T(8,128)(2,1)} %bitcast.148), custom_call_target="tpu_custom_call" | custom-call | tf_op jit(solution)/shard_map/project_back/pallas_call | solution.py:231
  170.2 5.6 %collective-permute-start.14 = (f32[128,1024]{1,0:T(8,128)S(1)}, f32[128,1024]{1,0:T(8,128)S(1)}, u32[]{:S(2)}, u32[]{:S(2)}) collective-permute-start(f32[128,1024]{1,0:T(8,128)S(1)} %project_back.1.mine), channel_id=1, source_target_pairs={{0,8},{8,0},{1,9},{9,1},{2,10},{10,2},{3,11},{11,3},{4,12},{12,4},... | collective-permute-start | bytes 1572872 | tf_op jit(solution)/shard_map/ppermute | solution.py:509
  177.3 13.3 %ffn_forward.1 = (bf16[8,256,256]{2,1,0:T(8,128)(2,1)S(1)}, f32[8,256,256]{2,1,0:T(8,128)S(1)}, f32[256,1024]{1,0:T(8,128)S(1)}) custom-call(f32[128,1024]{1,0:T(8,128)S(1)} %project_back.1.mine, f32[128,1024]{1,0:T(8,128)S(1)} %collective-permute-done.14.theirs, f32[4,1024]{1,0:T(4,128)S(1)} %reshape.403.vec, bf16[8,8,88,1024]{3,2,1,0:T(8,128)(2,1)} %bitcast.150, ...), custom_call_target="tpu_custom_call" | custom-call | tf_op jit(solution)/shard_map/ffn_forward/pallas_call | solution.py:275
  193.5 2.5 collective-permute-done.16.cot_got
  197.1 19.7 %ffn_backward.1 = (bf16[128,1024]{1,0:T(8,128)(2,1)}, bf16[4,4,2,2,80,1024]{5,4,3,2,1,0:T(8,128)(2,1)}, f32[256,1024]{1,0:T(8,128)}, f32[8,1024]{1,0:T(8,128)}) custom-call(f32[128,1024]{1,0:T(8,128)} %copy-done, f32[128,1024]{1,0:T(8,128)} %copy-done.1, f32[4,1024]{1,0:T(4,128)} %copy-done.6, f32[256,1024]{1,0:T(8,128)} %copy-done.4, ...), custom_call_target="tpu_custom_call" | custom-call | tf_op jit(solution)/shard_map/ffn_backward/pallas_call | solution.py:368
  218.1 1.6 collective-permute-done.18.ctx_got
  220.8 8.6 %first_backward.1 = (f32[128,1024]{1,0:T(8,128)}, bf16[8,128,128]{2,1,0:T(8,128)(2,1)}, bf16[4,4,2,2,80,1024]{5,4,3,2,1,0:T(8,128)(2,1)}) custom-call(f32[128,1024]{1,0:T(8,128)} %copy-done, f32[128,1024]{1,0:T(8,128)} %copy-done.1, f32[4,1024]{1,0:T(4,128)} %copy-done.6, f32[256,1024]{1,0:T(8,128)} %get-tuple-element.31.grad_own, ...), custom_call_target="tpu_custom_call", output_to_operand_aliasing={{2}: (9, {})} | custom-call | tf_op jit(solution)/shard_map/first_backward/pallas_call | solution.py:472
  230.4 10.9 %all_to_all.31.grad_context = bf16[8,128,128]{2,1,0:T(8,128)(2,1)S(1)} all-to-all(bf16[8,128,128]{2,1,0:T(8,128)(2,1)S(1)} %copy-done.19), channel_id=1, replica_groups=mesh['yl'=2,'x'=4,'core'=2,'z'=4,'yh'=2] {'z','yh'}, dimensions={0} | all-to-all | bytes 524288 | tf_op jit(solution)/shard_map/all_to_all | solution.py:513
  241.3 28.0 %attend_back.1 = (bf16[8,3,128,128]{3,2,1,0:T(8,128)(2,1)}, f32[1024,256]{1,0:T(8,128)S(1)}) custom-call(s32[2]{0:T(128)S(1)} %copy-done.7, bf16[8,3,128,128]{3,2,1,0:T(8,128)(2,1)S(1)} %all-to-all-done.1.heads_in, bf16[1024,256]{1,0:T(8,128)(2,1)S(1)} %gather_fusion.5, bf16[8,128,128]{2,1,0:T(8,128)(2,1)S(1)} %all_to_all.31.grad_context), custom_call_target="tpu_custom_call" | custom-call | tf_op jit(solution)/shard_map/attend_back/pallas_call | solution.py:188
  269.3 5.6 %all-to-all-start.4 = ((bf16[8,3,128,128]{3,2,1,0:T(8,128)(2,1)}), bf16[8,3,128,128]{3,2,1,0:T(8,128)(2,1)S(1)}, u32[]{:S(2)}, u32[]{:S(2)}) async-start(bf16[8,3,128,128]{3,2,1,0:T(8,128)(2,1)} %get-tuple-element.36), calls=%async_computation.4 | async-start | bytes 1572864 | tf_op jit(solution)/shard_map/all_to_all | solution.py:513
  275.0 1.8 fusion.9
  276.7 1.8 fusion
  278.5 2.0 collective-permute-start.26
  280.6 1.5 collective-permute-done.26
  282.2 7.8 %all-to-all-done.4.heads = bf16[8,3,128,128]{3,2,1,0:T(8,128)(2,1)S(1)} async-done(((bf16[8,3,128,128]{3,2,1,0:T(8,128)(2,1)}), bf16[8,3,128,128]{3,2,1,0:T(8,128)(2,1)S(1)}, u32[]{:S(2)}, u32[]{:S(2)}) %all-to-all-start.4) | async-done | bytes 786464 | tf_op jit(solution)/shard_map/all_to_all | solution.py:513
  290.8 2.9 collective-permute-start.19
  294.4 6.0 %collective-permute-start.28 = (f32[512,128]{0,1:T(8,128)}, f32[512,128]{0,1:T(8,128)}, u32[]{:S(2)}, u32[]{:S(2)}) collective-permute-start(f32[512,128]{0,1:T(8,128)} %slice_select_fusion), channel_id=1, source_target_pairs={{0,32},{16,48},{32,0},{48,16},{1,33},{17,49},{33,1},{49,17},{2,34}... | collective-permute-start | bytes 786440 | tf_op jit(solution)/shard_map/ppermute | solution.py:517
  300.6 2.6 convolution_convert_fusion
  303.2 8.8 %all-to-all-start.5 = ((bf16[64,24,1024]{2,1,0:T(8,128)(2,1)}), bf16[64,24,1024]{2,1,0:T(8,128)(2,1)S(1)}, u32[]{:S(2)}, u32[]{:S(2)}) async-start(bf16[64,24,1024]{2,1,0:T(8,128)(2,1)} %bitcast.40), calls=%async_computation.5 | async-start | bytes 6291456 | tf_op jit(solution)/shard_map/all_to_all | solution.py:513
  315.9 1.5 slice.136
  317.4 35.2 %collective-permute-done.30 = f32[512,128]{0,1:T(8,128)} collective-permute-done((f32[512,128]{0,1:T(8,128)S(1)}, f32[512,128]{0,1:T(8,128)}, u32[]{:S(2)}, u32[]{:S(2)}) %collective-permute-start.30) | collective-permute-done | bytes 262176 | tf_op jit(solution)/shard_map/ppermute | solution.py:517
  354.7 2.9 fusion.52
  359.1 1.7 collective-permute-start.34
  366.5 3.7 collective-permute-start.35
  371.9 2.2 fusion.3
  374.1 4.3 %collective-permute-done.21 = bf16[160,1024]{1,0:T(8,128)(2,1)S(1)} collective-permute-done((bf16[160,1024]{1,0:T(8,128)(2,1)S(1)}, bf16[160,1024]{1,0:T(8,128)(2,1)S(1)}, u32[]{:S(2)}, u32[]{:S(2)}) %collective-permute-start.21) | collective-permute-done | bytes 327712 | tf_op jit(solution)/shard_map/ppermute | solution.py:517
  381.7 4.5 %collective-permute-done.22 = bf16[80,1024]{1,0:T(8,128)(2,1)} collective-permute-done((bf16[80,1024]{1,0:T(8,128)(2,1)}, bf16[80,1024]{1,0:T(8,128)(2,1)}, u32[]{:S(2)}, u32[]{:S(2)}) %collective-permute-start.22) | collective-permute-done | bytes 163872 | tf_op jit(solution)/shard_map/ppermute | solution.py:517
  387.8 4.2 %collective-permute-start.23 = (f32[8,512]{1,0:T(8,128)S(1)}, f32[8,512]{1,0:T(8,128)S(1)}, u32[]{:S(2)}, u32[]{:S(2)}) collective-permute-start(f32[8,512]{1,0:T(8,128)S(1)} %select_bitcast_fusion), channel_id=1, source_target_pairs={{0,8},{8,0},{1,9},{9,1},{2,10},{10,2},{3,11},{11,3},{4,12},{12,4},... | collective-permute-start | bytes 49160 | tf_op jit(solution)/shard_map/ppermute | solution.py:509
  (200 shorter events, 55.9 us)
Async XLA Ops:
  7.2 157.8 %all-gather.3.cloned.1.call-start = ((), (), s32[]{:S(2)}) async-start(), calls=%async_computation.7 | async-start | bytes 11714560 | tf_op jit(solution)/shard_map/all_gather | solution.py:656
  7.9 2.2 collective-permute-start.13
  9.6 2.4 collective-permute-start.11
  9.7 1.5 collective-permute-start.12
  16.5 66.4 %collective-permute-start = (bf16[128,1024]{1,0:T(8,128)(2,1)}, bf16[128,1024]{1,0:T(8,128)(2,1)S(1)}, u32[]{:S(2)}, u32[]{:S(2)}) collective-permute-start(bf16[128,1024]{1,0:T(8,128)(2,1)} %tokens.1), channel_id=1, source_target_pairs={{0,8},{8,0},{1,9},{9,1},{2,10},{10,2},{3,11},{11,3},{4,12},{12,4},... | collective-permute-start | bytes 786440 | tf_op jit(solution)/shard_map/ppermute | solution.py:509
  19.8 56.4 %copy-start.22 = (bf16[64,128]{1,0:T(8,128)(2,1)S(1)}, bf16[64,128]{1,0:T(8,128)(2,1)}, u32[]{:S(2)}) copy-start(bf16[64,128]{1,0:T(8,128)(2,1)} %param.26) | copy-start | bytes 49156
  19.8 56.4 %copy-start.23 = (bf16[64,128]{1,0:T(8,128)(2,1)S(1)}, bf16[64,128]{1,0:T(8,128)(2,1)}, u32[]{:S(2)}) copy-start(bf16[64,128]{1,0:T(8,128)(2,1)} %param.27) | copy-start | bytes 49156
  19.8 81.1 %all-to-all-start = ((bf16[64,24,1024]{2,1,0:T(8,128)(2,1)}), bf16[64,24,1024]{2,1,0:T(8,128)(2,1)}, u32[]{:S(2)}, u32[]{:S(2)}) async-start(bf16[64,24,1024]{2,1,0:T(8,128)(2,1)} %broadcast_in_dim.79), calls=%async_computation | async-start | bytes 6291456 | tf_op jit(solution)/shard_map/all_to_all | solution.py:513
  30.9 35.9 %collective-permute-start.2 = (bf16[8,512]{1,0:T(8,128)(2,1)S(1)}, bf16[8,512]{1,0:T(8,128)(2,1)S(1)}, u32[]{:S(2)}, u32[]{:S(2)}) collective-permute-start(bf16[8,512]{1,0:T(8,128)(2,1)S(1)} %bitcast.185), channel_id=1, source_target_pairs={{0,1},{1,0},{2,3},{3,2},{4,5},{5,4},{6,7},{7,6},{8,9},{9,8},{10,11... | collective-permute-start | bytes 24584 | tf_op jit(solution)/shard_map/ppermute | solution.py:517
  67.4 4.5 %collective-permute-start.5 = (bf16[2,8,512]{2,1,0:T(8,128)(2,1)S(1)}, bf16[2,8,512]{2,1,0:T(8,128)(2,1)S(1)}, u32[]{:S(2)}, u32[]{:S(2)}) collective-permute-start(bf16[2,8,512]{2,1,0:T(8,128)(2,1)S(1)} %broadcast_select_fusion.14), channel_id=1, source_target_pairs={{0,6},{2,0},{4,2},{6,4},{1,7},{3,1},{5,3},{7,5},{8,14},{10,8},{12,... | collective-permute-start | bytes 49160 | tf_op jit(solution)/shard_map/ppermute | solution.py:517
  70.3 4.1 %collective-permute-start.4 = (bf16[2,8,512]{2,1,0:T(8,128)(2,1)S(1)}, bf16[2,8,512]{2,1,0:T(8,128)(2,1)S(1)}, u32[]{:S(2)}, u32[]{:S(2)}) collective-permute-start(bf16[2,8,512]{2,1,0:T(8,128)(2,1)S(1)} %broadcast_select_fusion.14), channel_id=1, source_target_pairs={{0,4},{2,6},{4,0},{6,2},{1,5},{3,7},{5,1},{7,3},{8,12},{10,14},{12... | collective-permute-start | bytes 49160 | tf_op jit(solution)/shard_map/ppermute | solution.py:517
  71.8 3.8 collective-permute-start.3
  76.3 3.1 collective-permute-start.6
  80.1 11.6 %collective-permute-start.9 = (bf16[2,64,768]{2,1,0:T(8,128)(2,1)S(1)}, bf16[2,64,768]{2,1,0:T(8,128)(2,1)S(1)}, u32[]{:S(2)}, u32[]{:S(2)}) collective-permute-start(bf16[2,64,768]{2,1,0:T(8,128)(2,1)S(1)} %broadcast_select_fusion.1), channel_id=1, source_target_pairs={{0,48},{16,0},{32,16},{48,32},{1,49},{17,1},{33,17},{49,33},{2,50}... | collective-permute-start | bytes 589832 | tf_op jit(solution)/shard_map/ppermute | solution.py:517
  80.1 16.0 %collective-permute-start.8 = (bf16[2,64,768]{2,1,0:T(8,128)(2,1)S(1)}, bf16[2,64,768]{2,1,0:T(8,128)(2,1)S(1)}, u32[]{:S(2)}, u32[]{:S(2)}) collective-permute-start(bf16[2,64,768]{2,1,0:T(8,128)(2,1)S(1)} %broadcast_select_fusion.1), channel_id=1, source_target_pairs={{0,32},{16,48},{32,0},{48,16},{1,33},{17,49},{33,1},{49,17},{2,34}... | collective-permute-start | bytes 589832 | tf_op jit(solution)/shard_map/ppermute | solution.py:517
  82.2 15.0 %collective-permute-start.7 = (bf16[2,64,768]{2,1,0:T(8,128)(2,1)S(1)}, bf16[2,64,768]{2,1,0:T(8,128)(2,1)S(1)}, u32[]{:S(2)}, u32[]{:S(2)}) collective-permute-start(bf16[2,64,768]{2,1,0:T(8,128)(2,1)S(1)} %broadcast_select_fusion.1), channel_id=1, source_target_pairs={{0,16},{16,32},{32,48},{48,0},{1,17},{17,33},{33,49},{49,1},{2,18}... | collective-permute-start | bytes 589832 | tf_op jit(solution)/shard_map/ppermute | solution.py:517
  82.9 20.9 %copy-start.12 = (bf16[256,1024]{1,0:T(8,128)(2,1)}, bf16[256,1024]{1,0:T(8,128)(2,1)S(1)}, u32[]{:S(2)}) copy-start(bf16[256,1024]{1,0:T(8,128)(2,1)S(1)} %constant_dynamic-update-slice_fusion) | copy-start | bytes 1572868
  99.0 28.9 %collective-permute-start.10 = (bf16[4,2,64,768]{3,2,1,0:T(8,128)(2,1)}, bf16[4,2,64,768]{3,2,1,0:T(8,128)(2,1)}, u32[]{:S(2)}, u32[]{:S(2)}) collective-permute-start(bf16[4,2,64,768]{3,2,1,0:T(8,128)(2,1)} %broadcast_select_fusion), channel_id=1, source_target_pairs={{0,64},{64,0},{1,65},{65,1},{2,66},{66,2},{3,67},{67,3},{4,68},{68... | collective-permute-start | bytes 2359304 | tf_op jit(solution)/shard_map/ppermute | solution.py:517
  104.7 2.5 collective-permute-start.1
  108.3 38.0 %all-to-all-start.1 = ((bf16[8,3,128,128]{3,2,1,0:T(8,128)(2,1)}), bf16[8,3,128,128]{3,2,1,0:T(8,128)(2,1)S(1)}, u32[]{:S(2)}, u32[]{:S(2)}) async-start(bf16[8,3,128,128]{3,2,1,0:T(8,128)(2,1)} %arrange.1), calls=%async_computation.1 | async-start | bytes 1572864 | tf_op jit(solution)/shard_map/all_to_all | solution.py:513
  113.5 256.7 %reduce-scatter.4.cloned.1.call-start = ((), (), s32[]{:S(2)}) async-start(), calls=%async_computation.8 | async-start | bytes 11141120
  170.2 7.2 %collective-permute-start.14 = (f32[128,1024]{1,0:T(8,128)S(1)}, f32[128,1024]{1,0:T(8,128)S(1)}, u32[]{:S(2)}, u32[]{:S(2)}) collective-permute-start(f32[128,1024]{1,0:T(8,128)S(1)} %project_back.1.mine), channel_id=1, source_target_pairs={{0,8},{8,0},{1,9},{9,1},{2,10},{10,2},{3,11},{11,3},{4,12},{12,4},... | collective-permute-start | bytes 1572872 | tf_op jit(solution)/shard_map/ppermute | solution.py:509
  193.0 3.0 collective-permute-start.15
  193.4 2.7 collective-permute-start.16
  216.8 3.0 collective-permute-start.17
  218.0 1.8 collective-permute-start.18
  269.3 20.6 %all-to-all-start.4 = ((bf16[8,3,128,128]{3,2,1,0:T(8,128)(2,1)}), bf16[8,3,128,128]{3,2,1,0:T(8,128)(2,1)S(1)}, u32[]{:S(2)}, u32[]{:S(2)}) async-start(bf16[8,3,128,128]{3,2,1,0:T(8,128)(2,1)} %get-tuple-element.36), calls=%async_computation.4 | async-start | bytes 1572864 | tf_op jit(solution)/shard_map/all_to_all | solution.py:513
  278.5 22.0 %copy-start.13 = (bf16[256,1024]{1,0:T(8,128)(2,1)S(1)}, bf16[256,1024]{1,0:T(8,128)(2,1)}, u32[]{:S(2)}) copy-start(bf16[256,1024]{1,0:T(8,128)(2,1)} %copy-done.12) | copy-start | bytes 1572868
  278.5 3.6 collective-permute-start.26
  282.2 21.0 %copy-start.9 = (f32[512,256]{0,1:T(8,128)}, f32[512,256]{0,1:T(8,128)S(1)}, u32[]{:S(2)}) copy-start(f32[512,256]{0,1:T(8,128)S(1)} %add.334) | copy-start | bytes 1572868
  290.8 9.7 %collective-permute-start.19 = (bf16[128,1536]{1,0:T(8,128)(2,1)S(1)}, bf16[128,1536]{1,0:T(8,128)(2,1)S(1)}, u32[]{:S(2)}, u32[]{:S(2)}) collective-permute-start(bf16[128,1536]{1,0:T(8,128)(2,1)S(1)} %get-tuple-element.38), channel_id=1, source_target_pairs={{0,8},{8,0},{1,9},{9,1},{2,10},{10,2},{3,11},{11,3},{4,12},{12,4},... | collective-permute-start | bytes 1179656 | tf_op jit(solution)/shard_map/ppermute | solution.py:509
  294.4 17.6 %collective-permute-start.29 = (f32[512,128]{0,1:T(8,128)}, f32[512,128]{0,1:T(8,128)S(1)}, u32[]{:S(2)}, u32[]{:S(2)}) collective-permute-start(f32[512,128]{0,1:T(8,128)} %slice_select_fusion), channel_id=1, source_target_pairs={{0,48},{16,0},{32,16},{48,32},{1,49},{17,1},{33,17},{49,33},{2,50}... | collective-permute-start | bytes 786440 | tf_op jit(solution)/shard_map/ppermute | solution.py:517
  294.4 18.8 %collective-permute-start.28 = (f32[512,128]{0,1:T(8,128)}, f32[512,128]{0,1:T(8,128)}, u32[]{:S(2)}, u32[]{:S(2)}) collective-permute-start(f32[512,128]{0,1:T(8,128)} %slice_select_fusion), channel_id=1, source_target_pairs={{0,32},{16,48},{32,0},{48,16},{1,33},{17,49},{33,1},{49,17},{2,34}... | collective-permute-start | bytes 786440 | tf_op jit(solution)/shard_map/ppermute | solution.py:517
  300.5 12.8 %collective-permute-start.27 = (f32[512,128]{0,1:T(8,128)}, f32[512,128]{0,1:T(8,128)}, u32[]{:S(2)}, u32[]{:S(2)}) collective-permute-start(f32[512,128]{0,1:T(8,128)} %slice_select_fusion), channel_id=1, source_target_pairs={{0,16},{16,32},{32,48},{48,0},{1,17},{17,33},{33,49},{49,1},{2,18}... | collective-permute-start | bytes 786440 | tf_op jit(solution)/shard_map/ppermute | solution.py:517
  303.2 77.3 %all-to-all-start.5 = ((bf16[64,24,1024]{2,1,0:T(8,128)(2,1)}), bf16[64,24,1024]{2,1,0:T(8,128)(2,1)S(1)}, u32[]{:S(2)}, u32[]{:S(2)}) async-start(bf16[64,24,1024]{2,1,0:T(8,128)(2,1)} %bitcast.40), calls=%async_computation.5 | async-start | bytes 6291456 | tf_op jit(solution)/shard_map/all_to_all | solution.py:513
  314.6 38.0 %collective-permute-start.30 = (f32[512,128]{0,1:T(8,128)S(1)}, f32[512,128]{0,1:T(8,128)}, u32[]{:S(2)}, u32[]{:S(2)}) collective-permute-start(f32[512,128]{0,1:T(8,128)S(1)} %add_add_fusion), channel_id=1, source_target_pairs={{0,64},{64,0},{1,65},{65,1},{2,66},{66,2},{3,67},{67,3},{4,68},{68... | collective-permute-start | bytes 786440 | tf_op jit(solution)/shard_map/ppermute | solution.py:517
  315.9 38.8 %copy-start.11 = (bf16[256,1536]{1,0:T(8,128)(2,1)S(1)}, bf16[256,1536]{1,0:T(8,128)(2,1)}, u32[]{:S(2)}) copy-start(bf16[256,1536]{1,0:T(8,128)(2,1)} %copy-done.10) | copy-start | bytes 2359300
  353.6 5.0 %collective-permute-start.31 = (f32[512,128]{0,1:T(8,128)S(1)}, f32[512,128]{0,1:T(8,128)S(1)}, u32[]{:S(2)}, u32[]{:S(2)}) collective-permute-start(f32[512,128]{0,1:T(8,128)S(1)} %add.338), channel_id=1, source_target_pairs={{0,8},{8,0},{1,9},{9,1},{2,10},{10,2},{3,11},{11,3},{4,12},{12,4},... | collective-permute-start | bytes 786440 | tf_op jit(solution)/shard_map/ppermute | solution.py:509
  358.5 13.4 %collective-permute-start.20 = (f32[128,1024]{1,0:T(8,128)}, f32[128,1024]{1,0:T(8,128)}, u32[]{:S(2)}, u32[]{:S(2)}) collective-permute-start(f32[128,1024]{1,0:T(8,128)} %slice.146), channel_id=1, source_target_pairs={{0,8},{8,0},{1,9},{9,1},{2,10},{10,2},{3,11},{11,3},{4,12},{12,4},... | collective-permute-start | bytes 1572872 | tf_op jit(solution)/shard_map/ppermute | solution.py:509
  359.1 5.6 %collective-permute-start.34 = (f32[2,8,512]{2,1,0:T(8,128)S(1)}, f32[2,8,512]{2,1,0:T(8,128)S(1)}, u32[]{:S(2)}, u32[]{:S(2)}) collective-permute-start(f32[2,8,512]{2,1,0:T(8,128)S(1)} %get-tuple-element.52), channel_id=1, source_target_pairs={{0,6},{2,0},{4,2},{6,4},{1,7},{3,1},{5,3},{7,5},{8,14},{10,8},{12,... | collective-permute-start | bytes 98312 | tf_op jit(solution)/shard_map/ppermute | solution.py:517
  360.7 4.3 %collective-permute-start.33 = (f32[2,8,512]{2,1,0:T(8,128)S(1)}, f32[2,8,512]{2,1,0:T(8,128)S(1)}, u32[]{:S(2)}, u32[]{:S(2)}) collective-permute-start(f32[2,8,512]{2,1,0:T(8,128)S(1)} %get-tuple-element.53), channel_id=1, source_target_pairs={{0,4},{2,6},{4,0},{6,2},{1,5},{3,7},{5,1},{7,3},{8,12},{10,14},{12... | collective-permute-start | bytes 98312 | tf_op jit(solution)/shard_map/ppermute | solution.py:517
  362.1 4.3 %collective-permute-start.32 = (f32[2,8,512]{2,1,0:T(8,128)S(1)}, f32[2,8,512]{2,1,0:T(8,128)S(1)}, u32[]{:S(2)}, u32[]{:S(2)}) collective-permute-start(f32[2,8,512]{2,1,0:T(8,128)S(1)} %get-tuple-element.51), channel_id=1, source_target_pairs={{0,2},{2,4},{4,6},{6,0},{1,3},{3,5},{5,7},{7,1},{8,10},{10,12},{12... | collective-permute-start | bytes 98312 | tf_op jit(solution)/shard_map/ppermute | solution.py:517
  366.5 4.8 %collective-permute-start.35 = (f32[8,512]{1,0:T(8,128)S(1)}, f32[8,512]{1,0:T(8,128)S(1)}, u32[]{:S(2)}, u32[]{:S(2)}) collective-permute-start(f32[8,512]{1,0:T(8,128)S(1)} %dynamic-slice_bitcast_fusion.5), channel_id=1, source_target_pairs={{0,1},{1,0},{2,3},{3,2},{4,5},{5,4},{6,7},{7,6},{8,9},{9,8},{10,11... | collective-permute-start | bytes 49160 | tf_op jit(solution)/shard_map/ppermute | solution.py:517
  371.2 7.2 %collective-permute-start.21 = (bf16[160,1024]{1,0:T(8,128)(2,1)S(1)}, bf16[160,1024]{1,0:T(8,128)(2,1)S(1)}, u32[]{:S(2)}, u32[]{:S(2)}) collective-permute-start(bf16[160,1024]{1,0:T(8,128)(2,1)S(1)} %dynamic-slice_bitcast_fusion), channel_id=1, source_target_pairs={{0,64},{64,0},{1,65},{65,1},{2,66},{66,2},{3,67},{67,3},{4,68},{68... | collective-permute-start | bytes 983048 | tf_op jit(solution)/shard_map/ppermute | solution.py:517
  380.1 6.0 %collective-permute-start.22 = (bf16[80,1024]{1,0:T(8,128)(2,1)}, bf16[80,1024]{1,0:T(8,128)(2,1)}, u32[]{:S(2)}, u32[]{:S(2)}) collective-permute-start(bf16[80,1024]{1,0:T(8,128)(2,1)} %dynamic-slice_bitcast_fusion.1), channel_id=1, source_target_pairs={{0,1},{1,0},{2,3},{3,2},{4,5},{5,4},{6,7},{7,6},{8,9},{9,8},{10,11... | collective-permute-start | bytes 491528 | tf_op jit(solution)/shard_map/ppermute | solution.py:517
  387.8 6.1 %collective-permute-start.23 = (f32[8,512]{1,0:T(8,128)S(1)}, f32[8,512]{1,0:T(8,128)S(1)}, u32[]{:S(2)}, u32[]{:S(2)}) collective-permute-start(f32[8,512]{1,0:T(8,128)S(1)} %select_bitcast_fusion), channel_id=1, source_target_pairs={{0,8},{8,0},{1,9},{9,1},{2,10},{10,2},{3,11},{11,3},{4,12},{12,4},... | collective-permute-start | bytes 49160 | tf_op jit(solution)/shard_map/ppermute | solution.py:509
  392.2 1.2 collective-permute-start.24
  392.3 2.3 collective-permute-start.25
  (21 other events, 136.9 us)
Sparse Core Ops, SparseCore 0:
  16.6 142.0 all-gather.2
  229.6 131.1 reduce-scatter.3
